TPU v7x, 128 devices: a whole 4x4x4 slice. The times are simulated.
128 devices in a mesh: tower: 2 (over core), seq: 32 (over z_lo, y, x), mp: 2 (over z_hi).
Axes of the slice: x: 4, y: 4, z: 4 (z_hi: 2, z_lo: 2; z = z_hi * 2 + z_lo), core: 2. Of those that a mesh axis runs over, the one named last changes fastest.
Arguments:
- queries: bfloat16 [2, 8192, 1536], P('tower', 'seq', 'mp'), as said below
- context: bfloat16 [2, 8192, 3072], P('tower', 'seq'), may hold values from -6 to 6
- kv_weight: bfloat16 [2, 3072, 2, 1536], P('tower', None, None, 'mp'), may hold values from -0.109375 to 0.109375
- spans: int32 [2, 32, 2], P('tower', 'seq'), may hold values from 0 to 31, as said below
- cotangent: bfloat16 [2, 8192, 1536], P('tower', 'seq', 'mp'), may hold values from -6 to 6
Outputs:
- attn_out: bfloat16 [2, 8192, 1536], P('tower', 'seq', 'mp')
- query_grad: bfloat16 [2, 8192, 1536], P('tower', 'seq', 'mp')
- context_grad: bfloat16 [2, 8192, 3072], P('tower', 'seq')
- weight_grad: bfloat16 [2, 3072, 2, 1536], P('tower', 'seq', None, 'mp')
Inputs may be any that keep to these rules, and one draw needn't show every extreme that they name: queries are drawn independently per entry; their rows may differ in scale. For shard s, s - 2 <= spans[t, s, 0] <= s <= spans[t, s, 1] <= s + 2; in each tower some shard has spans[t, s, 1] - spans[t, s, 0] = 4.
All inputs are finite; a program needn't handle non-finite values.
Results may differ from a plain program's by a relative error of at most 0.03.
Values may be sent and summed in bfloat16 or wider, within the bound.
No kernel may reach another device: no remote copies, remote signals or barrier semaphores. Data moves between devices by JAX's collectives and lax.ppermute only.
A program may use at most 128 MiB of HBM per device.

v0:
```python
import jax
import jax.numpy as jnp
from jax import lax
from jax.sharding import PartitionSpec as P

HD = 128
REACH = 2


NEG_FILL = -1e30


def partner(value, axis, apart):
    mask = 2**apart
    pairs = [(source, source ^ mask) for source in range(lax.axis_size(axis))]
    return lax.ppermute(value, axis, pairs)


def passed_along(value, axis, steps):
    count = lax.axis_size(axis)
    first, last = (max(0, -steps), min(count, count - steps))
    return lax.ppermute(value, axis, [(source, source + steps) for source in range(first, last)])


def local(queries, context, kv_weight, spans, cotangent):
    tok_rows = queries.shape[1]
    columns = queries.shape[2]
    head_count = columns // HD
    model_width = context.shape[2]
    scale = HD ** (-0.5)
    weight_flat = kv_weight[0].reshape(model_width, 2 * columns)
    local_kv = jnp.dot(context[0], weight_flat, preferred_element_type=jnp.float32).astype(
        jnp.bfloat16
    )
    other_kv = partner(local_kv, "tower", 0)
    position = lax.axis_index("seq")
    by_offset = {0: other_kv}
    for offset in range(-REACH, REACH + 1):
        if offset != 0:
            by_offset[offset] = passed_along(other_kv, "seq", -offset)
    window = jnp.concatenate([by_offset[offset] for offset in range(-REACH, REACH + 1)], axis=0)
    first_shard = position - REACH
    key_rows = window.shape[0]
    row_shard = first_shard + jnp.arange(key_rows, dtype=jnp.int32) // tok_rows
    allowed = (row_shard >= spans[0, 0, 0]) & (row_shard <= spans[0, 0, 1])
    query_heads = queries[0].reshape(tok_rows, head_count, HD)
    cot_heads = cotangent[0].reshape(tok_rows, head_count, HD)
    key_heads = window[:, :columns].reshape(key_rows, head_count, HD)
    value_heads = window[:, columns:].reshape(key_rows, head_count, HD)
    scores = (
        jnp.einsum("ihd,jhd->hij", query_heads, key_heads, preferred_element_type=jnp.float32)
        * scale
    )
    scores = jnp.where(allowed[None, None, :], scores, NEG_FILL)
    row_max = jnp.max(scores, axis=2, keepdims=True)
    expo = jnp.where(allowed[None, None, :], jnp.exp(scores - row_max), 0.0)
    weights = expo / jnp.sum(expo, axis=2, keepdims=True)
    rounded = weights.astype(jnp.bfloat16)
    attn_out = jnp.einsum("hij,jhd->ihd", rounded, value_heads, preferred_element_type=jnp.float32)
    attn_out = attn_out.astype(jnp.bfloat16).reshape(tok_rows, columns)
    dprob = jnp.einsum("ihd,jhd->hij", cot_heads, value_heads, preferred_element_type=jnp.float32)
    delta = jnp.sum(dprob * weights, axis=2, keepdims=True)
    dscore = (weights * (dprob - delta) * scale).astype(jnp.bfloat16)
    query_grad = jnp.einsum("hij,jhd->ihd", dscore, key_heads, preferred_element_type=jnp.float32)
    query_grad = query_grad.astype(jnp.bfloat16).reshape(tok_rows, columns)
    key_terms = jnp.einsum(
        "hij,ihd->jhd", dscore, query_heads, preferred_element_type=jnp.float32
    ).reshape(key_rows, columns)
    value_terms = jnp.einsum(
        "hij,ihd->jhd", rounded, cot_heads, preferred_element_type=jnp.float32
    ).reshape(key_rows, columns)
    terms = jnp.concatenate([key_terms, value_terms], axis=1)

    def block_of(offset):
        begin_row = (offset + REACH) * tok_rows
        return terms[begin_row : begin_row + tok_rows].astype(jnp.bfloat16)

    own_part = lax.optimization_barrier(block_of(0))
    summed = own_part.astype(jnp.float32)
    for offset in range(-REACH, REACH + 1):
        if offset != 0:
            arrived = passed_along(block_of(offset), "seq", offset)
            summed = summed + arrived.astype(jnp.float32)
    kv_grad = summed.astype(jnp.bfloat16)
    returned = partner(kv_grad, "tower", 0)
    partial_ctx = lax.dot_general(
        returned, weight_flat, (((1,), (1,)), ((), ())), preferred_element_type=jnp.float32
    )
    context_grad = lax.psum(partial_ctx, "mp").astype(jnp.bfloat16)
    weight_rows = model_width // lax.axis_size("seq")
    ctx_slice = context[0]
    weight_grad = lax.psum_scatter(
        lax.dot_general(
            ctx_slice, returned, (((0,), (0,)), ((), ())), preferred_element_type=jnp.float32
        ).astype(jnp.bfloat16),
        "seq",
        scatter_dimension=0,
        tiled=True,
    ).astype(jnp.float32)
    weight_grad = weight_grad.astype(jnp.bfloat16).reshape(1, weight_rows, 2, columns)
    return (attn_out[None], query_grad[None], context_grad[None], weight_grad)


def solution(mesh):
    return jax.shard_map(
        local,
        mesh=mesh,
        in_specs=(
            P("tower", "seq", "mp"),
            P("tower", "seq", None),
            P("tower", None, None, "mp"),
            P("tower", "seq", None),
            P("tower", "seq", "mp"),
        ),
        out_specs=(
            P("tower", "seq", "mp"),
            P("tower", "seq", "mp"),
            P("tower", "seq", None),
            P("tower", "seq", None, "mp"),
        ),
        check_vma=False,
    )
```

profile of v0, /device:TPU:0, one launch (start us, length us, event | category | flops | bytes accessed | tf_op | source)
XLA Modules:
  0.0 408.0 jit_solution(17787060378227609945)
XLA Ops:
  7.2 9.1 %copy.64 = bf16[384,8,2,768]{3,1,2,0:T(8,128)(2,1)} copy(bf16[384,8,2,768]{3,2,1,0:T(2,128)(2,1)} %bitcast.84) | data formatting | bytes 18874368
  16.3 6.3 %convolution_convert_fusion.1 = bf16[256,1536]{1,0:T(8,128)(2,1)S(1)} fusion(bf16[3072,1536]{1,0:T(8,128)(2,1)} %bitcast.85, bf16[1,256,3072]{2,1,0:T(8,128)(2,1)S(1)} %copy-done), kind=kOutput, calls=%fused_computation.23 | convolution fusion | flops 2416312320 | bytes 11796480 | tf_op jit(solution)/shard_map/dot_general | solution.py:32
  25.0 5.9 %collective-permute-start.1 = (bf16[256,1536]{1,0:T(8,128)(2,1)S(1)}, bf16[256,1536]{1,0:T(8,128)(2,1)}, u32[]{:S(2)}, u32[]{:S(2)}) collective-permute-start(bf16[256,1536]{1,0:T(8,128)(2,1)S(1)} %collective-permute-done), channel_id=1, source_target_pairs={{0,4},{2,6},{4,8},{6,10},{8,12},{10,14},{12,16},{14,18},{16,20},{1... | collective-permute-start | bytes 2359304 | tf_op jit(solution)/shard_map/ppermute | solution.py:22
  30.9 2.5 collective-permute-start.2
  40.9 7.0 %collective-permute-done.1 = bf16[256,1536]{1,0:T(8,128)(2,1)} collective-permute-done((bf16[256,1536]{1,0:T(8,128)(2,1)S(1)}, bf16[256,1536]{1,0:T(8,128)(2,1)}, u32[]{:S(2)}, u32[]{:S(2)}) %collective-permute-start.1) | collective-permute-done | bytes 786464 | tf_op jit(solution)/shard_map/ppermute | solution.py:22
  49.1 14.9 %collective-permute-done.2 = bf16[256,1536]{1,0:T(8,128)(2,1)S(1)} collective-permute-done((bf16[256,1536]{1,0:T(8,128)(2,1)S(1)}, bf16[256,1536]{1,0:T(8,128)(2,1)S(1)}, u32[]{:S(2)}, u32[]{:S(2)}) %collective-permute-start.2) | collective-permute-done | bytes 786464 | tf_op jit(solution)/shard_map/ppermute | solution.py:22
  66.3 16.5 %collective-permute-done.4 = bf16[256,1536]{1,0:T(8,128)(2,1)S(1)} collective-permute-done((bf16[256,1536]{1,0:T(8,128)(2,1)S(1)}, bf16[256,1536]{1,0:T(8,128)(2,1)S(1)}, u32[]{:S(2)}, u32[]{:S(2)}) %collective-permute-start.4) | collective-permute-done | bytes 786464 | tf_op jit(solution)/shard_map/ppermute | solution.py:22
  86.7 2.7 copy.39
  89.4 5.4 %fusion.46 = f32[6,1280,256]{2,1,0:T(8,128)} fusion(bf16[1280,6,128]{0,2,1:T(8,128)(2,1)S(1)} %bitcast.87, bf16[256,6,128]{0,2,1:T(8,128)(2,1)} %bitcast.93), kind=kOutput, calls=%fused_computation.61 | convolution fusion | flops 503316480 | bytes 10223616 | tf_op jit(solution)/shard_map/ihd,jhd->hij/dot_general | solution.py:61
  94.7 8.4 %fusion.45 = (f32[6,256]{1,0:T(8,128)S(1)}, f32[6,256,1280]{1,2,0:T(8,128)}) fusion(pred[1280]{0:T(1024)(128)(4,1)S(1)} %fusion.34, bf16[1280,6,128]{0,2,1:T(8,128)(2,1)} %bitcast.89, bf16[256,6,128]{0,2,1:T(8,128)(2,1)} %bitcast.97), kind=kOutput, calls=%fused_computation.60 | convolution fusion | flops 513148160 | bytes 10231040 | tf_op jit(solution)/shard_map/sub | solution.py:56
  103.2 6.0 %fusion.17 = bf16[6,1280,128]{1,2,0:T(8,128)(2,1)} fusion(bf16[256,6,128]{0,2,1:T(8,128)(2,1)} %bitcast.94, f32[6,256,1280]{1,2,0:T(8,128)} %get-tuple-element.26, f32[6,256]{1,0:T(8,128)S(1)} %get-tuple-element.25), kind=kOutput, calls=%fused_computation.24 | convolution fusion | flops 507248640 | bytes 10229760 | tf_op jit(solution)/shard_map/hij,ihd->jhd/dot_general | solution.py:69
  109.1 14.1 %fusion.15 = bf16[6,1280,128]{1,2,0:T(8,128)(2,1)} fusion(bf16[256,6,128]{0,2,1:T(8,128)(2,1)} %bitcast.98, f32[6,1280,256]{2,1,0:T(8,128)} %fusion.46, f32[6,256,1280]{1,2,0:T(8,128)} %get-tuple-element.26, f32[6,256]{1,0:T(8,128)S(1)} %get-tuple-element.25), kind=kOutput, calls=%fused_computation.21 | convolution fusion | flops 517081856 | bytes 18094080 | tf_op jit(solution)/shard_map/hij,ihd->jhd/dot_general | solution.py:66
  123.2 2.4 maximum_convert_fusion
  125.8 5.0 %collective-permute-start.8 = (bf16[256,1536]{0,1:T(8,128)(2,1)S(1)}, bf16[256,1536]{0,1:T(8,128)(2,1)S(1)}, u32[]{:S(2)}, u32[]{:S(2)}) collective-permute-start(bf16[256,1536]{0,1:T(8,128)(2,1)S(1)} %get-tuple-element.17), channel_id=1, source_target_pairs={{0,4},{2,6},{4,8},{6,10},{8,12},{10,14},{12,16},{14,18},{16,20},{1... | collective-permute-start | bytes 2359304 | tf_op jit(solution)/shard_map/ppermute | solution.py:22
  130.8 2.6 collective-permute-start.7
  136.0 12.8 %collective-permute-done.8 = bf16[256,1536]{0,1:T(8,128)(2,1)S(1)} collective-permute-done((bf16[256,1536]{0,1:T(8,128)(2,1)S(1)}, bf16[256,1536]{0,1:T(8,128)(2,1)S(1)}, u32[]{:S(2)}, u32[]{:S(2)}) %collective-permute-start.8) | collective-permute-done | bytes 786464 | tf_op jit(solution)/shard_map/ppermute | solution.py:22
  148.8 15.1 %collective-permute-done.7 = bf16[256,1536]{0,1:T(8,128)(2,1)S(1)} collective-permute-done((bf16[256,1536]{0,1:T(8,128)(2,1)S(1)}, bf16[256,1536]{0,1:T(8,128)(2,1)S(1)}, u32[]{:S(2)}, u32[]{:S(2)}) %collective-permute-start.7) | collective-permute-done | bytes 786464 | tf_op jit(solution)/shard_map/ppermute | solution.py:22
  164.9 17.8 %collective-permute-done.5 = bf16[256,1536]{0,1:T(8,128)(2,1)S(1)} collective-permute-done((bf16[256,1536]{0,1:T(8,128)(2,1)S(1)}, bf16[256,1536]{0,1:T(8,128)(2,1)S(1)}, u32[]{:S(2)}, u32[]{:S(2)}) %collective-permute-start.5) | collective-permute-done | bytes 786464 | tf_op jit(solution)/shard_map/ppermute | solution.py:22
  186.8 5.1 %fusion.2 = bf16[3072,1536]{0,1:T(8,128)(2,1)} fusion(bf16[256,1536]{0,1:T(8,128)(2,1)S(1)} %collective-permute-done.9, bf16[1,256,3072]{2,1,0:T(8,128)(2,1)S(1)} %copy-done), kind=kOutput, calls=%fused_computation.3 | convolution fusion | flops 2420637696 | bytes 11796480 | tf_op jit(solution)/shard_map/dot_general | solution.py:93
  192.0 12.7 %copy.62 = bf16[3072,1536]{1,0:T(8,128)(2,1)} copy(bf16[3072,1536]{0,1:T(8,128)(2,1)} %fusion.2) | data formatting | bytes 18874368
  204.7 4.7 %fusion.23 = bf16[6,128,256]{2,1,0:T(8,128)(2,1)} fusion(bf16[1280,6,128]{0,2,1:T(8,128)(2,1)S(1)} %bitcast.88, f32[6,256,1280]{1,2,0:T(8,128)} %get-tuple-element.26, f32[6,256]{1,0:T(8,128)S(1)} %get-tuple-element.25), kind=kOutput, calls=%fused_computation.32 | convolution fusion | flops 507445248 | bytes 10229760 | tf_op jit(solution)/shard_map/hij,jhd->ihd/dot_general | solution.py:59
  211.3 13.3 %fusion.26 = bf16[6,128,256]{2,1,0:T(8,128)(2,1)S(1)} fusion(bf16[1280,6,128]{0,2,1:T(8,128)(2,1)} %bitcast.90, f32[6,1280,256]{2,1,0:T(8,128)} %fusion.46, f32[6,256,1280]{1,2,0:T(8,128)} %get-tuple-element.26, f32[6,256]{1,0:T(8,128)S(1)} %get-tuple-element.25), kind=kOutput, calls=%fused_computation.33 | convolution fusion | flops 517278464 | bytes 18094080 | tf_op jit(solution)/shard_map/hij,jhd->ihd/dot_general | solution.py:64
  225.5 8.1 %fusion.47 = f32[256,3072]{1,0:T(8,128)} fusion(bf16[256,1536]{0,1:T(8,128)(2,1)S(1)} %copy-done.2, bf16[3072,1536]{1,0:T(8,128)(2,1)} %bitcast.86), kind=kOutput, calls=%fused_computation.62 | convolution fusion | flops 2415919104 | bytes 13369344 | tf_op jit(solution)/shard_map/dot_general | solution.py:86
  233.6 165.4 %all-reduce.1 = bf16[256,3072]{1,0:T(8,128)(2,1)} all-reduce(f32[256,3072]{1,0:T(8,128)} %fusion.47), channel_id=1, replica_groups=mesh['tower'=2,'seq'=32,'mp'=2] {'mp'}, use_global_device_ids=true, to_apply=%region_3.4 | all-reduce | flops 786432 | bytes 4718592 | tf_op jit(solution)/shard_map/psum | solution.py:89
  (40 shorter events, 30.0 us)
Async XLA Ops:
  7.2 9.1 %copy-start = (bf16[1,256,3072]{2,1,0:T(8,128)(2,1)S(1)}, bf16[1,256,3072]{2,1,0:T(8,128)(2,1)}, u32[]{:S(2)}) copy-start(bf16[1,256,3072]{2,1,0:T(8,128)(2,1)} %param.6) | copy-start | bytes 4718596
  7.2 391.9 %reduce-scatter.4.cloned.1.call-start = ((), (), s32[]{:S(2)}) async-start(), calls=%async_computation.1 | async-start | bytes 9732096
  16.3 17.1 %copy-start.4 = (s32[1,1,2]{2,1,0:T(1,128)S(1)}, s32[1,1,2]{2,1,0:T(1,128)}, u32[]{:S(2)}) copy-start(s32[1,1,2]{2,1,0:T(1,128)} %param.8) | copy-start | bytes 28
  16.3 20.3 %copy-start.3 = (bf16[1,256,768]{2,1,0:T(8,128)(2,1)S(1)}, bf16[1,256,768]{2,1,0:T(8,128)(2,1)}, u32[]{:S(2)}) copy-start(bf16[1,256,768]{2,1,0:T(8,128)(2,1)} %param.5) | copy-start | bytes 1179652
  22.6 2.4 collective-permute-start
  25.0 22.9 %collective-permute-start.1 = (bf16[256,1536]{1,0:T(8,128)(2,1)S(1)}, bf16[256,1536]{1,0:T(8,128)(2,1)}, u32[]{:S(2)}, u32[]{:S(2)}) collective-permute-start(bf16[256,1536]{1,0:T(8,128)(2,1)S(1)} %collective-permute-done), channel_id=1, source_target_pairs={{0,4},{2,6},{4,8},{6,10},{8,12},{10,14},{12,16},{14,18},{16,20},{1... | collective-permute-start | bytes 2359304 | tf_op jit(solution)/shard_map/ppermute | solution.py:22
  30.9 33.1 %collective-permute-start.2 = (bf16[256,1536]{1,0:T(8,128)(2,1)S(1)}, bf16[256,1536]{1,0:T(8,128)(2,1)S(1)}, u32[]{:S(2)}, u32[]{:S(2)}) collective-permute-start(bf16[256,1536]{1,0:T(8,128)(2,1)S(1)} %collective-permute-done), channel_id=1, source_target_pairs={{0,2},{2,4},{4,6},{6,8},{8,10},{10,12},{12,14},{14,16},{16,18},{18... | collective-permute-start | bytes 2359304 | tf_op jit(solution)/shard_map/ppermute | solution.py:22
  34.0 31.1 %collective-permute-start.3 = (bf16[256,1536]{1,0:T(8,128)(2,1)S(1)}, bf16[256,1536]{1,0:T(8,128)(2,1)}, u32[]{:S(2)}, u32[]{:S(2)}) collective-permute-start(bf16[256,1536]{1,0:T(8,128)(2,1)S(1)} %collective-permute-done), channel_id=1, source_target_pairs={{2,0},{4,2},{6,4},{8,6},{10,8},{12,10},{14,12},{16,14},{18,16},{20... | collective-permute-start | bytes 2359304 | tf_op jit(solution)/shard_map/ppermute | solution.py:22
  39.5 43.4 %collective-permute-start.4 = (bf16[256,1536]{1,0:T(8,128)(2,1)S(1)}, bf16[256,1536]{1,0:T(8,128)(2,1)S(1)}, u32[]{:S(2)}, u32[]{:S(2)}) collective-permute-start(bf16[256,1536]{1,0:T(8,128)(2,1)S(1)} %collective-permute-done), channel_id=1, source_target_pairs={{4,0},{6,2},{8,4},{10,6},{12,8},{14,10},{16,12},{18,14},{20,16},{2... | collective-permute-start | bytes 2359304 | tf_op jit(solution)/shard_map/ppermute | solution.py:22
  125.8 23.0 %collective-permute-start.8 = (bf16[256,1536]{0,1:T(8,128)(2,1)S(1)}, bf16[256,1536]{0,1:T(8,128)(2,1)S(1)}, u32[]{:S(2)}, u32[]{:S(2)}) collective-permute-start(bf16[256,1536]{0,1:T(8,128)(2,1)S(1)} %get-tuple-element.17), channel_id=1, source_target_pairs={{0,4},{2,6},{4,8},{6,10},{8,12},{10,14},{12,16},{14,18},{16,20},{1... | collective-permute-start | bytes 2359304 | tf_op jit(solution)/shard_map/ppermute | solution.py:22
  130.8 33.1 %collective-permute-start.7 = (bf16[256,1536]{0,1:T(8,128)(2,1)S(1)}, bf16[256,1536]{0,1:T(8,128)(2,1)S(1)}, u32[]{:S(2)}, u32[]{:S(2)}) collective-permute-start(bf16[256,1536]{0,1:T(8,128)(2,1)S(1)} %get-tuple-element.18), channel_id=1, source_target_pairs={{0,2},{2,4},{4,6},{6,8},{8,10},{10,12},{12,14},{14,16},{16,18},{18... | collective-permute-start | bytes 2359304 | tf_op jit(solution)/shard_map/ppermute | solution.py:22
  133.4 31.6 %collective-permute-start.6 = (bf16[256,1536]{0,1:T(8,128)(2,1)S(1)}, bf16[256,1536]{0,1:T(8,128)(2,1)S(1)}, u32[]{:S(2)}, u32[]{:S(2)}) collective-permute-start(bf16[256,1536]{0,1:T(8,128)(2,1)S(1)} %get-tuple-element.19), channel_id=1, source_target_pairs={{2,0},{4,2},{6,4},{8,6},{10,8},{12,10},{14,12},{16,14},{18,16},{20... | collective-permute-start | bytes 2359304 | tf_op jit(solution)/shard_map/ppermute | solution.py:22
  134.7 48.1 %collective-permute-start.5 = (bf16[256,1536]{0,1:T(8,128)(2,1)S(1)}, bf16[256,1536]{0,1:T(8,128)(2,1)S(1)}, u32[]{:S(2)}, u32[]{:S(2)}) collective-permute-start(bf16[256,1536]{0,1:T(8,128)(2,1)S(1)} %get-tuple-element.20), channel_id=1, source_target_pairs={{4,0},{6,2},{8,4},{10,6},{12,8},{14,10},{16,12},{18,14},{20,16},{2... | collective-permute-start | bytes 2359304 | tf_op jit(solution)/shard_map/ppermute | solution.py:22
  183.4 2.6 collective-permute-start.9
  186.0 0.9 copy-start.1
  211.3 14.2 %copy-start.2 = (bf16[256,1536]{0,1:T(8,128)(2,1)S(1)}, bf16[256,1536]{0,1:T(8,128)(2,1)}, u32[]{:S(2)}) copy-start(bf16[256,1536]{0,1:T(8,128)(2,1)} %copy-done.1) | copy-start | bytes 2359300
Sparse Core Ops, SparseCore 0:
  204.8 185.6 reduce-scatter.3
where the time goes:
time: 409 us; the launch traced here: 408 us
  blocking collectives  165 us (40%)
  waiting for transfers between devices  90.7 us (22%)
  matrix products  71.4 us (17%)
  local copies, waits for them, and re-layouts  40.2 us (10%)
  starting transfers between devices  21.7 us (5%)
  between operations  14.2 us (3%)
  other arithmetic  4.3 us (1%)
    psum x1, blocking collectives, local(): context_grad = lax.psum(partial_ctx, 'mp').astype(jnp.bfloat16)  165 us
    ppermute x8, waiting for transfers between devices, passed_along(): lax.ppermute(value, axis, [(source, source + steps) for source in range(f...  86.2 us
    unnamed x22, local copies, waits for them, and re-layouts  32.9 us
    ppermute x8, starting transfers between devices, passed_along(): lax.ppermute(value, axis, [(source, source + steps) for source in range(f...  21.3 us
    dot_general x1, matrix products, local(): jnp.einsum('hij,ihd->jhd', dscore, query_heads, preferred_element_type=jn...  14.1 us
    dot_general x1, matrix products, local(): jnp.einsum('hij,jhd->ihd', dscore, key_heads, preferred_element_type=jnp....  13.3 us
    sub x1, matrix products, local(): expo = jnp.where(allowed[None, None, :], jnp.exp(scores - row_max), 0.0)  8.41 us
  transfers between devices with their start and end apart: 11, of which 10 were waited for; matrix products, arithmetic and copies ran while one was open for 9% of the time, Pallas kernels for 0%

commit v1 on v0

v1 whole, which is shorter than its diff:
```python
import functools

import jax
import jax.numpy as jnp
from jax import lax
from jax.experimental import pallas as pl
from jax.experimental.pallas import tpu as pltpu
from jax.sharding import PartitionSpec as P

HD = 128
REACH = 2
NEG_FILL = -1e30
F32, BF16 = jnp.float32, jnp.bfloat16
ZS, YS, XS = 2, 4, 4
PAIR = 2
WINDOW = 6


def moved(value, axis, pairs):
    return lax.ppermute(value, axis, pairs)


def swapped(value, axis):
    return moved(value, axis, [(0, 1), (1, 0)])


def seq_pairs(to):
    pairs = []
    for source in range(ZS * YS * XS):
        target = to(source // (YS * XS), source // XS % YS, source % XS)
        if target is not None:
            z, y, x = target
            pairs.append((source, (z * YS + y % YS) * XS + x % XS))
    return pairs


def along_x(steps):
    return seq_pairs(lambda z, y, x: (z, y, x + steps))


def along_y(steps):
    return seq_pairs(lambda z, y, x: (z, y + steps, x))


def across_z():
    return seq_pairs(lambda z, y, x: (1 - z, y, x))


def to_pair(steps, same):
    count = ZS * YS * XS
    pairs = []
    for source in range(count):
        pair, member = source // PAIR, source % PAIR
        target = (pair + steps) * PAIR + (member if same else 1 - member)
        if 0 <= target < count:
            pairs.append((source, target))
    return pairs


def dot(a, b, dims):
    return lax.dot_general(a, b, ((dims[0], dims[1]), ((), ())), preferred_element_type=F32)


def attention_kernel(meta, q_own, c_own, q_pair, c_pair, *refs):
    kv_refs, (od_own, od_pair), g_refs = refs[:6], refs[6:8], refs[8:14]
    kv_s, q_s, c_s, g_s = refs[14:]
    rows = q_own.shape[0]
    member = meta[0]
    scale = HD ** (-0.5)
    order = (2 + member, 3 - member, member, 1 - member, 4 + member, 5 - member)
    for ref, place in zip(kv_refs, order):
        kv_s[pl.ds(pl.multiple_of(place * rows, rows), rows), :] = ref[...]
    for ref, pair_ref, scratch in ((q_own, q_pair, q_s), (c_own, c_pair, c_s)):
        scratch[pl.ds(pl.multiple_of(member * rows, rows), rows), :] = ref[...]
        scratch[pl.ds(pl.multiple_of((1 - member) * rows, rows), rows), :] = pair_ref[...]
    g_s[...] = jnp.zeros_like(g_s)
    span = 2 * REACH + 1
    for i in range(PAIR):
        q = q_s[i * rows : (i + 1) * rows, :]
        c = c_s[i * rows : (i + 1) * rows, :]
        window = slice(i * rows, (i + span) * rows)
        keys = kv_s[window, :HD]
        values = kv_s[window, HD:]
        low, high = meta[2 + 2 * i], meta[3 + 2 * i]
        scores = dot(keys, q, ((1,), (1,))) * scale
        blocks = []
        for j in range(span):
            shard = meta[1] + i + j
            keep = (shard >= low) & (shard <= high)
            blocks.append(jnp.where(keep, scores[j * rows : (j + 1) * rows], NEG_FILL))
        scores = jnp.concatenate(blocks, axis=0)
        expo = jnp.exp(scores - jnp.max(scores, axis=0, keepdims=True))
        probs = expo * (1.0 / jnp.sum(expo, axis=0, keepdims=True))
        rounded = probs.astype(BF16)
        dprobs = dot(values, c, ((1,), (1,)))
        delta = jnp.sum(dprobs * probs, axis=0, keepdims=True)
        dscores = (probs * (dprobs - delta) * scale).astype(BF16)
        out = dot(values, rounded, ((0,), (0,)))
        dq = dot(keys, dscores, ((0,), (0,)))
        g_s[window, :HD] += dot(dscores, q, ((1,), (0,)))
        g_s[window, HD:] += dot(rounded, c, ((1,), (0,)))
        both = jnp.concatenate([out, dq], axis=0).T.astype(BF16)

        @pl.when(member == i)
        def _():
            od_own[...] = both

        @pl.when(member != i)
        def _():
            od_pair[...] = both

    for ref, place in zip(g_refs, order):
        ref[...] = g_s[pl.ds(pl.multiple_of(place * rows, rows), rows), :].astype(BF16)


def attention(meta, queries, cotangent, arrived_qc, kv_own, kv_rest):
    rows, columns = queries.shape
    heads = columns // HD // PAIR
    half = heads * 2 * HD
    one = lambda of: pl.BlockSpec((rows, HD), of)
    two = lambda of: pl.BlockSpec((rows, 2 * HD), of)
    plain = two(lambda h, m: (0, h))
    own = lambda h, m: (0, heads * m[0] + h)
    shape = jax.ShapeDtypeStruct((rows, half), BF16)
    work = 2 * heads * rows * rows * 5
    return pl.pallas_call(
        attention_kernel,
        out_shape=[shape] * 8,
        grid_spec=pltpu.PrefetchScalarGridSpec(
            num_scalar_prefetch=1,
            grid=(heads,),
            in_specs=[
                one(own),
                one(own),
                one(lambda h, m: (0, h)),
                one(lambda h, m: (0, heads + h)),
                two(own),
            ]
            + [plain] * 5,
            out_specs=[plain] * 8,
            scratch_shapes=[
                pltpu.VMEM((WINDOW * rows, 2 * HD), BF16),
                pltpu.VMEM((PAIR * rows, HD), BF16),
                pltpu.VMEM((PAIR * rows, HD), BF16),
                pltpu.VMEM((WINDOW * rows, 2 * HD), F32),
            ],
        ),
        compiler_params=pltpu.CompilerParams(vmem_limit_bytes=40 * 2**20),
        cost_estimate=pl.CostEstimate(
            flops=work * 10 * HD, bytes_accessed=8 * 2**20, transcendentals=work
        ),
        name="attention",
    )(meta, queries, cotangent, arrived_qc, arrived_qc, kv_own, *kv_rest)


def local(queries, context, kv_weight, spans, cotangent):
    queries, context, cotangent = queries[0], context[0], cotangent[0]
    rows, columns = queries.shape
    heads = columns // HD
    width = context.shape[1]
    half = columns
    position = lax.axis_index("seq")
    member = position % PAIR
    x, y, z = position % XS, position // XS % YS, position // (XS * YS)

    other_half = (1 - member) * (columns // 2)
    qc = jnp.concatenate(
        [lax.dynamic_slice_in_dim(v, other_half, columns // 2, axis=1) for v in (queries, cotangent)],
        axis=1,
    )
    pair_swap = to_pair(0, False)
    arrived_qc = moved(qc, "seq", pair_swap)
    own_span = spans[0, 0]
    pair_span = moved(own_span, "seq", pair_swap)

    by_y = context.reshape(rows, ZS, YS, width // (ZS * YS))
    ctx_part = lambda k: lax.dynamic_index_in_dim(by_y, (y + k) % YS, 2, keepdims=False).reshape(
        rows, width // YS
    )
    ctx_cols = [ctx_part(0)] + [moved(ctx_part(k), "seq", along_y(k)) for k in range(1, YS)]

    weight = (
        kv_weight[0].reshape(width, 2, heads, HD).transpose(0, 2, 1, 3).reshape(width, 2 * columns)
    )
    local_kv = dot(context, weight, ((1,), (0,))).astype(BF16)
    other_kv = swapped(local_kv, "tower")
    same_half = lax.dynamic_slice_in_dim(other_kv, member * half, half, axis=1)
    next_half = lax.dynamic_slice_in_dim(other_kv, (1 - member) * half, half, axis=1)
    kv_rest = [
        moved(next_half, "seq", pair_swap),
        moved(same_half, "seq", to_pair(1, True)),
        moved(next_half, "seq", to_pair(1, False)),
        moved(same_half, "seq", to_pair(-1, True)),
        moved(next_half, "seq", to_pair(-1, False)),
    ]
    first = jnp.where(member == 0, own_span, pair_span)
    second = jnp.where(member == 0, pair_span, own_span)
    base = position - member - REACH
    meta = jnp.concatenate([jnp.stack([member, base]), first, second]).astype(jnp.int32)
    od_own, od_pair, g_own, *g_rest = attention(
        meta, queries, cotangent, arrived_qc, other_kv, kv_rest
    )
    arrived = [
        moved(g, "seq", pairs)
        for g, pairs in zip(
            g_rest,
            (pair_swap, to_pair(-1, True), to_pair(-1, False), to_pair(1, True), to_pair(1, False)),
        )
    ]
    total = lambda parts: functools.reduce(jnp.add, [p.astype(F32) for p in parts]).astype(BF16)
    g_same = total([g_own, arrived[1], arrived[3]])
    g_next = total([arrived[0], arrived[2], arrived[4]])
    kv_grad = jnp.concatenate(
        [jnp.where(member == 0, g_same, g_next), jnp.where(member == 0, g_next, g_same)], axis=1
    )
    returned = swapped(kv_grad, "tower")

    gathered = [returned] + [moved(returned, "seq", along_y(k)) for k in range(1, YS)]

    partial_ctx = dot(returned, weight, ((1,), (1,))).astype(BF16)
    partial_ctx = lax.optimization_barrier(partial_ctx)
    context_grad = (
        partial_ctx.astype(F32) + swapped(partial_ctx, "mp").astype(F32)
    ).astype(BF16)

    partial_w = dot(
        jnp.concatenate(ctx_cols, axis=0), jnp.concatenate(gathered, axis=0), ((0,), (0,))
    ).astype(BF16)
    by_x = partial_w.reshape(ZS, XS, width // (ZS * YS * XS), 2 * columns)
    x_part = lambda k: lax.dynamic_index_in_dim(by_x, (x + k) % XS, 1, keepdims=False)
    over_x = functools.reduce(
        jnp.add,
        [x_part(0).astype(F32)]
        + [moved(x_part(k), "seq", along_x(k)).astype(F32) for k in range(1, XS)],
    )
    z_part = lambda k: lax.dynamic_index_in_dim(over_x, (z + k) % ZS, 0, keepdims=False)
    weight_grad = z_part(0) + moved(z_part(1).astype(BF16), "seq", across_z()).astype(F32)
    weight_grad = (
        weight_grad.astype(BF16)
        .reshape(-1, heads, 2, HD)
        .transpose(0, 2, 1, 3)
        .reshape(1, -1, 2, columns)
    )

    od_back = moved(od_pair, "seq", pair_swap)
    lo = jnp.where(member == 0, od_own, od_back).reshape(rows, heads // 2, 2, HD)
    hi = jnp.where(member == 0, od_back, od_own).reshape(rows, heads // 2, 2, HD)
    od = jnp.concatenate([lo, hi], axis=1)
    attn_out = od[:, :, 0].reshape(1, rows, columns)
    query_grad = od[:, :, 1].reshape(1, rows, columns)
    return attn_out, query_grad, context_grad[None], weight_grad


def solution(mesh):
    return jax.shard_map(
        local,
        mesh=mesh,
        in_specs=(
            P("tower", "seq", "mp"),
            P("tower", "seq", None),
            P("tower", None, None, "mp"),
            P("tower", "seq", None),
            P("tower", "seq", "mp"),
        ),
        out_specs=(
            P("tower", "seq", "mp"),
            P("tower", "seq", "mp"),
            P("tower", "seq", None),
            P("tower", "seq", None, "mp"),
        ),
        check_vma=False,
    )
```

time: 409 us -> 256 us (0.63)
  blocking collectives: 165 us -> 0 us
  matrix products: 71.4 us -> 19.2 us
  waiting for transfers between devices: 90.7 us -> 122 us
  starting transfers between devices: 21.7 us -> 43.8 us
  Pallas kernels: 0 us -> 14 us
  between operations: 14.2 us -> 0.99 us
  local copies, waits for them, and re-layouts: 40.2 us -> 45.9 us
  other arithmetic: 4.3 us -> 8.5 us
    psum x1 -> x0, blocking collectives: 165 us -> none  [local(): context_grad = lax.psum(partial_ctx, 'mp').astype(jnp.bfloat16)]
    dot_general x8 -> x3, matrix products: 63 us -> 19.2 us  [dot(): lax.dot_general(a, b, ((dims[0], dims[1]), ((), ())), preferred_element_t...]
    ppermute x10 -> x26, waiting for transfers between devices: 90.7 us -> 122 us  [moved(): return lax.ppermute(value, axis, pairs)]
    ppermute x10 -> x26, starting transfers between devices: 21.7 us -> 43.8 us  [moved(): return lax.ppermute(value, axis, pairs)]
    pallas_call x0 -> x1, Pallas kernels: none -> 14 us  [attention(): pl.pallas_call(attention_kernel, out_shape=[shape] * 8, grid_spec=pltpu.P...]
    sub x1 -> x0, matrix products: 8.41 us -> none  [local(): expo = jnp.where(allowed[None, None, :], jnp.exp(scores - row_max), 0.0)]
    transpose x0 -> x1, local copies, waits for them, and re-layouts: none -> 8.29 us  [local(): kv_weight[0].reshape(width, 2, heads, HD).transpose(0, 2, 1, 3)]
    slice x5 -> x0, local copies, waits for them, and re-layouts: 7.31 us -> none  [the longest x2 3.8 us: local(): key_heads = window[:, :columns].reshape(key_rows, head_count, HD)]
  transfers between devices with their start and end apart: 11 -> 26, of which waited for: 10 -> 14; matrix products, arithmetic and copies ran while one was open for 9% -> 11% of each run, Pallas kernels for 0% -> 0%
where the time goes in v1:
time: 256 us; the launch traced here: 254 us
  waiting for transfers between devices  122 us (48%)
  local copies, waits for them, and re-layouts  45.9 us (18%)
  starting transfers between devices  43.8 us (17%)
  matrix products  19.2 us (8%)
  Pallas kernels  14 us (5%)
  other arithmetic  8.5 us (3%)
    ppermute x26, waiting for transfers between devices, moved(): return lax.ppermute(value, axis, pairs)  122 us
    ppermute x26, starting transfers between devices, moved(): return lax.ppermute(value, axis, pairs)  43.8 us
    unnamed x30, local copies, waits for them, and re-layouts  32.5 us
    dot_general x3, matrix products, dot(): lax.dot_general(a, b, ((dims[0], dims[1]), ((), ())), preferred_element_t...  19.2 us
    pallas_call x1, Pallas kernels, attention(): pl.pallas_call(attention_kernel, out_shape=[shape] * 8, grid_spec=pltpu.P...  14 us
    transpose x1, local copies, waits for them, and re-layouts, local(): kv_weight[0].reshape(width, 2, heads, HD).transpose(0, 2, 1, 3)  8.29 us
  transfers between devices with their start and end apart: 26, of which 14 were waited for; matrix products, arithmetic and copies ran while one was open for 11% of the time, Pallas kernels for 0%

profile of v1, /device:TPU:0, one launch (start us, length us, event | category | flops | bytes accessed | tf_op | source)
XLA Modules:
  0.0 254.4 jit_solution(15177111551164453199)
XLA Ops:
  0.6 23.7 %copy.17 = bf16[1,3072,2,768]{1,3,2,0:T(8,128)(2,1)} copy(bf16[1,3072,2,768]{3,2,1,0:T(2,128)(2,1)} %param.7) | data formatting | bytes 18874368 | tf_op args[2]
  24.3 8.3 %copy.18 = bf16[3072,6,2,128]{0,3,2,1:T(8,128)(2,1)} copy(bf16[3072,6,2,128]{0,3,1,2:T(8,128)(2,1)} %bitcast.53) | data formatting | bytes 18874368 | tf_op jit(solution)/shard_map/transpose | solution.py:183
  32.6 7.3 %convolution_convert_fusion.2 = bf16[256,1536]{1,0:T(8,128)(2,1)} fusion(bf16[3072,1536]{0,1:T(8,128)(2,1)} %bitcast.54, bf16[1,256,3072]{2,1,0:T(8,128)(2,1)S(1)} %copy-done.6), kind=kOutput, calls=%fused_computation.10 | convolution fusion | flops 2416312320 | bytes 11796480 | tf_op jit(solution)/shard_map/dot_general | solution.py:61
  45.3 4.0 %collective-permute-start.5 = (bf16[256,768]{1,0:T(8,128)(2,1)}, bf16[256,768]{1,0:T(8,128)(2,1)S(1)}, u32[]{:S(2)}, u32[]{:S(2)}) collective-permute-start(bf16[256,768]{1,0:T(8,128)(2,1)} %get-tuple-element.42), channel_id=1, source_target_pairs={{0,6},{2,4},{4,10},{6,8},{8,14},{10,12},{12,18},{14,16},{16,22},{1... | collective-permute-start | bytes 1179656 | tf_op jit(solution)/shard_map/ppermute | solution.py:20
  55.6 5.7 %collective-permute-done.3.refs_1_ = bf16[256,768]{1,0:T(8,128)(2,1)S(1)} collective-permute-done((bf16[256,768]{1,0:T(8,128)(2,1)}, bf16[256,768]{1,0:T(8,128)(2,1)S(1)}, u32[]{:S(2)}, u32[]{:S(2)}) %collective-permute-start.3) | collective-permute-done | bytes 393248 | tf_op jit(solution)/shard_map/ppermute | solution.py:20
  61.3 7.2 %collective-permute-done.4.refs_2_ = bf16[256,768]{1,0:T(8,128)(2,1)S(1)} collective-permute-done((bf16[256,768]{1,0:T(8,128)(2,1)}, bf16[256,768]{1,0:T(8,128)(2,1)S(1)}, u32[]{:S(2)}, u32[]{:S(2)}) %collective-permute-start.4) | collective-permute-done | bytes 393248 | tf_op jit(solution)/shard_map/ppermute | solution.py:20
  69.3 10.9 %collective-permute-done.6.refs_4_ = bf16[256,768]{1,0:T(8,128)(2,1)S(1)} collective-permute-done((bf16[256,768]{1,0:T(8,128)(2,1)}, bf16[256,768]{1,0:T(8,128)(2,1)S(1)}, u32[]{:S(2)}, u32[]{:S(2)}) %collective-permute-start.6) | collective-permute-done | bytes 393248 | tf_op jit(solution)/shard_map/ppermute | solution.py:20
  80.9 5.5 %collective-permute-done.7.refs_5_ = bf16[256,768]{1,0:T(8,128)(2,1)} collective-permute-done((bf16[256,768]{1,0:T(8,128)(2,1)}, bf16[256,768]{1,0:T(8,128)(2,1)}, u32[]{:S(2)}, u32[]{:S(2)}) %collective-permute-start.7) | collective-permute-done | bytes 393248 | tf_op jit(solution)/shard_map/ppermute | solution.py:20
  88.4 14.0 %attention.1 = (bf16[256,768]{1,0:T(8,128)(2,1)S(1)}, bf16[256,768]{1,0:T(8,128)(2,1)S(1)}, bf16[256,768]{1,0:T(8,128)(2,1)S(1)}, bf16[256,768]{1,0:T(8,128)(2,1...) custom-call(s32[6]{0:T(128)S(1)} %pad_add_fusion.meta, ...), custom_call_target="tpu_custom_call" | custom-call | flops 2516582400 | bytes 8388608 | tf_op jit(solution)/shard_map/attention/pallas_call | solution.py:126
  102.4 4.3 %collective-permute-start.10 = (bf16[256,768]{1,0:T(8,128)(2,1)S(1)}, bf16[256,768]{1,0:T(8,128)(2,1)S(1)}, u32[]{:S(2)}, u32[]{:S(2)}) collective-permute-start(bf16[256,768]{1,0:T(8,128)(2,1)S(1)} %get-tuple-element.16), channel_id=1, source_target_pairs={{0,4},{2,6},{4,8},{6,10},{8,12},{10,14},{12,16},{14,18},{16,20},{1... | collective-permute-start | bytes 1179656 | tf_op jit(solution)/shard_map/ppermute | solution.py:20
  108.0 7.2 %collective-permute-start.13 = (bf16[256,768]{1,0:T(8,128)(2,1)S(1)}, bf16[256,768]{1,0:T(8,128)(2,1)S(1)}, u32[]{:S(2)}, u32[]{:S(2)}) collective-permute-start(bf16[256,768]{1,0:T(8,128)(2,1)S(1)} %get-tuple-element.19), channel_id=1, source_target_pairs={{0,6},{2,4},{4,10},{6,8},{8,14},{10,12},{12,18},{14,16},{16,22},{1... | collective-permute-start | bytes 1179656 | tf_op jit(solution)/shard_map/ppermute | solution.py:20
  116.7 12.3 %collective-permute-done.9 = bf16[256,768]{1,0:T(8,128)(2,1)S(1)} collective-permute-done((bf16[256,768]{1,0:T(8,128)(2,1)S(1)}, bf16[256,768]{1,0:T(8,128)(2,1)S(1)}, u32[]{:S(2)}, u32[]{:S(2)}) %collective-permute-start.9) | collective-permute-done | bytes 393248 | tf_op jit(solution)/shard_map/ppermute | solution.py:20
  129.0 15.3 %collective-permute-done.12 = bf16[256,768]{1,0:T(8,128)(2,1)S(1)} collective-permute-done((bf16[256,768]{1,0:T(8,128)(2,1)S(1)}, bf16[256,768]{1,0:T(8,128)(2,1)S(1)}, u32[]{:S(2)}, u32[]{:S(2)}) %collective-permute-start.12) | collective-permute-done | bytes 393248 | tf_op jit(solution)/shard_map/ppermute | solution.py:20
  147.6 4.0 %collective-permute-start.18 = (bf16[256,768]{0,1:T(8,128)(2,1)}, bf16[256,768]{0,1:T(8,128)(2,1)S(1)}, u32[]{:S(2)}, u32[]{:S(2)}) collective-permute-start(bf16[256,768]{0,1:T(8,128)(2,1)} %bitcast.18), channel_id=1, source_target_pairs={{0,24},{2,26},{4,28},{6,30},{8,0},{10,2},{12,4},{14,6},{16,8},{18,... | collective-permute-start | bytes 1179656 | tf_op jit(solution)/shard_map/ppermute | solution.py:20
  157.2 12.6 %collective-permute-done.18 = bf16[256,768]{0,1:T(8,128)(2,1)S(1)} collective-permute-done((bf16[256,768]{0,1:T(8,128)(2,1)}, bf16[256,768]{0,1:T(8,128)(2,1)S(1)}, u32[]{:S(2)}, u32[]{:S(2)}) %collective-permute-start.18) | collective-permute-done | bytes 393248 | tf_op jit(solution)/shard_map/ppermute | solution.py:20
  169.8 7.8 %convolution_convert_fusion = bf16[256,3072]{1,0:T(8,128)(2,1)} fusion(bf16[256,1536]{1,0:T(8,128)(2,1)} %collective-permute-done.14, bf16[3072,1536]{0,1:T(8,128)(2,1)} %bitcast.55), kind=kOutput, calls=%fused_computation | convolution fusion | flops 2416705536 | bytes 11796480 | tf_op jit(solution)/shard_map/dot_general | solution.py:61
  178.0 3.6 %collective-permute-start.15 = (bf16[256,3072]{1,0:T(8,128)(2,1)}, bf16[256,3072]{1,0:T(8,128)(2,1)}, u32[]{:S(2)}, u32[]{:S(2)}) collective-permute-start(bf16[256,3072]{1,0:T(8,128)(2,1)} %convolution_convert_fusion), channel_id=1, source_target_pairs={{0,1},{1,0},{2,3},{3,2},{4,5},{5,4},{6,7},{7,6},{8,9},{9,8},{10,11... | collective-permute-start | bytes 4718600 | tf_op jit(solution)/shard_map/ppermute | solution.py:20
  181.6 21.6 %collective-permute-done.21 = bf16[256,1536]{1,0:T(8,128)(2,1)S(1)} collective-permute-done((bf16[256,1536]{1,0:T(8,128)(2,1)}, bf16[256,1536]{1,0:T(8,128)(2,1)S(1)}, u32[]{:S(2)}, u32[]{:S(2)}) %collective-permute-start.21) | collective-permute-done | bytes 786464 | tf_op jit(solution)/shard_map/ppermute | solution.py:20
  203.1 3.4 %collective-permute-done.19 = bf16[256,1536]{1,0:T(8,128)(2,1)S(1)} collective-permute-done((bf16[256,1536]{1,0:T(8,128)(2,1)}, bf16[256,1536]{1,0:T(8,128)(2,1)S(1)}, u32[]{:S(2)}, u32[]{:S(2)}) %collective-permute-start.19) | collective-permute-done | bytes 786464 | tf_op jit(solution)/shard_map/ppermute | solution.py:20
  206.6 4.1 %convolution_convert_fusion.1 = bf16[768,1536]{1,0:T(8,128)(2,1)S(1)} fusion(bf16[256,1536]{1,0:T(8,128)(2,1)S(1)} %collective-permute-done.21, bf16[256,1536]{1,0:T(8,128)(2,1)S(1)} %collective-permute-done.20, bf16[256,1536]{1,0:T(8,128)(2,1)S(1)} %collective-permute-done.19, bf16[256,1536]{1,0:T(8,128)(2,1)} %collective-permute-done.14, ...), kind=kOutput, calls=%fused_computation.1 | convolution fusion | flops 2435973120 | bytes 7077888 | tf_op jit(solution)/shard_map/dot_general | solution.py:61
  220.7 7.7 %collective-permute-done.24 = bf16[2,96,1536]{2,1,0:T(8,128)(2,1)} collective-permute-done((bf16[2,96,1536]{2,1,0:T(8,128)(2,1)}, bf16[2,96,1536]{2,1,0:T(8,128)(2,1)}, u32[]{:S(2)}, u32[]{:S(2)}) %collective-permute-start.24) | collective-permute-done | bytes 589856 | tf_op jit(solution)/shard_map/ppermute | solution.py:20
  231.3 11.5 %collective-permute-done.22 = bf16[2,96,1536]{2,1,0:T(8,128)(2,1)} collective-permute-done((bf16[2,96,1536]{2,1,0:T(8,128)(2,1)}, bf16[2,96,1536]{2,1,0:T(8,128)(2,1)}, u32[]{:S(2)}, u32[]{:S(2)}) %collective-permute-start.22) | collective-permute-done | bytes 589856 | tf_op jit(solution)/shard_map/ppermute | solution.py:20
  244.6 3.6 %fusion.7 = bf16[1,256,3072]{2,1,0:T(8,128)(2,1)} fusion(bf16[256,3072]{1,0:T(8,128)(2,1)} %collective-permute-done.15, bf16[256,3072]{1,0:T(8,128)(2,1)} %convolution_convert_fusion), kind=kLoop, calls=%fused_computation.11 | loop fusion | flops 3145728 | bytes 4718592 | tf_op jit(solution)/shard_map/broadcast_in_dim | solution.py:251
  248.2 5.3 %collective-permute-done.25 = bf16[96,1536]{1,0:T(8,128)(2,1)S(1)} collective-permute-done((bf16[96,1536]{1,0:T(8,128)(2,1)S(1)}, bf16[96,1536]{1,0:T(8,128)(2,1)S(1)}, u32[]{:S(2)}, u32[]{:S(2)}) %collective-permute-start.25) | collective-permute-done | bytes 294944 | tf_op jit(solution)/shard_map/ppermute | solution.py:20
  (83 shorter events, 42.5 us)
Async XLA Ops:
  40.8 13.5 %collective-permute-start.1 = (bf16[256,768]{1,0:T(8,128)(2,1)}, bf16[256,768]{1,0:T(8,128)(2,1)S(1)}, u32[]{:S(2)}, u32[]{:S(2)}) collective-permute-start(bf16[256,768]{1,0:T(8,128)(2,1)} %pad_maximum_fusion.2), channel_id=1, source_target_pairs={{0,2},{2,0},{4,6},{6,4},{8,10},{10,8},{12,14},{14,12},{16,18},{18,... | collective-permute-start | bytes 1179656 | tf_op jit(solution)/shard_map/ppermute | solution.py:20
  42.3 10.6 %collective-permute-start = (s32[2]{0:T(128)S(1)}, s32[2]{0:T(128)S(1)}, u32[]{:S(2)}, u32[]{:S(2)}) collective-permute-start(s32[2]{0:T(128)S(1)} %bitcast.64), channel_id=1, source_target_pairs={{0,2},{2,0},{4,6},{6,4},{8,10},{10,8},{12,14},{14,12},{16,18},{18,... | collective-permute-start | bytes 32 | tf_op jit(solution)/shard_map/ppermute | solution.py:20
  43.7 17.6 %collective-permute-start.3 = (bf16[256,768]{1,0:T(8,128)(2,1)}, bf16[256,768]{1,0:T(8,128)(2,1)S(1)}, u32[]{:S(2)}, u32[]{:S(2)}) collective-permute-start(bf16[256,768]{1,0:T(8,128)(2,1)} %get-tuple-element.42), channel_id=1, source_target_pairs={{0,2},{2,0},{4,6},{6,4},{8,10},{10,8},{12,14},{14,12},{16,18},{18,... | collective-permute-start | bytes 1179656 | tf_op jit(solution)/shard_map/ppermute | solution.py:20
  45.3 24.0 %collective-permute-start.5 = (bf16[256,768]{1,0:T(8,128)(2,1)}, bf16[256,768]{1,0:T(8,128)(2,1)S(1)}, u32[]{:S(2)}, u32[]{:S(2)}) collective-permute-start(bf16[256,768]{1,0:T(8,128)(2,1)} %get-tuple-element.42), channel_id=1, source_target_pairs={{0,6},{2,4},{4,10},{6,8},{8,14},{10,12},{12,18},{14,16},{16,22},{1... | collective-permute-start | bytes 1179656 | tf_op jit(solution)/shard_map/ppermute | solution.py:20
  49.3 19.2 %collective-permute-start.4 = (bf16[256,768]{1,0:T(8,128)(2,1)}, bf16[256,768]{1,0:T(8,128)(2,1)S(1)}, u32[]{:S(2)}, u32[]{:S(2)}) collective-permute-start(bf16[256,768]{1,0:T(8,128)(2,1)} %get-tuple-element.41), channel_id=1, source_target_pairs={{0,4},{2,6},{4,8},{6,10},{8,12},{10,14},{12,16},{14,18},{16,20},{1... | collective-permute-start | bytes 1179656 | tf_op jit(solution)/shard_map/ppermute | solution.py:20
  52.9 27.2 %collective-permute-start.6 = (bf16[256,768]{1,0:T(8,128)(2,1)}, bf16[256,768]{1,0:T(8,128)(2,1)S(1)}, u32[]{:S(2)}, u32[]{:S(2)}) collective-permute-start(bf16[256,768]{1,0:T(8,128)(2,1)} %get-tuple-element.41), channel_id=1, source_target_pairs={{4,0},{6,2},{8,4},{10,6},{12,8},{14,10},{16,12},{18,14},{20,16},{2... | collective-permute-start | bytes 1179656 | tf_op jit(solution)/shard_map/ppermute | solution.py:20
  54.2 32.2 %collective-permute-start.7 = (bf16[256,768]{1,0:T(8,128)(2,1)}, bf16[256,768]{1,0:T(8,128)(2,1)}, u32[]{:S(2)}, u32[]{:S(2)}) collective-permute-start(bf16[256,768]{1,0:T(8,128)(2,1)} %get-tuple-element.42), channel_id=1, source_target_pairs={{4,2},{6,0},{8,6},{10,4},{12,10},{14,8},{16,14},{18,12},{20,18},{2... | collective-permute-start | bytes 1179656 | tf_op jit(solution)/shard_map/ppermute | solution.py:20
  102.4 14.3 %collective-permute-start.10 = (bf16[256,768]{1,0:T(8,128)(2,1)S(1)}, bf16[256,768]{1,0:T(8,128)(2,1)S(1)}, u32[]{:S(2)}, u32[]{:S(2)}) collective-permute-start(bf16[256,768]{1,0:T(8,128)(2,1)S(1)} %get-tuple-element.16), channel_id=1, source_target_pairs={{0,4},{2,6},{4,8},{6,10},{8,12},{10,14},{12,16},{14,18},{16,20},{1... | collective-permute-start | bytes 1179656 | tf_op jit(solution)/shard_map/ppermute | solution.py:20
  106.7 22.3 %collective-permute-start.9 = (bf16[256,768]{1,0:T(8,128)(2,1)S(1)}, bf16[256,768]{1,0:T(8,128)(2,1)S(1)}, u32[]{:S(2)}, u32[]{:S(2)}) collective-permute-start(bf16[256,768]{1,0:T(8,128)(2,1)S(1)} %get-tuple-element.15), channel_id=1, source_target_pairs={{4,0},{6,2},{8,4},{10,6},{12,8},{14,10},{16,12},{18,14},{20,16},{2... | collective-permute-start | bytes 1179656 | tf_op jit(solution)/shard_map/ppermute | solution.py:20
  108.0 21.0 %collective-permute-start.13 = (bf16[256,768]{1,0:T(8,128)(2,1)S(1)}, bf16[256,768]{1,0:T(8,128)(2,1)S(1)}, u32[]{:S(2)}, u32[]{:S(2)}) collective-permute-start(bf16[256,768]{1,0:T(8,128)(2,1)S(1)} %get-tuple-element.19), channel_id=1, source_target_pairs={{0,6},{2,4},{4,10},{6,8},{8,14},{10,12},{12,18},{14,16},{16,22},{1... | collective-permute-start | bytes 1179656 | tf_op jit(solution)/shard_map/ppermute | solution.py:20
  115.3 29.0 %collective-permute-start.12 = (bf16[256,768]{1,0:T(8,128)(2,1)S(1)}, bf16[256,768]{1,0:T(8,128)(2,1)S(1)}, u32[]{:S(2)}, u32[]{:S(2)}) collective-permute-start(bf16[256,768]{1,0:T(8,128)(2,1)S(1)} %get-tuple-element.18), channel_id=1, source_target_pairs={{4,2},{6,0},{8,6},{10,4},{12,10},{14,8},{16,14},{18,12},{20,18},{2... | collective-permute-start | bytes 1179656 | tf_op jit(solution)/shard_map/ppermute | solution.py:20
  116.6 27.7 %collective-permute-start.11 = (bf16[256,768]{1,0:T(8,128)(2,1)S(1)}, bf16[256,768]{1,0:T(8,128)(2,1)S(1)}, u32[]{:S(2)}, u32[]{:S(2)}) collective-permute-start(bf16[256,768]{1,0:T(8,128)(2,1)S(1)} %get-tuple-element.17), channel_id=1, source_target_pairs={{0,2},{2,0},{4,6},{6,4},{8,10},{10,8},{12,14},{14,12},{16,18},{18,... | collective-permute-start | bytes 1179656 | tf_op jit(solution)/shard_map/ppermute | solution.py:20
  147.6 22.2 %collective-permute-start.18 = (bf16[256,768]{0,1:T(8,128)(2,1)}, bf16[256,768]{0,1:T(8,128)(2,1)S(1)}, u32[]{:S(2)}, u32[]{:S(2)}) collective-permute-start(bf16[256,768]{0,1:T(8,128)(2,1)} %bitcast.18), channel_id=1, source_target_pairs={{0,24},{2,26},{4,28},{6,30},{8,0},{10,2},{12,4},{14,6},{16,8},{18,... | collective-permute-start | bytes 1179656 | tf_op jit(solution)/shard_map/ppermute | solution.py:20
  151.7 26.0 %collective-permute-start.17 = (bf16[256,768]{0,1:T(8,128)(2,1)S(1)}, bf16[256,768]{0,1:T(8,128)(2,1)S(1)}, u32[]{:S(2)}, u32[]{:S(2)}) collective-permute-start(bf16[256,768]{0,1:T(8,128)(2,1)S(1)} %bitcast.62), channel_id=1, source_target_pairs={{0,16},{2,18},{4,20},{6,22},{8,24},{10,26},{12,28},{14,30},{16,0},... | collective-permute-start | bytes 1179656 | tf_op jit(solution)/shard_map/ppermute | solution.py:20
  151.7 26.3 %collective-permute-start.16 = (bf16[256,768]{0,1:T(8,128)(2,1)}, bf16[256,768]{0,1:T(8,128)(2,1)S(1)}, u32[]{:S(2)}, u32[]{:S(2)}) collective-permute-start(bf16[256,768]{0,1:T(8,128)(2,1)} %bitcast.16), channel_id=1, source_target_pairs={{0,8},{2,10},{4,12},{6,14},{8,16},{10,18},{12,20},{14,22},{16,24},... | collective-permute-start | bytes 1179656 | tf_op jit(solution)/shard_map/ppermute | solution.py:20
  152.5 50.6 %collective-permute-start.21 = (bf16[256,1536]{1,0:T(8,128)(2,1)}, bf16[256,1536]{1,0:T(8,128)(2,1)S(1)}, u32[]{:S(2)}, u32[]{:S(2)}) collective-permute-start(bf16[256,1536]{1,0:T(8,128)(2,1)} %collective-permute-done.14), channel_id=1, source_target_pairs={{0,24},{2,26},{4,28},{6,30},{8,0},{10,2},{12,4},{14,6},{16,8},{18,... | collective-permute-start | bytes 2359304 | tf_op jit(solution)/shard_map/ppermute | solution.py:20
  154.9 48.2 %collective-permute-start.20 = (bf16[256,1536]{1,0:T(8,128)(2,1)}, bf16[256,1536]{1,0:T(8,128)(2,1)S(1)}, u32[]{:S(2)}, u32[]{:S(2)}) collective-permute-start(bf16[256,1536]{1,0:T(8,128)(2,1)} %collective-permute-done.14), channel_id=1, source_target_pairs={{0,16},{2,18},{4,20},{6,22},{8,24},{10,26},{12,28},{14,30},{16,0},... | collective-permute-start | bytes 2359304 | tf_op jit(solution)/shard_map/ppermute | solution.py:20
  169.8 36.7 %collective-permute-start.19 = (bf16[256,1536]{1,0:T(8,128)(2,1)}, bf16[256,1536]{1,0:T(8,128)(2,1)S(1)}, u32[]{:S(2)}, u32[]{:S(2)}) collective-permute-start(bf16[256,1536]{1,0:T(8,128)(2,1)} %collective-permute-done.14), channel_id=1, source_target_pairs={{0,8},{2,10},{4,12},{6,14},{8,16},{10,18},{12,20},{14,22},{16,24},... | collective-permute-start | bytes 2359304 | tf_op jit(solution)/shard_map/ppermute | solution.py:20
  177.7 36.6 %collective-permute-start.8 = (bf16[256,768]{1,0:T(8,128)(2,1)S(1)}, bf16[256,768]{1,0:T(8,128)(2,1)S(1)}, u32[]{:S(2)}, u32[]{:S(2)}) collective-permute-start(bf16[256,768]{1,0:T(8,128)(2,1)S(1)} %get-tuple-element.13), channel_id=1, source_target_pairs={{0,2},{2,0},{4,6},{6,4},{8,10},{10,8},{12,14},{14,12},{16,18},{18,... | collective-permute-start | bytes 1179656 | tf_op jit(solution)/shard_map/ppermute | solution.py:20
  178.0 66.6 %collective-permute-start.15 = (bf16[256,3072]{1,0:T(8,128)(2,1)}, bf16[256,3072]{1,0:T(8,128)(2,1)}, u32[]{:S(2)}, u32[]{:S(2)}) collective-permute-start(bf16[256,3072]{1,0:T(8,128)(2,1)} %convolution_convert_fusion), channel_id=1, source_target_pairs={{0,1},{1,0},{2,3},{3,2},{4,5},{5,4},{6,7},{7,6},{8,9},{9,8},{10,11... | collective-permute-start | bytes 4718600 | tf_op jit(solution)/shard_map/ppermute | solution.py:20
  211.9 16.5 %collective-permute-start.24 = (bf16[2,96,1536]{2,1,0:T(8,128)(2,1)}, bf16[2,96,1536]{2,1,0:T(8,128)(2,1)}, u32[]{:S(2)}, u32[]{:S(2)}) collective-permute-start(bf16[2,96,1536]{2,1,0:T(8,128)(2,1)} %get-tuple-element.29), channel_id=1, source_target_pairs={{0,6},{2,0},{4,2},{6,4},{8,14},{10,8},{12,10},{14,12},{16,22},{18,... | collective-permute-start | bytes 1769480 | tf_op jit(solution)/shard_map/ppermute | solution.py:20
  213.2 18.1 %collective-permute-start.23 = (bf16[2,96,1536]{2,1,0:T(8,128)(2,1)}, bf16[2,96,1536]{2,1,0:T(8,128)(2,1)}, u32[]{:S(2)}, u32[]{:S(2)}) collective-permute-start(bf16[2,96,1536]{2,1,0:T(8,128)(2,1)} %get-tuple-element.30), channel_id=1, source_target_pairs={{0,4},{2,6},{4,0},{6,2},{8,12},{10,14},{12,8},{14,10},{16,20},{18,... | collective-permute-start | bytes 1769480 | tf_op jit(solution)/shard_map/ppermute | solution.py:20
  214.2 28.5 %collective-permute-start.22 = (bf16[2,96,1536]{2,1,0:T(8,128)(2,1)}, bf16[2,96,1536]{2,1,0:T(8,128)(2,1)}, u32[]{:S(2)}, u32[]{:S(2)}) collective-permute-start(bf16[2,96,1536]{2,1,0:T(8,128)(2,1)} %get-tuple-element.28), channel_id=1, source_target_pairs={{0,2},{2,4},{4,6},{6,0},{8,10},{10,12},{12,14},{14,8},{16,18},{18,... | collective-permute-start | bytes 1769480 | tf_op jit(solution)/shard_map/ppermute | solution.py:20
  244.5 9.0 %collective-permute-start.25 = (bf16[96,1536]{1,0:T(8,128)(2,1)S(1)}, bf16[96,1536]{1,0:T(8,128)(2,1)S(1)}, u32[]{:S(2)}, u32[]{:S(2)}) collective-permute-start(bf16[96,1536]{1,0:T(8,128)(2,1)S(1)} %fusion.20), channel_id=1, source_target_pairs={{0,32},{2,34},{4,36},{6,38},{8,40},{10,42},{12,44},{14,46},{16,48}... | collective-permute-start | bytes 884744 | tf_op jit(solution)/shard_map/ppermute | solution.py:20
  (15 other events, 166.9 us)

commit v2 on v1

v2 whole, which is shorter than its diff:
```python
import functools

import jax
import jax.numpy as jnp
from jax import lax
from jax.experimental import pallas as pl
from jax.experimental.pallas import tpu as pltpu
from jax.sharding import PartitionSpec as P

HD = 128
REACH = 2
NEG_FILL = -1e30
F32, BF16 = jnp.float32, jnp.bfloat16
ZS, YS, XS = 2, 4, 4
PAIR = 2
WINDOW = 6


def moved(value, axis, pairs):
    return lax.ppermute(value, axis, pairs)


def swapped(value, axis):
    return moved(value, axis, [(0, 1), (1, 0)])


def moved_across(value, pairs):
    both = [
        (tower * ZS * YS * XS + source, (1 - tower) * ZS * YS * XS + target)
        for tower in range(2)
        for source, target in pairs
    ]
    return lax.ppermute(value, ("tower", "seq"), both)


def seq_pairs(to):
    pairs = []
    for source in range(ZS * YS * XS):
        row, x = to(source // XS, source % XS)
        if 0 <= row < ZS * YS:
            pairs.append((source, row * XS + x))
    return pairs


def across_z():
    return seq_pairs(lambda row, x: ((row + YS) % (ZS * YS), x))


def in_row(flip):
    return seq_pairs(lambda row, x: (row, x ^ flip))


def next_row(back, flip):
    return seq_pairs(lambda row, x: (row + (1 if (x >= PAIR) != back else -1), x ^ flip))


def dot(a, b, dims):
    return lax.dot_general(a, b, ((dims[0], dims[1]), ((), ())), preferred_element_type=F32)


def projection_kernel(context, weight, kv, weight_out, total):
    step = pl.program_id(0)
    sides = jnp.swapaxes(weight[...], 0, 1)
    heads = sides.shape[2] // HD
    block = jnp.concatenate(
        [sides[side, :, h * HD : (h + 1) * HD] for h in range(heads) for side in range(2)], axis=1
    )
    weight_out[...] = block
    part = dot(context[...], block, ((1,), (0,)))

    @pl.when(step == 0)
    def _():
        total[...] = part

    @pl.when(step > 0)
    def _():
        total[...] += part

    @pl.when(step == pl.num_programs(0) - 1)
    def _():
        kv[...] = total[...].astype(BF16)


def projection(context, weight):
    rows, width = context.shape
    columns = weight.shape[2]
    depth = width // 4
    return pl.pallas_call(
        projection_kernel,
        out_shape=[
            jax.ShapeDtypeStruct((rows, 2 * columns), BF16),
            jax.ShapeDtypeStruct((width, 2 * columns), BF16),
        ],
        grid=(width // depth,),
        in_specs=[
            pl.BlockSpec((rows, depth), lambda i: (0, i)),
            pl.BlockSpec((depth, 2, columns), lambda i: (i, 0, 0)),
        ],
        out_specs=[
            pl.BlockSpec((rows, 2 * columns), lambda i: (0, 0)),
            pl.BlockSpec((depth, 2 * columns), lambda i: (i, 0)),
        ],
        scratch_shapes=[pltpu.VMEM((rows, 2 * columns), F32)],
        compiler_params=pltpu.CompilerParams(vmem_limit_bytes=60 * 2**20),
        cost_estimate=pl.CostEstimate(
            flops=4 * rows * width * columns, bytes_accessed=40 * 2**20, transcendentals=0
        ),
        name="projection",
    )(context, weight)


def attention_kernel(meta, q_a, c_a, q_b, c_b, *refs):
    kv_refs, (od_a, od_b), g_refs = refs[:6], refs[6:8], refs[8:11]
    kv_s, q_s, c_s, g_s = refs[11:]
    rows, heads = q_a.shape[0], od_a.shape[1] // (2 * HD)
    member, side = meta[0], meta[6]
    scale = HD ** (-0.5)
    near, far = 4 * side, 4 * (1 - side)
    order = (near + member, near + 1 - member, 2 + member, 3 - member, far + member, far + 1 - member)
    for ref, place in zip(kv_refs, order):
        kv_s[pl.ds(pl.multiple_of(place * rows, rows), rows), :] = ref[...]
    for ref, other, scratch in ((q_a, q_b, q_s), (c_a, c_b, c_s)):
        scratch[pl.ds(pl.multiple_of(member * rows, rows), rows), :] = ref[...]
        scratch[pl.ds(pl.multiple_of((1 - member) * rows, rows), rows), :] = other[...]
    g_s[...] = jnp.zeros_like(g_s)
    span = 2 * REACH + 1
    for i in range(PAIR):
        q = q_s[i * rows : (i + 1) * rows, :]
        c = c_s[i * rows : (i + 1) * rows, :]
        window = slice(i * rows, (i + span) * rows)
        keys = kv_s[window, :HD]
        values = kv_s[window, HD:]
        low, high = meta[2 + 2 * i], meta[3 + 2 * i]
        scores = dot(keys, q, ((1,), (1,))) * scale
        blocks = []
        for j in range(span):
            shard = meta[1] + i + j
            keep = (shard >= low) & (shard <= high)
            blocks.append(jnp.where(keep, scores[j * rows : (j + 1) * rows], NEG_FILL))
        scores = jnp.concatenate(blocks, axis=0)
        expo = jnp.exp(scores - jnp.max(scores, axis=0, keepdims=True))
        probs = expo * (1.0 / jnp.sum(expo, axis=0, keepdims=True))
        rounded = probs.astype(BF16)
        dprobs = dot(values, c, ((1,), (1,)))
        delta = jnp.sum(dprobs * probs, axis=0, keepdims=True)
        dscores = (probs * (dprobs - delta) * scale).astype(BF16)
        out = dot(values, rounded, ((0,), (0,)))
        dq = dot(keys, dscores, ((0,), (0,)))
        g_s[window, :HD] += dot(dscores, q, ((1,), (0,)))
        g_s[window, HD:] += dot(rounded, c, ((1,), (0,)))
        head = pl.program_id(0)
        parts = [
            (value.T.astype(BF16), pl.ds(pl.multiple_of((side_ * heads + head) * HD, HD), HD))
            for side_, value in enumerate((out, dq))
        ]

        @pl.when(member == i)
        def _():
            for value, columns in parts:
                od_a[:, columns] = value

        @pl.when(member != i)
        def _():
            for value, columns in parts:
                od_b[:, columns] = value

    for index, place in enumerate(order):
        begin = index % PAIR * rows
        g_refs[index // PAIR][begin : begin + rows, :] = g_s[
            pl.ds(pl.multiple_of(place * rows, rows), rows), :
        ].astype(BF16)


def attention(meta, qc_a, qc_b, kv_blocks):
    rows, half = kv_blocks[0].shape[0], qc_a.shape[1]
    heads = half // (2 * HD)
    one = lambda of: pl.BlockSpec((rows, HD), of)
    two = lambda of: pl.BlockSpec((rows, 2 * HD), of)
    plain = two(lambda h, m: (0, h))
    query, cot = one(lambda h, m: (0, h)), one(lambda h, m: (0, heads + h))
    shape = jax.ShapeDtypeStruct((rows, half), BF16)
    pair_shape = jax.ShapeDtypeStruct((PAIR * rows, half), BF16)
    whole = pl.BlockSpec((rows, half), lambda h, m: (0, 0))
    pair_block = pl.BlockSpec((PAIR * rows, 2 * HD), lambda h, m: (0, h))
    work = 2 * heads * rows * rows * 5
    return pl.pallas_call(
        attention_kernel,
        out_shape=[shape] * 2 + [pair_shape] * 3,
        grid_spec=pltpu.PrefetchScalarGridSpec(
            num_scalar_prefetch=1,
            grid=(heads,),
            in_specs=[query, cot, query, cot] + [plain] * 6,
            out_specs=[whole] * 2 + [pair_block] * 3,
            scratch_shapes=[
                pltpu.VMEM((WINDOW * rows, 2 * HD), BF16),
                pltpu.VMEM((PAIR * rows, HD), BF16),
                pltpu.VMEM((PAIR * rows, HD), BF16),
                pltpu.VMEM((WINDOW * rows, 2 * HD), F32),
            ],
        ),
        compiler_params=pltpu.CompilerParams(vmem_limit_bytes=62 * 2**20),
        cost_estimate=pl.CostEstimate(
            flops=work * 10 * HD, bytes_accessed=8 * 2**20, transcendentals=work
        ),
        name="attention",
    )(meta, qc_a, qc_a, qc_b, qc_b, *kv_blocks)


def weight_kernel(own, own_z, pair, pair_z, grad, grad_z, out):
    rows = own.shape[0]
    total = dot(own[...], grad[:rows, :], ((0,), (0,)))
    total += dot(pair[...], grad[rows:, :], ((0,), (0,)))
    total += dot(own_z[...], grad_z[:rows, :], ((0,), (0,)))
    total += dot(pair_z[...], grad_z[rows:, :], ((0,), (0,)))
    out[...] = total.astype(BF16)


def weight_partial(contexts, grads):
    rows, width = contexts[0].shape
    columns = grads[0].shape[1]
    split = 4
    block = width // split
    return pl.pallas_call(
        weight_kernel,
        out_shape=jax.ShapeDtypeStruct((width, columns), BF16),
        grid=(split,),
        in_specs=[pl.BlockSpec((v.shape[0], block), lambda i: (0, i)) for v in contexts]
        + [pl.BlockSpec(g.shape, lambda i: (0, 0)) for g in grads],
        out_specs=pl.BlockSpec((block, columns), lambda i: (i, 0)),
        compiler_params=pltpu.CompilerParams(vmem_limit_bytes=24 * 2**20),
        cost_estimate=pl.CostEstimate(
            flops=8 * rows * width * columns, bytes_accessed=8 * 2**20, transcendentals=0
        ),
        name="weight_partial",
    )(*contexts, *grads)


def context_kernel(grad, weight, out):
    out[...] = dot(grad[...], weight[...], ((1,), (1,))).astype(BF16)


def context_partial(grad, weight):
    rows, columns = grad.shape
    width = weight.shape[0]
    block = width // 4
    return pl.pallas_call(
        context_kernel,
        out_shape=jax.ShapeDtypeStruct((rows, width), BF16),
        grid=(width // block,),
        in_specs=[
            pl.BlockSpec((rows, columns), lambda i: (0, 0)),
            pl.BlockSpec((block, columns), lambda i: (i, 0)),
        ],
        out_specs=pl.BlockSpec((rows, block), lambda i: (0, i)),
        compiler_params=pltpu.CompilerParams(vmem_limit_bytes=60 * 2**20),
        cost_estimate=pl.CostEstimate(
            flops=2 * rows * width * columns, bytes_accessed=12 * 2**20, transcendentals=0
        ),
        name="context_partial",
    )(grad, weight)


def local(queries, context, kv_weight, spans, cotangent):
    queries, context, cotangent = queries[0], context[0], cotangent[0]
    rows, columns = queries.shape
    heads = columns // HD
    width = context.shape[1]
    position = lax.axis_index("seq")
    member = position % PAIR
    side = position % XS // PAIR
    z = position // (XS * YS)
    same_x, cross_x, pair_x = in_row(2), in_row(3), in_row(1)
    half_of = lambda v, which: lax.dynamic_slice_in_dim(
        v, which * (v.shape[1] // 2), v.shape[1] // 2, axis=1
    )
    in_order = lambda mine, other: jnp.concatenate(
        [jnp.where(member == 0, mine, other), jnp.where(member == 0, other, mine)], axis=1
    )
    total = lambda parts: functools.reduce(jnp.add, [p.astype(F32) for p in parts])

    span_rows = jnp.broadcast_to(jnp.pad(spans[0].astype(BF16), ((0, 0), (0, columns - 2))), (16, columns))
    qc_of = lambda which: jnp.concatenate(
        [
            jnp.concatenate([half_of(queries, which), half_of(cotangent, which)], axis=1),
            span_rows,
        ],
        axis=0,
    )
    qc_a = moved(qc_of(member), "seq", same_x)
    qc_b = moved(qc_of(1 - member), "seq", cross_x)

    local_kv, weight = projection(context, kv_weight[0])
    local_kv, qc_a, qc_b = lax.optimization_barrier((local_kv, qc_a, qc_b))
    same_half, next_half = half_of(local_kv, member), half_of(local_kv, 1 - member)
    kv_blocks = [
        swapped(same_half, "tower"),
        moved_across(next_half, pair_x),
        moved_across(same_half, same_x),
        moved_across(next_half, cross_x),
        moved_across(same_half, next_row(False, 0)),
        moved_across(next_half, next_row(False, 1)),
    ]
    ctx_own = half_of(context, z)
    kv_blocks, late_own, late_context = lax.optimization_barrier((kv_blocks, ctx_own, context))
    ctx_z = moved(half_of(late_context, 1 - z), "seq", across_z())
    ctx_pair = moved(late_own, "seq", pair_x)

    span_a, span_b = qc_a[rows, :2].astype(jnp.int32), qc_b[rows, :2].astype(jnp.int32)
    first = jnp.where(member == 0, span_a, span_b)
    second = jnp.where(member == 0, span_b, span_a)
    base = position - member - 4 * side
    meta = jnp.concatenate([jnp.stack([member, base]), first, second, side[None]]).astype(jnp.int32)
    od_a, od_b, g_near, g_mid, g_far = attention(meta, qc_a, qc_b, kv_blocks)

    g_mid = moved_across(g_mid, same_x)
    g_far, ctx_pair, ctx_z = lax.optimization_barrier((g_far, ctx_pair, ctx_z))
    g_far = moved_across(g_far, next_row(True, 0))
    returned = total([swapped(g_near, "tower"), g_mid, g_far]).astype(BF16)
    late_z, _ = lax.optimization_barrier((ctx_z, returned))
    ctx_pair_z = moved(late_z, "seq", pair_x)
    returned_z = moved(returned, "seq", across_z())
    other_rows = moved(returned[rows:], "seq", pair_x)
    od_a, od_b, _ = lax.optimization_barrier((od_a, od_b, returned))
    od_a, od_b = moved(od_a, "seq", same_x), moved(od_b, "seq", cross_x)
    other_rows, od_b = lax.optimization_barrier((other_rows, od_b))
    own_shard = in_order(returned[:rows], other_rows)
    partial_ctx = context_partial(own_shard, weight)
    sum_parts = [partial_ctx[:, : width // 3], partial_ctx[:, width // 3 :]]
    sum_first = swapped(sum_parts[0], "mp")


    partial_w = weight_partial([ctx_own, ctx_z, ctx_pair, ctx_pair_z], [returned, returned_z])
    partial_w, sum_first = lax.optimization_barrier((partial_w, sum_first))
    late_half, _ = lax.optimization_barrier((sum_parts[1], sum_first))
    sum_second = swapped(late_half, "mp")
    groups = [
        [(z_ * YS + y) * XS + PAIR * s + m for y in range(YS) for s in range(XS // PAIR)]
        for z_ in range(ZS)
        for m in range(PAIR)
    ]
    parts = lax.all_to_all(
        partial_w.reshape(len(groups[0]), -1, columns), "seq", 0, 0, axis_index_groups=groups
    )
    half_grad = jnp.sum(parts.astype(F32), axis=0).astype(BF16).reshape(PAIR, -1, columns)
    own_rows = lax.dynamic_index_in_dim(half_grad, member, 0, keepdims=False)
    pair_rows = lax.dynamic_index_in_dim(half_grad, 1 - member, 0, keepdims=False)
    weight_grad = (
        in_order(own_rows, moved(pair_rows, "seq", pair_x))
        .reshape(-1, heads, 2, HD)
        .transpose(0, 2, 1, 3)
        .reshape(1, -1, 2, columns)
    )

    context_grad = jnp.concatenate(
        [
            total([mine, other]).astype(BF16)
            for mine, other in zip(sum_parts, (sum_first, sum_second))
        ],
        axis=1,
    )
    attn_out = in_order(od_a[:, : columns // 2], od_b[:, : columns // 2])
    query_grad = in_order(od_a[:, columns // 2 :], od_b[:, columns // 2 :])
    return attn_out[None], query_grad[None], context_grad[None], weight_grad


def solution(mesh):
    return jax.shard_map(
        local,
        mesh=mesh,
        in_specs=(
            P("tower", "seq", "mp"),
            P("tower", "seq", None),
            P("tower", None, None, "mp"),
            P("tower", "seq", None),
            P("tower", "seq", "mp"),
        ),
        out_specs=(
            P("tower", "seq", "mp"),
            P("tower", "seq", "mp"),
            P("tower", "seq", None),
            P("tower", "seq", None, "mp"),
        ),
        check_vma=False,
    )
```

time: 256 us -> 196 us (0.77)
  local copies, waits for them, and re-layouts: 45.9 us -> 10.3 us
  waiting for transfers between devices: 122 us -> 86.9 us
  Pallas kernels: 14 us -> 41.1 us
  matrix products: 19.2 us -> 0 us
  starting transfers between devices: 43.8 us -> 46.9 us
    ppermute x26 -> x14, waiting for transfers between devices: 122 us -> 49.4 us  [moved(): return lax.ppermute(value, axis, pairs)]
    ppermute x0 -> x7, waiting for transfers between devices: none -> 37.5 us  [moved_across(): return lax.ppermute(value, ('tower', 'seq'), both)]
    unnamed x30 -> x18, local copies, waits for them, and re-layouts: 32.5 us -> 1.6 us
    pallas_call x1 -> x4, Pallas kernels: 14 us -> 41.1 us  [the longest x1 15.2 us: attention(): pl.pallas_call(attention_kernel, out_shape=[shape] * 2 + [pair_shape] * 3...]
    dot_general x3 -> x0, matrix products: 19.2 us -> none  [dot(): lax.dot_general(a, b, ((dims[0], dims[1]), ((), ())), preferred_element_t...]
    ppermute x26 -> x14, starting transfers between devices: 43.8 us -> 25.6 us  [moved(): return lax.ppermute(value, axis, pairs)]
    ppermute x0 -> x7, starting transfers between devices: none -> 15.1 us  [moved_across(): return lax.ppermute(value, ('tower', 'seq'), both)]
    transpose x1 -> x0, local copies, waits for them, and re-layouts: 8.29 us -> none  [local(): kv_weight[0].reshape(width, 2, heads, HD).transpose(0, 2, 1, 3)]
  transfers between devices with their start and end apart: 26 -> 22, of which waited for: 14 -> 14; matrix products, arithmetic and copies ran while one was open for 11% -> 4% of each run, Pallas kernels for 0% -> 21%
where the time goes in v2:
time: 196 us; the launch traced here: 195 us
  waiting for transfers between devices  86.9 us (44%)
  starting transfers between devices  46.9 us (24%)
  Pallas kernels  41.1 us (21%)
  local copies, waits for them, and re-layouts  10.3 us (5%)
  other arithmetic  8.87 us (5%)
    ppermute x14, waiting for transfers between devices, moved(): return lax.ppermute(value, axis, pairs)  49.4 us
    ppermute x7, waiting for transfers between devices, moved_across(): return lax.ppermute(value, ('tower', 'seq'), both)  37.5 us
    ppermute x14, starting transfers between devices, moved(): return lax.ppermute(value, axis, pairs)  25.6 us
    pallas_call x1, Pallas kernels, attention(): pl.pallas_call(attention_kernel, out_shape=[shape] * 2 + [pair_shape] * 3...  15.2 us
    ppermute x7, starting transfers between devices, moved_across(): return lax.ppermute(value, ('tower', 'seq'), both)  15.1 us
    pallas_call x1, Pallas kernels, projection(): pl.pallas_call(projection_kernel, out_shape=[jax.ShapeDtypeStruct((rows,...  13.2 us
    pallas_call x1, Pallas kernels, context_partial(): pl.pallas_call(context_kernel, out_shape=jax.ShapeDtypeStruct((rows, widt...  7.03 us
    all_to_all x1, starting transfers between devices, local(): lax.all_to_all(partial_w.reshape(len(groups[0]), -1, columns), 'seq', 0,...  6.24 us
  transfers between devices with their start and end apart: 22, of which 14 were waited for; matrix products, arithmetic and copies ran while one was open for 4% of the time, Pallas kernels for 21%

profile of v2, /device:TPU:0, one launch (start us, length us, event | category | flops | bytes accessed | tf_op | source)
XLA Modules:
  0.0 195.0 jit_solution(16649076318727017723)
XLA Ops:
  2.7 2.9 %collective-permute-start.1 = (bf16[272,768]{1,0:T(8,128)(2,1)S(1)}, bf16[272,768]{1,0:T(8,128)(2,1)S(1)}, u32[]{:S(2)}, u32[]{:S(2)}) collective-permute-start(bf16[272,768]{1,0:T(8,128)(2,1)S(1)} %get-tuple-element.82), channel_id=1, source_target_pairs={{0,6},{2,4},{4,2},{6,0},{8,14},{10,12},{12,10},{14,8},{16,22},{18,... | collective-permute-start | bytes 1253384 | tf_op jit(solution)/shard_map/ppermute | solution.py:20
  6.5 13.2 %projection.1 = (bf16[256,1536]{1,0:T(8,128)(2,1)}, bf16[3072,1536]{1,0:T(8,128)(2,1)}) custom-call(bf16[256,3072]{1,0:T(8,128)(2,1)} %bitcast.38, bf16[3072,2,768]{2,1,0:T(2,128)(2,1)} %bitcast.37), custom_call_target="tpu_custom_call" | custom-call | flops 2415919104 | bytes 41943040 | tf_op jit(solution)/shard_map/projection/pallas_call | solution.py:88
  19.7 4.6 %collective-permute-done.1.q_b.c_b = bf16[272,768]{1,0:T(8,128)(2,1)S(1)} collective-permute-done((bf16[272,768]{1,0:T(8,128)(2,1)S(1)}, bf16[272,768]{1,0:T(8,128)(2,1)S(1)}, u32[]{:S(2)}, u32[]{:S(2)}) %collective-permute-start.1) | collective-permute-done | bytes 417824 | tf_op jit(solution)/shard_map/ppermute | solution.py:20
  27.0 4.0 %collective-permute-start.5 = (bf16[256,768]{1,0:T(8,128)(2,1)S(1)}, bf16[256,768]{1,0:T(8,128)(2,1)S(1)}, u32[]{:S(2)}, u32[]{:S(2)}) collective-permute-start(bf16[256,768]{1,0:T(8,128)(2,1)S(1)} %get-tuple-element.74), channel_id=1, source_target_pairs={{0,70},{2,68},{4,66},{6,64},{8,78},{10,76},{12,74},{14,72},{16,86}... | collective-permute-start | bytes 1179656 | tf_op jit(solution)/shard_map/ppermute | solution.py:33
  33.3 3.3 %collective-permute-start.4 = (bf16[256,768]{1,0:T(8,128)(2,1)S(1)}, bf16[256,768]{1,0:T(8,128)(2,1)}, u32[]{:S(2)}, u32[]{:S(2)}) collective-permute-start(bf16[256,768]{1,0:T(8,128)(2,1)S(1)} %get-tuple-element.75), channel_id=1, source_target_pairs={{0,68},{2,70},{4,64},{6,66},{8,76},{10,78},{12,72},{14,74},{16,84}... | collective-permute-start | bytes 1179656 | tf_op jit(solution)/shard_map/ppermute | solution.py:33
  36.5 3.4 %collective-permute-done.7.refs_5_ = bf16[256,768]{1,0:T(8,128)(2,1)S(1)} collective-permute-done((bf16[256,768]{1,0:T(8,128)(2,1)S(1)}, bf16[256,768]{1,0:T(8,128)(2,1)S(1)}, u32[]{:S(2)}, u32[]{:S(2)}) %collective-permute-start.7) | collective-permute-done | bytes 393248 | tf_op jit(solution)/shard_map/ppermute | solution.py:33
  42.2 5.3 %collective-permute-done.6.refs_4_ = bf16[256,768]{1,0:T(8,128)(2,1)} collective-permute-done((bf16[256,768]{1,0:T(8,128)(2,1)S(1)}, bf16[256,768]{1,0:T(8,128)(2,1)}, u32[]{:S(2)}, u32[]{:S(2)}) %collective-permute-start.6) | collective-permute-done | bytes 393248 | tf_op jit(solution)/shard_map/ppermute | solution.py:33
  47.6 11.6 %collective-permute-done.4.refs_2_ = bf16[256,768]{1,0:T(8,128)(2,1)} collective-permute-done((bf16[256,768]{1,0:T(8,128)(2,1)S(1)}, bf16[256,768]{1,0:T(8,128)(2,1)}, u32[]{:S(2)}, u32[]{:S(2)}) %collective-permute-start.4) | collective-permute-done | bytes 393248 | tf_op jit(solution)/shard_map/ppermute | solution.py:33
  59.1 2.1 %constant_dynamic-slice_fusion = bf16[256,1536]{1,0:T(8,128)(2,1)} fusion(bf16[256,3072]{1,0:T(8,128)(2,1)} %bitcast.39, s32[]{:T(128)S(6)} %select_n.122), kind=kLoop, calls=%fused_computation.25 | loop fusion | bytes 1572868 | tf_op jit(solution)/shard_map/dynamic_slice | solution.py:273
  63.8 15.2 %attention.1 = (bf16[256,768]{1,0:T(8,128)(2,1)}, bf16[256,768]{1,0:T(8,128)(2,1)}, bf16[512,768]{1,0:T(8,128)(2,1)}, bf16[512,768]{1,0:T(8,128)(2,1)}, bf16[512,768]{1,0:T(8,128)(2,1)}) custom-call(s32[7]{0:T(128)} %concatenate.34.meta, bf16[272,768]{1,0:T(8,128)(2,1)} %copy-done.4, bf16[272,768]{1,0:T(8,128)(2,1)} %copy-done.4, ...), custom_call_target="tpu_custom_call" | custom-call | flops 2516582400 | bytes 8388608 | tf_op jit(solution)/shard_map/attention/pallas_call | solution.py:186
  79.1 2.5 %collective-permute-start.9 = (bf16[512,768]{1,0:T(8,128)(2,1)}, bf16[512,768]{1,0:T(8,128)(2,1)S(1)}, u32[]{:S(2)}, u32[]{:S(2)}) collective-permute-start(bf16[512,768]{1,0:T(8,128)(2,1)} %get-tuple-element.46), channel_id=1, source_target_pairs={{0,68},{2,70},{4,64},{6,66},{8,76},{10,78},{12,72},{14,74},{16,84}... | collective-permute-start | bytes 2359304 | tf_op jit(solution)/shard_map/ppermute | solution.py:33
  84.1 16.1 %collective-permute-done.9 = bf16[512,768]{1,0:T(8,128)(2,1)S(1)} collective-permute-done((bf16[512,768]{1,0:T(8,128)(2,1)}, bf16[512,768]{1,0:T(8,128)(2,1)S(1)}, u32[]{:S(2)}, u32[]{:S(2)}) %collective-permute-start.9) | collective-permute-done | bytes 786464 | tf_op jit(solution)/shard_map/ppermute | solution.py:33
  102.9 3.4 %collective-permute-start.15 = (bf16[256,768]{1,0:T(8,128)(2,1)S(1)}, bf16[256,768]{1,0:T(8,128)(2,1)S(1)}, u32[]{:S(2)}, u32[]{:S(2)}) collective-permute-start(bf16[256,768]{1,0:T(8,128)(2,1)S(1)} %copy-done.8), channel_id=1, source_target_pairs={{0,6},{2,4},{4,2},{6,0},{8,14},{10,12},{12,10},{14,8},{16,22},{18,... | collective-permute-start | bytes 1179656 | tf_op jit(solution)/shard_map/ppermute | solution.py:20
  108.5 4.7 %collective-permute-done.14 = bf16[256,768]{1,0:T(8,128)(2,1)S(1)} collective-permute-done((bf16[256,768]{1,0:T(8,128)(2,1)S(1)}, bf16[256,768]{1,0:T(8,128)(2,1)S(1)}, u32[]{:S(2)}, u32[]{:S(2)}) %collective-permute-start.14) | collective-permute-done | bytes 393248 | tf_op jit(solution)/shard_map/ppermute | solution.py:20
  113.1 2.5 %collective-permute-done.15 = bf16[256,768]{1,0:T(8,128)(2,1)S(1)} collective-permute-done((bf16[256,768]{1,0:T(8,128)(2,1)S(1)}, bf16[256,768]{1,0:T(8,128)(2,1)S(1)}, u32[]{:S(2)}, u32[]{:S(2)}) %collective-permute-start.15) | collective-permute-done | bytes 393248 | tf_op jit(solution)/shard_map/ppermute | solution.py:20
  116.7 7.0 %context_partial.1 = bf16[256,3072]{1,0:T(8,128)(2,1)} custom-call(bf16[256,1536]{1,0:T(8,128)(2,1)} %pad_maximum_fusion.grad, bf16[3072,1536]{1,0:T(8,128)(2,1)} %get-tuple-element.55.weight), custom_call_target="tpu_custom_call" | custom-call | flops 2415919104 | bytes 12582912 | tf_op jit(solution)/shard_map/context_partial/pallas_call | solution.py:246
  124.8 3.7 %collective-permute-start.18 = (bf16[256,1024]{1,0:T(8,128)(2,1)S(1)}, bf16[256,1024]{1,0:T(8,128)(2,1)S(1)}, u32[]{:S(2)}, u32[]{:S(2)}) collective-permute-start(bf16[256,1024]{1,0:T(8,128)(2,1)S(1)} %slice.44), channel_id=1, source_target_pairs={{0,1},{1,0},{2,3},{3,2},{4,5},{5,4},{6,7},{7,6},{8,9},{9,8},{10,11... | collective-permute-start | bytes 1572872 | tf_op jit(solution)/shard_map/ppermute | solution.py:20
  130.1 5.7 %weight_partial.1 = bf16[1536,768]{1,0:T(8,128)(2,1)} custom-call(bf16[256,1536]{1,0:T(8,128)(2,1)S(1)} %dynamic-slice_bitcast_fusion.own, bf16[256,1536]{1,0:T(8,128)(2,1)S(1)} %collective-permute-done.11.own_z, bf16[256,1536]{1,0:T(8,128)(2,1)} %collective-permute-done.10.pair, bf16[256,1536]{1,0:T(8,128)(2,1)} %collective-permute-done.16.pair_z, ...), custom_call_target="tpu_custom_call" | custom-call | flops 2415919104 | bytes 8388608 | tf_op jit(solution)/shard_map/weight_partial/pallas_call | solution.py:223
  135.8 4.3 %collective-permute-done.18 = bf16[256,1024]{1,0:T(8,128)(2,1)S(1)} collective-permute-done((bf16[256,1024]{1,0:T(8,128)(2,1)S(1)}, bf16[256,1024]{1,0:T(8,128)(2,1)S(1)}, u32[]{:S(2)}, u32[]{:S(2)}) %collective-permute-start.18) | collective-permute-done | bytes 524320 | tf_op jit(solution)/shard_map/ppermute | solution.py:20
  140.9 6.2 %all-to-all-start = ((bf16[8,192,768]{2,1,0:T(8,128)(2,1)}), bf16[8,192,768]{2,1,0:T(8,128)(2,1)}, u32[]{:S(2)}, u32[]{:S(2)}) async-start(bf16[8,192,768]{2,1,0:T(8,128)(2,1)} %bitcast.16), calls=%async_computation | async-start | bytes 4718592 | tf_op jit(solution)/shard_map/all_to_all | solution.py:341
  147.2 3.5 %collective-permute-start.13 = (bf16[256,768]{1,0:T(8,128)(2,1)}, bf16[256,768]{1,0:T(8,128)(2,1)S(1)}, u32[]{:S(2)}, u32[]{:S(2)}) collective-permute-start(bf16[256,768]{1,0:T(8,128)(2,1)} %get-tuple-element.51), channel_id=1, source_target_pairs={{0,4},{2,6},{4,0},{6,2},{8,12},{10,14},{12,8},{14,10},{16,20},{18,... | collective-permute-start | bytes 1179656 | tf_op jit(solution)/shard_map/ppermute | solution.py:20
  150.8 3.3 %collective-permute-start.19 = (bf16[256,2048]{1,0:T(8,128)(2,1)S(1)}, bf16[256,2048]{1,0:T(8,128)(2,1)}, u32[]{:S(2)}, u32[]{:S(2)}) collective-permute-start(bf16[256,2048]{1,0:T(8,128)(2,1)S(1)} %slice.45), channel_id=1, source_target_pairs={{0,1},{1,0},{2,3},{3,2},{4,5},{5,4},{6,7},{7,6},{8,9},{9,8},{10,11... | collective-permute-start | bytes 3145736 | tf_op jit(solution)/shard_map/ppermute | solution.py:20
  154.1 29.1 %collective-permute-done.13 = bf16[256,768]{1,0:T(8,128)(2,1)S(1)} collective-permute-done((bf16[256,768]{1,0:T(8,128)(2,1)}, bf16[256,768]{1,0:T(8,128)(2,1)S(1)}, u32[]{:S(2)}, u32[]{:S(2)}) %collective-permute-start.13) | collective-permute-done | bytes 393248 | tf_op jit(solution)/shard_map/ppermute | solution.py:20
  188.8 2.2 %collective-permute-start.20 = (bf16[96,768]{1,0:T(8,128)(2,1)S(1)}, bf16[96,768]{1,0:T(8,128)(2,1)S(1)}, u32[]{:S(2)}, u32[]{:S(2)}) collective-permute-start(bf16[96,768]{1,0:T(8,128)(2,1)S(1)} %dynamic-slice_bitcast_fusion.5), channel_id=1, source_target_pairs={{0,2},{2,0},{4,6},{6,4},{8,10},{10,8},{12,14},{14,12},{16,18},{18,... | collective-permute-start | bytes 442376 | tf_op jit(solution)/shard_map/ppermute | solution.py:20
  (69 shorter events, 34.3 us)
Async XLA Ops:
  2.7 21.5 %collective-permute-start.1 = (bf16[272,768]{1,0:T(8,128)(2,1)S(1)}, bf16[272,768]{1,0:T(8,128)(2,1)S(1)}, u32[]{:S(2)}, u32[]{:S(2)}) collective-permute-start(bf16[272,768]{1,0:T(8,128)(2,1)S(1)} %get-tuple-element.82), channel_id=1, source_target_pairs={{0,6},{2,4},{4,2},{6,0},{8,14},{10,12},{12,10},{14,8},{16,22},{18,... | collective-permute-start | bytes 1253384 | tf_op jit(solution)/shard_map/ppermute | solution.py:20
  5.7 18.6 %collective-permute-start = (bf16[272,768]{1,0:T(8,128)(2,1)S(1)}, bf16[272,768]{1,0:T(8,128)(2,1)S(1)}, u32[]{:S(2)}, u32[]{:S(2)}) collective-permute-start(bf16[272,768]{1,0:T(8,128)(2,1)S(1)} %get-tuple-element.83), channel_id=1, source_target_pairs={{0,4},{2,6},{4,0},{6,2},{8,12},{10,14},{12,8},{14,10},{16,20},{18,... | collective-permute-start | bytes 1253384 | tf_op jit(solution)/shard_map/ppermute | solution.py:20
  24.3 38.9 %copy-start.3 = (bf16[272,768]{1,0:T(8,128)(2,1)}, bf16[272,768]{1,0:T(8,128)(2,1)S(1)}, u32[]{:S(2)}) copy-start(bf16[272,768]{1,0:T(8,128)(2,1)S(1)} %collective-permute-done.1.q_b.c_b) | copy-start | bytes 1253380
  24.3 38.9 %copy-start.4 = (bf16[272,768]{1,0:T(8,128)(2,1)}, bf16[272,768]{1,0:T(8,128)(2,1)S(1)}, u32[]{:S(2)}) copy-start(bf16[272,768]{1,0:T(8,128)(2,1)S(1)} %collective-permute-done.q_a.c_a) | copy-start | bytes 1253380
  25.7 14.2 %collective-permute-start.7 = (bf16[256,768]{1,0:T(8,128)(2,1)S(1)}, bf16[256,768]{1,0:T(8,128)(2,1)S(1)}, u32[]{:S(2)}, u32[]{:S(2)}) collective-permute-start(bf16[256,768]{1,0:T(8,128)(2,1)S(1)} %get-tuple-element.74), channel_id=1, source_target_pairs={{4,78},{6,76},{8,66},{10,64},{12,86},{14,84},{16,74},{18,72},{20,9... | collective-permute-start | bytes 1179656 | tf_op jit(solution)/shard_map/ppermute | solution.py:33
  27.0 14.8 %collective-permute-start.5 = (bf16[256,768]{1,0:T(8,128)(2,1)S(1)}, bf16[256,768]{1,0:T(8,128)(2,1)S(1)}, u32[]{:S(2)}, u32[]{:S(2)}) collective-permute-start(bf16[256,768]{1,0:T(8,128)(2,1)S(1)} %get-tuple-element.74), channel_id=1, source_target_pairs={{0,70},{2,68},{4,66},{6,64},{8,78},{10,76},{12,74},{14,72},{16,86}... | collective-permute-start | bytes 1179656 | tf_op jit(solution)/shard_map/ppermute | solution.py:33
  31.1 11.2 %collective-permute-start.3 = (bf16[256,768]{1,0:T(8,128)(2,1)S(1)}, bf16[256,768]{1,0:T(8,128)(2,1)S(1)}, u32[]{:S(2)}, u32[]{:S(2)}) collective-permute-start(bf16[256,768]{1,0:T(8,128)(2,1)S(1)} %get-tuple-element.74), channel_id=1, source_target_pairs={{0,66},{2,64},{4,70},{6,68},{8,74},{10,72},{12,78},{14,76},{16,82}... | collective-permute-start | bytes 1179656 | tf_op jit(solution)/shard_map/ppermute | solution.py:33
  32.0 15.6 %collective-permute-start.6 = (bf16[256,768]{1,0:T(8,128)(2,1)S(1)}, bf16[256,768]{1,0:T(8,128)(2,1)}, u32[]{:S(2)}, u32[]{:S(2)}) collective-permute-start(bf16[256,768]{1,0:T(8,128)(2,1)S(1)} %get-tuple-element.75), channel_id=1, source_target_pairs={{4,76},{6,78},{8,64},{10,66},{12,84},{14,86},{16,72},{18,74},{20,9... | collective-permute-start | bytes 1179656 | tf_op jit(solution)/shard_map/ppermute | solution.py:33
  33.3 25.9 %collective-permute-start.4 = (bf16[256,768]{1,0:T(8,128)(2,1)S(1)}, bf16[256,768]{1,0:T(8,128)(2,1)}, u32[]{:S(2)}, u32[]{:S(2)}) collective-permute-start(bf16[256,768]{1,0:T(8,128)(2,1)S(1)} %get-tuple-element.75), channel_id=1, source_target_pairs={{0,68},{2,70},{4,64},{6,66},{8,76},{10,78},{12,72},{14,74},{16,84}... | collective-permute-start | bytes 1179656 | tf_op jit(solution)/shard_map/ppermute | solution.py:33
  39.9 19.2 %collective-permute-start.2 = (bf16[256,768]{1,0:T(8,128)(2,1)S(1)}, bf16[256,768]{1,0:T(8,128)(2,1)}, u32[]{:S(2)}, u32[]{:S(2)}) collective-permute-start(bf16[256,768]{1,0:T(8,128)(2,1)S(1)} %get-tuple-element.75), channel_id=1, source_target_pairs={{0,64},{64,0},{1,65},{65,1},{2,66},{66,2},{3,67},{67,3},{4,68},{68... | collective-permute-start | bytes 1179656 | tf_op jit(solution)/shard_map/ppermute | solution.py:20
  61.2 20.3 %collective-permute-start.11 = (bf16[256,1536]{1,0:T(8,128)(2,1)}, bf16[256,1536]{1,0:T(8,128)(2,1)S(1)}, u32[]{:S(2)}, u32[]{:S(2)}) collective-permute-start(bf16[256,1536]{1,0:T(8,128)(2,1)} %constant_dynamic-slice_fusion), channel_id=1, source_target_pairs={{0,32},{2,34},{4,36},{6,38},{8,40},{10,42},{12,44},{14,46},{16,48}... | collective-permute-start | bytes 2359304 | tf_op jit(solution)/shard_map/ppermute | solution.py:20
  63.1 19.1 %collective-permute-start.10 = (bf16[256,1536]{1,0:T(8,128)(2,1)S(1)}, bf16[256,1536]{1,0:T(8,128)(2,1)}, u32[]{:S(2)}, u32[]{:S(2)}) collective-permute-start(bf16[256,1536]{1,0:T(8,128)(2,1)S(1)} %dynamic-slice_bitcast_fusion.own), channel_id=1, source_target_pairs={{0,2},{2,0},{4,6},{6,4},{8,10},{10,8},{12,14},{14,12},{16,18},{18,... | collective-permute-start | bytes 2359304 | tf_op jit(solution)/shard_map/ppermute | solution.py:20
  79.0 5.1 %collective-permute-start.8 = (bf16[512,768]{1,0:T(8,128)(2,1)}, bf16[512,768]{1,0:T(8,128)(2,1)S(1)}, u32[]{:S(2)}, u32[]{:S(2)}) collective-permute-start(bf16[512,768]{1,0:T(8,128)(2,1)} %get-tuple-element.45), channel_id=1, source_target_pairs={{0,64},{64,0},{1,65},{65,1},{2,66},{66,2},{3,67},{67,3},{4,68},{68... | collective-permute-start | bytes 2359304 | tf_op jit(solution)/shard_map/ppermute | solution.py:20
  79.1 21.1 %collective-permute-start.9 = (bf16[512,768]{1,0:T(8,128)(2,1)}, bf16[512,768]{1,0:T(8,128)(2,1)S(1)}, u32[]{:S(2)}, u32[]{:S(2)}) collective-permute-start(bf16[512,768]{1,0:T(8,128)(2,1)} %get-tuple-element.46), channel_id=1, source_target_pairs={{0,68},{2,70},{4,64},{6,66},{8,76},{10,78},{12,72},{14,74},{16,84}... | collective-permute-start | bytes 2359304 | tf_op jit(solution)/shard_map/ppermute | solution.py:33
  82.2 18.8 %collective-permute-start.12 = (bf16[512,768]{1,0:T(8,128)(2,1)}, bf16[512,768]{1,0:T(8,128)(2,1)S(1)}, u32[]{:S(2)}, u32[]{:S(2)}) collective-permute-start(bf16[512,768]{1,0:T(8,128)(2,1)} %get-tuple-element.50), channel_id=1, source_target_pairs={{0,72},{2,74},{8,80},{10,82},{12,68},{14,70},{16,88},{18,90},{20,7... | collective-permute-start | bytes 2359304 | tf_op jit(solution)/shard_map/ppermute | solution.py:33
  101.4 11.8 %collective-permute-start.14 = (bf16[256,768]{1,0:T(8,128)(2,1)S(1)}, bf16[256,768]{1,0:T(8,128)(2,1)S(1)}, u32[]{:S(2)}, u32[]{:S(2)}) collective-permute-start(bf16[256,768]{1,0:T(8,128)(2,1)S(1)} %slice.41), channel_id=1, source_target_pairs={{0,2},{2,0},{4,6},{6,4},{8,10},{10,8},{12,14},{14,12},{16,18},{18,... | collective-permute-start | bytes 1179656 | tf_op jit(solution)/shard_map/ppermute | solution.py:20
  102.9 12.8 %collective-permute-start.15 = (bf16[256,768]{1,0:T(8,128)(2,1)S(1)}, bf16[256,768]{1,0:T(8,128)(2,1)S(1)}, u32[]{:S(2)}, u32[]{:S(2)}) collective-permute-start(bf16[256,768]{1,0:T(8,128)(2,1)S(1)} %copy-done.8), channel_id=1, source_target_pairs={{0,6},{2,4},{4,2},{6,0},{8,14},{10,12},{12,10},{14,8},{16,22},{18,... | collective-permute-start | bytes 1179656 | tf_op jit(solution)/shard_map/ppermute | solution.py:20
  106.3 23.8 %collective-permute-start.17 = (bf16[512,768]{1,0:T(8,128)(2,1)S(1)}, bf16[512,768]{1,0:T(8,128)(2,1)S(1)}, u32[]{:S(2)}, u32[]{:S(2)}) collective-permute-start(bf16[512,768]{1,0:T(8,128)(2,1)S(1)} %add_convert_fusion.1.grad), channel_id=1, source_target_pairs={{0,32},{2,34},{4,36},{6,38},{8,40},{10,42},{12,44},{14,46},{16,48}... | collective-permute-start | bytes 2359304 | tf_op jit(solution)/shard_map/ppermute | solution.py:20
  106.7 23.4 %collective-permute-start.16 = (bf16[256,1536]{1,0:T(8,128)(2,1)S(1)}, bf16[256,1536]{1,0:T(8,128)(2,1)}, u32[]{:S(2)}, u32[]{:S(2)}) collective-permute-start(bf16[256,1536]{1,0:T(8,128)(2,1)S(1)} %collective-permute-done.11.own_z), channel_id=1, source_target_pairs={{0,2},{2,0},{4,6},{6,4},{8,10},{10,8},{12,14},{14,12},{16,18},{18,... | collective-permute-start | bytes 2359304 | tf_op jit(solution)/shard_map/ppermute | solution.py:20
  124.8 15.4 %collective-permute-start.18 = (bf16[256,1024]{1,0:T(8,128)(2,1)S(1)}, bf16[256,1024]{1,0:T(8,128)(2,1)S(1)}, u32[]{:S(2)}, u32[]{:S(2)}) collective-permute-start(bf16[256,1024]{1,0:T(8,128)(2,1)S(1)} %slice.44), channel_id=1, source_target_pairs={{0,1},{1,0},{2,3},{3,2},{4,5},{5,4},{6,7},{7,6},{8,9},{9,8},{10,11... | collective-permute-start | bytes 1572872 | tf_op jit(solution)/shard_map/ppermute | solution.py:20
  140.9 45.8 %all-to-all-start = ((bf16[8,192,768]{2,1,0:T(8,128)(2,1)}), bf16[8,192,768]{2,1,0:T(8,128)(2,1)}, u32[]{:S(2)}, u32[]{:S(2)}) async-start(bf16[8,192,768]{2,1,0:T(8,128)(2,1)} %bitcast.16), calls=%async_computation | async-start | bytes 4718592 | tf_op jit(solution)/shard_map/all_to_all | solution.py:341
  147.2 36.0 %collective-permute-start.13 = (bf16[256,768]{1,0:T(8,128)(2,1)}, bf16[256,768]{1,0:T(8,128)(2,1)S(1)}, u32[]{:S(2)}, u32[]{:S(2)}) collective-permute-start(bf16[256,768]{1,0:T(8,128)(2,1)} %get-tuple-element.51), channel_id=1, source_target_pairs={{0,4},{2,6},{4,0},{6,2},{8,12},{10,14},{12,8},{14,10},{16,20},{18,... | collective-permute-start | bytes 1179656 | tf_op jit(solution)/shard_map/ppermute | solution.py:20
  150.8 34.3 %collective-permute-start.19 = (bf16[256,2048]{1,0:T(8,128)(2,1)S(1)}, bf16[256,2048]{1,0:T(8,128)(2,1)}, u32[]{:S(2)}, u32[]{:S(2)}) collective-permute-start(bf16[256,2048]{1,0:T(8,128)(2,1)S(1)} %slice.45), channel_id=1, source_target_pairs={{0,1},{1,0},{2,3},{3,2},{4,5},{5,4},{6,7},{7,6},{8,9},{9,8},{10,11... | collective-permute-start | bytes 3145736 | tf_op jit(solution)/shard_map/ppermute | solution.py:20
  188.8 5.3 %collective-permute-start.20 = (bf16[96,768]{1,0:T(8,128)(2,1)S(1)}, bf16[96,768]{1,0:T(8,128)(2,1)S(1)}, u32[]{:S(2)}, u32[]{:S(2)}) collective-permute-start(bf16[96,768]{1,0:T(8,128)(2,1)S(1)} %dynamic-slice_bitcast_fusion.5), channel_id=1, source_target_pairs={{0,2},{2,0},{4,6},{6,4},{8,10},{10,8},{12,14},{14,12},{16,18},{18,... | collective-permute-start | bytes 442376 | tf_op jit(solution)/shard_map/ppermute | solution.py:20
  (7 other events, 96.9 us)

commit v3 on v2

--- a/solution.py
+++ b/solution.py
@@ -10,6 +10,7 @@
 HD = 128
 REACH = 2
 NEG_FILL = -1e30
+LOG2E = 1.4426950408889634
 F32, BF16 = jnp.float32, jnp.bfloat16
 ZS, YS, XS = 2, 4, 4
 PAIR = 2
@@ -58,7 +59,7 @@
     return lax.dot_general(a, b, ((dims[0], dims[1]), ((), ())), preferred_element_type=F32)
 
 
-def projection_kernel(context, weight, kv, weight_out, total):
+def projection_kernel(which, context, weight, kv, weight_out, total):
     step = pl.program_id(0)
     sides = jnp.swapaxes(weight[...], 0, 1)
     heads = sides.shape[2] // HD
@@ -81,32 +82,35 @@
         kv[...] = total[...].astype(BF16)
 
 
-def projection(context, weight):
+def projection(which, context, weight):
     rows, width = context.shape
-    columns = weight.shape[2]
-    depth = width // 4
+    columns = weight.shape[2] // 2
+    depth = width // 3
     return pl.pallas_call(
         projection_kernel,
         out_shape=[
             jax.ShapeDtypeStruct((rows, 2 * columns), BF16),
             jax.ShapeDtypeStruct((width, 2 * columns), BF16),
         ],
-        grid=(width // depth,),
-        in_specs=[
-            pl.BlockSpec((rows, depth), lambda i: (0, i)),
-            pl.BlockSpec((depth, 2, columns), lambda i: (i, 0, 0)),
-        ],
-        out_specs=[
-            pl.BlockSpec((rows, 2 * columns), lambda i: (0, 0)),
-            pl.BlockSpec((depth, 2 * columns), lambda i: (i, 0)),
-        ],
-        scratch_shapes=[pltpu.VMEM((rows, 2 * columns), F32)],
+        grid_spec=pltpu.PrefetchScalarGridSpec(
+            num_scalar_prefetch=1,
+            grid=(width // depth,),
+            in_specs=[
+                pl.BlockSpec((rows, depth), lambda i, w: (0, i)),
+                pl.BlockSpec((depth, 2, columns), lambda i, w: (i, 0, w[0])),
+            ],
+            out_specs=[
+                pl.BlockSpec((rows, 2 * columns), lambda i, w: (0, 0)),
+                pl.BlockSpec((depth, 2 * columns), lambda i, w: (i, 0)),
+            ],
+            scratch_shapes=[pltpu.VMEM((rows, 2 * columns), F32)],
+        ),
         compiler_params=pltpu.CompilerParams(vmem_limit_bytes=60 * 2**20),
         cost_estimate=pl.CostEstimate(
-            flops=4 * rows * width * columns, bytes_accessed=40 * 2**20, transcendentals=0
+            flops=4 * rows * width * columns, bytes_accessed=20 * 2**20, transcendentals=0
         ),
         name="projection",
-    )(context, weight)
+    )(which.reshape(1), context, weight)
 
 
 def attention_kernel(meta, q_a, c_a, q_b, c_b, *refs):
@@ -115,6 +119,8 @@
     rows, heads = q_a.shape[0], od_a.shape[1] // (2 * HD)
     member, side = meta[0], meta[6]
     scale = HD ** (-0.5)
+    unit = scale * LOG2E
+    results = []
     near, far = 4 * side, 4 * (1 - side)
     order = (near + member, near + 1 - member, 2 + member, 3 - member, far + member, far + 1 - member)
     for ref, place in zip(kv_refs, order):
@@ -131,38 +137,36 @@
         keys = kv_s[window, :HD]
         values = kv_s[window, HD:]
         low, high = meta[2 + 2 * i], meta[3 + 2 * i]
-        scores = dot(keys, q, ((1,), (1,))) * scale
-        blocks = []
+        scores = dot(keys, q, ((1,), (1,)))
+        block = lambda v, j: v[j * rows : (j + 1) * rows]
+        offsets = []
         for j in range(span):
             shard = meta[1] + i + j
-            keep = (shard >= low) & (shard <= high)
-            blocks.append(jnp.where(keep, scores[j * rows : (j + 1) * rows], NEG_FILL))
-        scores = jnp.concatenate(blocks, axis=0)
-        expo = jnp.exp(scores - jnp.max(scores, axis=0, keepdims=True))
-        probs = expo * (1.0 / jnp.sum(expo, axis=0, keepdims=True))
+            offsets.append(jnp.where((shard >= low) & (shard <= high), 0.0, NEG_FILL))
+        row_max = functools.reduce(
+            jnp.maximum,
+            [jnp.max(block(scores, j), axis=0, keepdims=True) + offsets[j] for j in range(span)],
+        )
+        expo = [
+            jnp.exp2(block(scores, j) * unit + (offsets[j] - row_max * unit)) for j in range(span)
+        ]
+        norm = functools.reduce(jnp.add, [jnp.sum(e, axis=0, keepdims=True) for e in expo])
+        probs = jnp.concatenate(expo, axis=0) * (1.0 / norm)
         rounded = probs.astype(BF16)
         dprobs = dot(values, c, ((1,), (1,)))
         delta = jnp.sum(dprobs * probs, axis=0, keepdims=True)
-        dscores = (probs * (dprobs - delta) * scale).astype(BF16)
+        dscores = (probs * (dprobs - delta)).astype(BF16)
         out = dot(values, rounded, ((0,), (0,)))
-        dq = dot(keys, dscores, ((0,), (0,)))
+        dq = dot(keys, dscores, ((0,), (0,))) * scale
         g_s[window, :HD] += dot(dscores, q, ((1,), (0,)))
         g_s[window, HD:] += dot(rounded, c, ((1,), (0,)))
-        head = pl.program_id(0)
-        parts = [
-            (value.T.astype(BF16), pl.ds(pl.multiple_of((side_ * heads + head) * HD, HD), HD))
-            for side_, value in enumerate((out, dq))
-        ]
-
-        @pl.when(member == i)
-        def _():
-            for value, columns in parts:
-                od_a[:, columns] = value
-
-        @pl.when(member != i)
-        def _():
-            for value, columns in parts:
-                od_b[:, columns] = value
+        results.append([value.T.astype(BF16) for value in (out, dq)])
+    head = pl.program_id(0)
+    for part, (first, second) in enumerate(zip(*results)):
+        columns = pl.ds(pl.multiple_of((part * heads + head) * HD, HD), HD)
+        od_a[:, columns] = jnp.where(member == 0, first, second)
+        od_b[:, columns] = jnp.where(member == 0, second, first)
+    g_s[:, :HD] *= scale
 
     for index, place in enumerate(order):
         begin = index % PAIR * rows
@@ -235,29 +239,30 @@
     )(*contexts, *grads)
 
 
-def context_kernel(grad, weight, out):
-    out[...] = dot(grad[...], weight[...], ((1,), (1,))).astype(BF16)
-
-
-def context_partial(grad, weight):
-    rows, columns = grad.shape
-    width = weight.shape[0]
+def context_kernel(grad, grad_next, weight, weight_next, out):
+    total = dot(grad[...], weight[...], ((1,), (1,)))
+    total += dot(grad_next[...], weight_next[...], ((1,), (1,)))
+    out[...] = total.astype(BF16)
+
+
+def context_partial(returned, other_rows, weight_same, weight_next):
+    rows, columns = other_rows.shape
+    width = weight_same.shape[0]
     block = width // 4
+    grad = pl.BlockSpec((rows, columns), lambda i: (0, 0))
+    weight = pl.BlockSpec((block, columns), lambda i: (i, 0))
     return pl.pallas_call(
         context_kernel,
         out_shape=jax.ShapeDtypeStruct((rows, width), BF16),
         grid=(width // block,),
-        in_specs=[
-            pl.BlockSpec((rows, columns), lambda i: (0, 0)),
-            pl.BlockSpec((block, columns), lambda i: (i, 0)),
-        ],
+        in_specs=[grad, grad, weight, weight],
         out_specs=pl.BlockSpec((rows, block), lambda i: (0, i)),
         compiler_params=pltpu.CompilerParams(vmem_limit_bytes=60 * 2**20),
         cost_estimate=pl.CostEstimate(
-            flops=2 * rows * width * columns, bytes_accessed=12 * 2**20, transcendentals=0
+            flops=4 * rows * width * columns, bytes_accessed=12 * 2**20, transcendentals=0
         ),
         name="context_partial",
-    )(grad, weight)
+    )(returned, other_rows, weight_same, weight_next)
 
 
 def local(queries, context, kv_weight, spans, cotangent):
@@ -289,9 +294,10 @@
     qc_a = moved(qc_of(member), "seq", same_x)
     qc_b = moved(qc_of(1 - member), "seq", cross_x)
 
-    local_kv, weight = projection(context, kv_weight[0])
-    local_kv, qc_a, qc_b = lax.optimization_barrier((local_kv, qc_a, qc_b))
-    same_half, next_half = half_of(local_kv, member), half_of(local_kv, 1 - member)
+    next_half, weight_next = projection(1 - member, context, kv_weight[0])
+    late_context, _ = lax.optimization_barrier((context, next_half))
+    same_half, weight_same = projection(member, late_context, kv_weight[0])
+    same_half, qc_a, qc_b = lax.optimization_barrier((same_half, qc_a, qc_b))
     kv_blocks = [
         swapped(same_half, "tower"),
         moved_across(next_half, pair_x),
@@ -301,8 +307,10 @@
         moved_across(next_half, next_row(False, 1)),
     ]
     ctx_own = half_of(context, z)
-    kv_blocks, late_own, late_context = lax.optimization_barrier((kv_blocks, ctx_own, context))
-    ctx_z = moved(half_of(late_context, 1 - z), "seq", across_z())
+    kv_blocks, late_own, ctx_rest = lax.optimization_barrier(
+        (kv_blocks, ctx_own, half_of(context, 1 - z))
+    )
+    ctx_z = moved(ctx_rest, "seq", across_z())
     ctx_pair = moved(late_own, "seq", pair_x)
 
     span_a, span_b = qc_a[rows, :2].astype(jnp.int32), qc_b[rows, :2].astype(jnp.int32)
@@ -313,41 +321,37 @@
     od_a, od_b, g_near, g_mid, g_far = attention(meta, qc_a, qc_b, kv_blocks)
 
     g_mid = moved_across(g_mid, same_x)
-    g_far, ctx_pair, ctx_z = lax.optimization_barrier((g_far, ctx_pair, ctx_z))
+    g_near, ctx_pair, ctx_z = lax.optimization_barrier((g_near, ctx_pair, ctx_z))
     g_far = moved_across(g_far, next_row(True, 0))
     returned = total([swapped(g_near, "tower"), g_mid, g_far]).astype(BF16)
     late_z, _ = lax.optimization_barrier((ctx_z, returned))
     ctx_pair_z = moved(late_z, "seq", pair_x)
     returned_z = moved(returned, "seq", across_z())
     other_rows = moved(returned[rows:], "seq", pair_x)
-    od_a, od_b, _ = lax.optimization_barrier((od_a, od_b, returned))
-    od_a, od_b = moved(od_a, "seq", same_x), moved(od_b, "seq", cross_x)
+    od_b, _ = lax.optimization_barrier((od_b, returned))
+    od_b = moved(od_b, "seq", cross_x)
     other_rows, od_b = lax.optimization_barrier((other_rows, od_b))
-    own_shard = in_order(returned[:rows], other_rows)
-    partial_ctx = context_partial(own_shard, weight)
+    partial_ctx = context_partial(returned, other_rows, weight_same, weight_next)
+    od_a, _ = lax.optimization_barrier((od_a, partial_ctx))
+    od_a = moved(od_a, "seq", same_x)
     sum_parts = [partial_ctx[:, : width // 3], partial_ctx[:, width // 3 :]]
     sum_first = swapped(sum_parts[0], "mp")
 
 
     partial_w = weight_partial([ctx_own, ctx_z, ctx_pair, ctx_pair_z], [returned, returned_z])
-    partial_w, sum_first = lax.optimization_barrier((partial_w, sum_first))
+    partial_w, sum_first, od_a = lax.optimization_barrier((partial_w, sum_first, od_a))
     late_half, _ = lax.optimization_barrier((sum_parts[1], sum_first))
     sum_second = swapped(late_half, "mp")
-    groups = [
-        [(z_ * YS + y) * XS + PAIR * s + m for y in range(YS) for s in range(XS // PAIR)]
-        for z_ in range(ZS)
-        for m in range(PAIR)
-    ]
+    plane = YS * XS
+    groups = [[z_ * plane + i for i in range(plane)] for z_ in range(ZS)]
     parts = lax.all_to_all(
-        partial_w.reshape(len(groups[0]), -1, columns), "seq", 0, 0, axis_index_groups=groups
-    )
-    half_grad = jnp.sum(parts.astype(F32), axis=0).astype(BF16).reshape(PAIR, -1, columns)
-    own_rows = lax.dynamic_index_in_dim(half_grad, member, 0, keepdims=False)
-    pair_rows = lax.dynamic_index_in_dim(half_grad, 1 - member, 0, keepdims=False)
+        partial_w.reshape(plane, -1, columns), "seq", 0, 0, axis_index_groups=groups
+    )
     weight_grad = (
-        in_order(own_rows, moved(pair_rows, "seq", pair_x))
-        .reshape(-1, heads, 2, HD)
-        .transpose(0, 2, 1, 3)
+        jnp.sum(parts.reshape(plane // PAIR, PAIR, -1, columns).astype(F32), axis=0)
+        .astype(BF16)
+        .reshape(PAIR, -1, heads // PAIR, 2, HD)
+        .transpose(1, 3, 0, 2, 4)
         .reshape(1, -1, 2, columns)
     )
 

time: 196 us -> 172 us (0.88)
  waiting for transfers between devices: 86.9 us -> 70.4 us
  starting transfers between devices: 46.9 us -> 41.3 us
  other arithmetic: 8.87 us -> 6.57 us
    ppermute x14 -> x13, waiting for transfers between devices: 49.4 us -> 34.2 us  [moved(): return lax.ppermute(value, axis, pairs)]
    ppermute x7, waiting for transfers between devices: 37.5 us -> 28.1 us  [moved_across(): return lax.ppermute(value, ('tower', 'seq'), both)]
    all_to_all x1, waiting for transfers between devices: 0.01 us -> 8.06 us  [local(): lax.all_to_all(partial_w.reshape(plane, -1, columns), 'seq', 0, 0, axis_i...]
    ppermute x14 -> x13, starting transfers between devices: 25.6 us -> 21.9 us  [moved(): return lax.ppermute(value, axis, pairs)]
    pallas_call x1 -> x2, Pallas kernels: 13.2 us -> 16.6 us  [projection(): pl.pallas_call(projection_kernel, out_shape=[jax.ShapeDtypeStruct((rows,...]
    unnamed x18 -> x32, local copies, waits for them, and re-layouts: 1.6 us -> 3.84 us
    dynamic_slice x4 -> x2, local copies, waits for them, and re-layouts: 6.04 us -> 3.81 us  [local(): lax.dynamic_slice_in_dim(v, which * (v.shape[1] // 2), v.shape[1] // 2, a...]
  transfers between devices with their start and end apart: 22 -> 21, of which waited for: 14 -> 10; matrix products, arithmetic and copies ran while one was open for 4% -> 5% of each run, Pallas kernels for 21% -> 25%
where the time goes in v3:
time: 172 us
  waiting for transfers between devices  70.4 us (41%)
  Pallas kernels  42.9 us (25%)
  starting transfers between devices  41.3 us (24%)
  local copies, waits for them, and re-layouts  9.55 us (6%)
  other arithmetic  6.57 us (4%)
    ppermute x13, waiting for transfers between devices, moved(): return lax.ppermute(value, axis, pairs)  34.2 us
    ppermute x7, waiting for transfers between devices, moved_across(): return lax.ppermute(value, ('tower', 'seq'), both)  28.1 us
    ppermute x13, starting transfers between devices, moved(): return lax.ppermute(value, axis, pairs)  21.9 us
    pallas_call x2, Pallas kernels, projection(): pl.pallas_call(projection_kernel, out_shape=[jax.ShapeDtypeStruct((rows,...  16.6 us
    ppermute x7, starting transfers between devices, moved_across(): return lax.ppermute(value, ('tower', 'seq'), both)  14.8 us
    pallas_call x1, Pallas kernels, attention(): pl.pallas_call(attention_kernel, out_shape=[shape] * 2 + [pair_shape] * 3...  13.5 us
    all_to_all x1, waiting for transfers between devices, local(): lax.all_to_all(partial_w.reshape(plane, -1, columns), 'seq', 0, 0, axis_i...  8.06 us
    pallas_call x1, Pallas kernels, context_partial(): pl.pallas_call(context_kernel, out_shape=jax.ShapeDtypeStruct((rows, widt...  7 us
  transfers between devices with their start and end apart: 21, of which 10 were waited for; matrix products, arithmetic and copies ran while one was open for 5% of the time, Pallas kernels for 25%

profile of v3, /device:TPU:0, one launch (start us, length us, event | category | flops | bytes accessed | tf_op | source)
XLA Modules:
  0.0 171.6 jit_solution(8935770549566429649)
XLA Ops:
  2.7 2.9 %collective-permute-start.1 = (bf16[272,768]{1,0:T(8,128)(2,1)S(1)}, bf16[272,768]{1,0:T(8,128)(2,1)S(1)}, u32[]{:S(2)}, u32[]{:S(2)}) collective-permute-start(bf16[272,768]{1,0:T(8,128)(2,1)S(1)} %get-tuple-element.86), channel_id=1, source_target_pairs={{0,6},{2,4},{4,2},{6,0},{8,14},{10,12},{12,10},{14,8},{16,22},{18,... | collective-permute-start | bytes 1253384 | tf_op jit(solution)/shard_map/ppermute | solution.py:21
  6.5 8.3 %projection.2 = (bf16[256,768]{1,0:T(8,128)(2,1)}, bf16[3072,768]{1,0:T(8,128)(2,1)}) custom-call(s32[1]{0:T(128)} %bitcast.4.which, bf16[256,3072]{1,0:T(8,128)(2,1)} %bitcast.35, bf16[3072,2,768]{2,1,0:T(2,128)(2,1)} %bitcast.33), custom_call_target="tpu_custom_call" | custom-call | flops 1207959552 | bytes 20971520 | tf_op jit(solution)/shard_map/projection/pallas_call | solution.py:89
  16.1 4.7 %collective-permute-start.5 = (bf16[256,768]{1,0:T(8,128)(2,1)}, bf16[256,768]{1,0:T(8,128)(2,1)S(1)}, u32[]{:S(2)}, u32[]{:S(2)}) collective-permute-start(bf16[256,768]{1,0:T(8,128)(2,1)} %get-tuple-element.37), channel_id=1, source_target_pairs={{0,70},{2,68},{4,66},{6,64},{8,78},{10,76},{12,74},{14,72},{16,86}... | collective-permute-start | bytes 1179656 | tf_op jit(solution)/shard_map/ppermute | solution.py:34
  20.8 8.3 %projection.3 = (bf16[256,768]{1,0:T(8,128)(2,1)}, bf16[3072,768]{1,0:T(8,128)(2,1)}) custom-call(s32[1]{0:T(128)} %bitcast.1.which, bf16[256,3072]{1,0:T(8,128)(2,1)} %bitcast.36, bf16[3072,2,768]{2,1,0:T(2,128)(2,1)} %bitcast.34), custom_call_target="tpu_custom_call" | custom-call | flops 1207959552 | bytes 20971520 | tf_op jit(solution)/shard_map/projection/pallas_call | solution.py:89
  30.4 3.5 %collective-permute-start.4 = (bf16[256,768]{1,0:T(8,128)(2,1)}, bf16[256,768]{1,0:T(8,128)(2,1)}, u32[]{:S(2)}, u32[]{:S(2)}) collective-permute-start(bf16[256,768]{1,0:T(8,128)(2,1)} %get-tuple-element.42), channel_id=1, source_target_pairs={{0,68},{2,70},{4,64},{6,66},{8,76},{10,78},{12,72},{14,74},{16,84}... | collective-permute-start | bytes 1179656 | tf_op jit(solution)/shard_map/ppermute | solution.py:34
  34.0 2.5 %dynamic-slice_bitcast_fusion = (bf16[256,1536]{1,0:T(8,128)(2,1)}, bf16[256,1536]{1,0:T(8,128)(2,1)S(1)}) fusion(bf16[1,256,3072]{2,1,0:T(8,128)(2,1)} %param.6, s32[]{:T(128)S(6)} %select_n.83, s32[]{:T(128)S(6)} %select_n.73), kind=kLoop, calls=%fused_computation.4 | loop fusion | bytes 3145736 | tf_op jit(solution)/shard_map/dynamic_slice | solution.py:278
  36.6 5.7 %collective-permute-done.6.refs_4_ = bf16[256,768]{1,0:T(8,128)(2,1)S(1)} collective-permute-done((bf16[256,768]{1,0:T(8,128)(2,1)}, bf16[256,768]{1,0:T(8,128)(2,1)S(1)}, u32[]{:S(2)}, u32[]{:S(2)}) %collective-permute-start.6) | collective-permute-done | bytes 393248 | tf_op jit(solution)/shard_map/ppermute | solution.py:34
  42.2 5.0 %collective-permute-done.4.refs_2_ = bf16[256,768]{1,0:T(8,128)(2,1)} collective-permute-done((bf16[256,768]{1,0:T(8,128)(2,1)}, bf16[256,768]{1,0:T(8,128)(2,1)}, u32[]{:S(2)}, u32[]{:S(2)}) %collective-permute-start.4) | collective-permute-done | bytes 393248 | tf_op jit(solution)/shard_map/ppermute | solution.py:34
  48.0 2.2 %collective-permute-start.9 = (bf16[256,1536]{1,0:T(8,128)(2,1)}, bf16[256,1536]{1,0:T(8,128)(2,1)}, u32[]{:S(2)}, u32[]{:S(2)}) collective-permute-start(bf16[256,1536]{1,0:T(8,128)(2,1)} %get-tuple-element.51), channel_id=1, source_target_pairs={{0,32},{2,34},{4,36},{6,38},{8,40},{10,42},{12,44},{14,46},{16,48}... | collective-permute-start | bytes 2359304 | tf_op jit(solution)/shard_map/ppermute | solution.py:21
  50.8 13.5 %attention.1 = (bf16[256,768]{1,0:T(8,128)(2,1)}, bf16[256,768]{1,0:T(8,128)(2,1)}, bf16[512,768]{1,0:T(8,128)(2,1)}, bf16[512,768]{1,0:T(8,128)(2,1)}, bf16[512,768]{1,0:T(8,128)(2,1)}) custom-call(s32[7]{0:T(128)} %concatenate.28.meta, bf16[272,768]{1,0:T(8,128)(2,1)} %copy-done.9, bf16[272,768]{1,0:T(8,128)(2,1)} %copy-done.9, ...), custom_call_target="tpu_custom_call" | custom-call | flops 2516582400 | bytes 8388608 | tf_op jit(solution)/shard_map/attention/pallas_call | solution.py:190
  65.8 2.4 %collective-permute-start.12 = (bf16[512,768]{1,0:T(8,128)(2,1)}, bf16[512,768]{1,0:T(8,128)(2,1)S(1)}, u32[]{:S(2)}, u32[]{:S(2)}) collective-permute-start(bf16[512,768]{1,0:T(8,128)(2,1)} %get-tuple-element.56), channel_id=1, source_target_pairs={{0,72},{2,74},{8,80},{10,82},{12,68},{14,70},{16,88},{18,90},{20,7... | collective-permute-start | bytes 2359304 | tf_op jit(solution)/shard_map/ppermute | solution.py:34
  68.6 17.0 %collective-permute-done.11 = bf16[512,768]{1,0:T(8,128)(2,1)S(1)} collective-permute-done((bf16[512,768]{1,0:T(8,128)(2,1)}, bf16[512,768]{1,0:T(8,128)(2,1)S(1)}, u32[]{:S(2)}, u32[]{:S(2)}) %collective-permute-start.11) | collective-permute-done | bytes 786464 | tf_op jit(solution)/shard_map/ppermute | solution.py:34
  87.2 2.3 %collective-permute-start.16 = (bf16[256,768]{1,0:T(8,128)(2,1)S(1)}, bf16[256,768]{1,0:T(8,128)(2,1)S(1)}, u32[]{:S(2)}, u32[]{:S(2)}) collective-permute-start(bf16[256,768]{1,0:T(8,128)(2,1)S(1)} %copy-done.14), channel_id=1, source_target_pairs={{0,6},{2,4},{4,2},{6,0},{8,14},{10,12},{12,10},{14,8},{16,22},{18,... | collective-permute-start | bytes 1179656 | tf_op jit(solution)/shard_map/ppermute | solution.py:21
  91.2 7.3 %collective-permute-done.15.grad_next = bf16[256,768]{1,0:T(8,128)(2,1)S(1)} collective-permute-done((bf16[256,768]{1,0:T(8,128)(2,1)S(1)}, bf16[256,768]{1,0:T(8,128)(2,1)S(1)}, u32[]{:S(2)}, u32[]{:S(2)}) %collective-permute-start.15) | collective-permute-done | bytes 393248 | tf_op jit(solution)/shard_map/ppermute | solution.py:21
  99.3 7.0 %context_partial.1 = bf16[256,3072]{1,0:T(8,128)(2,1)} custom-call(bf16[512,768]{1,0:T(8,128)(2,1)} %copy-done, bf16[256,768]{1,0:T(8,128)(2,1)} %copy-done.5, bf16[3072,768]{1,0:T(8,128)(2,1)} %get-tuple-element.61.weight, bf16[3072,768]{1,0:T(8,128)(2,1)} %get-tuple-element.62.weight_next), custom_call_target="tpu_custom_call" | custom-call | flops 2415919104 | bytes 12582912 | tf_op jit(solution)/shard_map/context_partial/pallas_call | solution.py:254
  107.4 3.8 %collective-permute-start.17 = (bf16[256,1024]{1,0:T(8,128)(2,1)S(1)}, bf16[256,1024]{1,0:T(8,128)(2,1)S(1)}, u32[]{:S(2)}, u32[]{:S(2)}) collective-permute-start(bf16[256,1024]{1,0:T(8,128)(2,1)S(1)} %slice.37), channel_id=1, source_target_pairs={{0,1},{1,0},{2,3},{3,2},{4,5},{5,4},{6,7},{7,6},{8,9},{9,8},{10,11... | collective-permute-start | bytes 1572872 | tf_op jit(solution)/shard_map/ppermute | solution.py:21
  111.2 2.7 %collective-permute-start.18 = (bf16[256,768]{1,0:T(8,128)(2,1)}, bf16[256,768]{1,0:T(8,128)(2,1)S(1)}, u32[]{:S(2)}, u32[]{:S(2)}) collective-permute-start(bf16[256,768]{1,0:T(8,128)(2,1)} %get-tuple-element.64), channel_id=1, source_target_pairs={{0,4},{2,6},{4,0},{6,2},{8,12},{10,14},{12,8},{14,10},{16,20},{18,... | collective-permute-start | bytes 1179656 | tf_op jit(solution)/shard_map/ppermute | solution.py:21
  115.3 5.8 %weight_partial.1 = bf16[1536,768]{1,0:T(8,128)(2,1)} custom-call(bf16[256,1536]{1,0:T(8,128)(2,1)S(1)} %get-tuple-element.50.own, bf16[256,1536]{1,0:T(8,128)(2,1)} %collective-permute-done.9.own_z, bf16[256,1536]{1,0:T(8,128)(2,1)S(1)} %collective-permute-done.8.pair, bf16[256,1536]{1,0:T(8,128)(2,1)S(1)} %collective-permute-done.13.pair_z, ...), custom_call_target="tpu_custom_call" | custom-call | flops 2415919104 | bytes 8388608 | tf_op jit(solution)/shard_map/weight_partial/pallas_call | solution.py:227
  121.1 4.6 %collective-permute-done.18 = bf16[256,768]{1,0:T(8,128)(2,1)S(1)} collective-permute-done((bf16[256,768]{1,0:T(8,128)(2,1)}, bf16[256,768]{1,0:T(8,128)(2,1)S(1)}, u32[]{:S(2)}, u32[]{:S(2)}) %collective-permute-start.18) | collective-permute-done | bytes 393248 | tf_op jit(solution)/shard_map/ppermute | solution.py:21
  127.2 4.6 %all-to-all-start = ((bf16[16,96,768]{2,1,0:T(8,128)(2,1)}), bf16[16,96,768]{2,1,0:T(8,128)(2,1)}, u32[]{:S(2)}, u32[]{:S(2)}) async-start(bf16[16,96,768]{2,1,0:T(8,128)(2,1)} %bitcast.18), calls=%async_computation | async-start | bytes 4718592 | tf_op jit(solution)/shard_map/all_to_all | solution.py:347
  132.0 3.7 %collective-permute-start.19 = (bf16[256,2048]{1,0:T(8,128)(2,1)S(1)}, bf16[256,2048]{1,0:T(8,128)(2,1)S(1)}, u32[]{:S(2)}, u32[]{:S(2)}) collective-permute-start(bf16[256,2048]{1,0:T(8,128)(2,1)S(1)} %slice.38), channel_id=1, source_target_pairs={{0,1},{1,0},{2,3},{3,2},{4,5},{5,4},{6,7},{7,6},{8,9},{9,8},{10,11... | collective-permute-start | bytes 3145736 | tf_op jit(solution)/shard_map/ppermute | solution.py:21
  137.5 21.2 %collective-permute-done.19 = bf16[256,2048]{1,0:T(8,128)(2,1)S(1)} collective-permute-done((bf16[256,2048]{1,0:T(8,128)(2,1)S(1)}, bf16[256,2048]{1,0:T(8,128)(2,1)S(1)}, u32[]{:S(2)}, u32[]{:S(2)}) %collective-permute-start.19) | collective-permute-done | bytes 1048608 | tf_op jit(solution)/shard_map/ppermute | solution.py:21
  160.3 8.1 %all-to-all-done = bf16[16,96,768]{2,1,0:T(8,128)(2,1)} async-done(((bf16[16,96,768]{2,1,0:T(8,128)(2,1)}), bf16[16,96,768]{2,1,0:T(8,128)(2,1)}, u32[]{:S(2)}, u32[]{:S(2)}) %all-to-all-start) | async-done | bytes 2359328 | tf_op jit(solution)/shard_map/all_to_all | solution.py:347
  168.4 2.1 %reduce_sum.12 = bf16[2,96,768]{2,1,0:T(8,128)(2,1)S(1)} reduce(bf16[8,2,96,768]{3,2,1,0:T(8,128)(2,1)} %bitcast.19, bf16[]{:T(256)} %constant.69.clone.1), dimensions={0}, to_apply=%region_0.1 | reduce | flops 1032192 | bytes 2654210 | tf_op jit(solution)/shard_map/reduce_sum | solution.py:351
  (75 shorter events, 21.5 us)
Async XLA Ops:
  2.7 26.4 %collective-permute-start.1 = (bf16[272,768]{1,0:T(8,128)(2,1)S(1)}, bf16[272,768]{1,0:T(8,128)(2,1)S(1)}, u32[]{:S(2)}, u32[]{:S(2)}) collective-permute-start(bf16[272,768]{1,0:T(8,128)(2,1)S(1)} %get-tuple-element.86), channel_id=1, source_target_pairs={{0,6},{2,4},{4,2},{6,0},{8,14},{10,12},{12,10},{14,8},{16,22},{18,... | collective-permute-start | bytes 1253384 | tf_op jit(solution)/shard_map/ppermute | solution.py:21
  5.7 23.5 %collective-permute-start = (bf16[272,768]{1,0:T(8,128)(2,1)S(1)}, bf16[272,768]{1,0:T(8,128)(2,1)S(1)}, u32[]{:S(2)}, u32[]{:S(2)}) collective-permute-start(bf16[272,768]{1,0:T(8,128)(2,1)S(1)} %get-tuple-element.87), channel_id=1, source_target_pairs={{0,4},{2,6},{4,0},{6,2},{8,12},{10,14},{12,8},{14,10},{16,20},{18,... | collective-permute-start | bytes 1253384 | tf_op jit(solution)/shard_map/ppermute | solution.py:21
  14.8 19.2 %collective-permute-start.7 = (bf16[256,768]{1,0:T(8,128)(2,1)}, bf16[256,768]{1,0:T(8,128)(2,1)S(1)}, u32[]{:S(2)}, u32[]{:S(2)}) collective-permute-start(bf16[256,768]{1,0:T(8,128)(2,1)} %get-tuple-element.37), channel_id=1, source_target_pairs={{4,78},{6,76},{8,66},{10,64},{12,86},{14,84},{16,74},{18,72},{20,9... | collective-permute-start | bytes 1179656 | tf_op jit(solution)/shard_map/ppermute | solution.py:34
  16.1 20.4 %collective-permute-start.5 = (bf16[256,768]{1,0:T(8,128)(2,1)}, bf16[256,768]{1,0:T(8,128)(2,1)S(1)}, u32[]{:S(2)}, u32[]{:S(2)}) collective-permute-start(bf16[256,768]{1,0:T(8,128)(2,1)} %get-tuple-element.37), channel_id=1, source_target_pairs={{0,70},{2,68},{4,66},{6,64},{8,78},{10,76},{12,74},{14,72},{16,86}... | collective-permute-start | bytes 1179656 | tf_op jit(solution)/shard_map/ppermute | solution.py:34
  20.8 15.7 %collective-permute-start.3 = (bf16[256,768]{1,0:T(8,128)(2,1)}, bf16[256,768]{1,0:T(8,128)(2,1)S(1)}, u32[]{:S(2)}, u32[]{:S(2)}) collective-permute-start(bf16[256,768]{1,0:T(8,128)(2,1)} %get-tuple-element.37), channel_id=1, source_target_pairs={{0,66},{2,64},{4,70},{6,68},{8,74},{10,72},{12,78},{14,76},{16,82}... | collective-permute-start | bytes 1179656 | tf_op jit(solution)/shard_map/ppermute | solution.py:34
  29.1 21.0 %copy-start.8 = (bf16[272,768]{1,0:T(8,128)(2,1)}, bf16[272,768]{1,0:T(8,128)(2,1)S(1)}, u32[]{:S(2)}) copy-start(bf16[272,768]{1,0:T(8,128)(2,1)S(1)} %collective-permute-done.1.q_b.c_b) | copy-start | bytes 1253380
  29.1 21.0 %copy-start.9 = (bf16[272,768]{1,0:T(8,128)(2,1)}, bf16[272,768]{1,0:T(8,128)(2,1)S(1)}, u32[]{:S(2)}) copy-start(bf16[272,768]{1,0:T(8,128)(2,1)S(1)} %collective-permute-done.q_a.c_a) | copy-start | bytes 1253380
  29.1 13.1 %collective-permute-start.6 = (bf16[256,768]{1,0:T(8,128)(2,1)}, bf16[256,768]{1,0:T(8,128)(2,1)S(1)}, u32[]{:S(2)}, u32[]{:S(2)}) collective-permute-start(bf16[256,768]{1,0:T(8,128)(2,1)} %get-tuple-element.42), channel_id=1, source_target_pairs={{4,76},{6,78},{8,64},{10,66},{12,84},{14,86},{16,72},{18,74},{20,9... | collective-permute-start | bytes 1179656 | tf_op jit(solution)/shard_map/ppermute | solution.py:34
  30.4 16.8 %collective-permute-start.4 = (bf16[256,768]{1,0:T(8,128)(2,1)}, bf16[256,768]{1,0:T(8,128)(2,1)}, u32[]{:S(2)}, u32[]{:S(2)}) collective-permute-start(bf16[256,768]{1,0:T(8,128)(2,1)} %get-tuple-element.42), channel_id=1, source_target_pairs={{0,68},{2,70},{4,64},{6,66},{8,76},{10,78},{12,72},{14,74},{16,84}... | collective-permute-start | bytes 1179656 | tf_op jit(solution)/shard_map/ppermute | solution.py:34
  34.0 13.3 %collective-permute-start.2 = (bf16[256,768]{1,0:T(8,128)(2,1)}, bf16[256,768]{1,0:T(8,128)(2,1)}, u32[]{:S(2)}, u32[]{:S(2)}) collective-permute-start(bf16[256,768]{1,0:T(8,128)(2,1)} %get-tuple-element.42), channel_id=1, source_target_pairs={{0,64},{64,0},{1,65},{65,1},{2,66},{66,2},{3,67},{67,3},{4,68},{68... | collective-permute-start | bytes 1179656 | tf_op jit(solution)/shard_map/ppermute | solution.py:21
  47.3 20.9 %collective-permute-start.8 = (bf16[256,1536]{1,0:T(8,128)(2,1)S(1)}, bf16[256,1536]{1,0:T(8,128)(2,1)S(1)}, u32[]{:S(2)}, u32[]{:S(2)}) collective-permute-start(bf16[256,1536]{1,0:T(8,128)(2,1)S(1)} %get-tuple-element.50.own), channel_id=1, source_target_pairs={{0,2},{2,0},{4,6},{6,4},{8,10},{10,8},{12,14},{14,12},{16,18},{18,... | collective-permute-start | bytes 2359304 | tf_op jit(solution)/shard_map/ppermute | solution.py:21
  48.0 20.3 %collective-permute-start.9 = (bf16[256,1536]{1,0:T(8,128)(2,1)}, bf16[256,1536]{1,0:T(8,128)(2,1)}, u32[]{:S(2)}, u32[]{:S(2)}) collective-permute-start(bf16[256,1536]{1,0:T(8,128)(2,1)} %get-tuple-element.51), channel_id=1, source_target_pairs={{0,32},{2,34},{4,36},{6,38},{8,40},{10,42},{12,44},{14,46},{16,48}... | collective-permute-start | bytes 2359304 | tf_op jit(solution)/shard_map/ppermute | solution.py:21
  64.2 21.4 %collective-permute-start.11 = (bf16[512,768]{1,0:T(8,128)(2,1)}, bf16[512,768]{1,0:T(8,128)(2,1)S(1)}, u32[]{:S(2)}, u32[]{:S(2)}) collective-permute-start(bf16[512,768]{1,0:T(8,128)(2,1)} %get-tuple-element.55), channel_id=1, source_target_pairs={{0,68},{2,70},{4,64},{6,66},{8,76},{10,78},{12,72},{14,74},{16,84}... | collective-permute-start | bytes 2359304 | tf_op jit(solution)/shard_map/ppermute | solution.py:34
  65.8 20.3 %collective-permute-start.12 = (bf16[512,768]{1,0:T(8,128)(2,1)}, bf16[512,768]{1,0:T(8,128)(2,1)S(1)}, u32[]{:S(2)}, u32[]{:S(2)}) collective-permute-start(bf16[512,768]{1,0:T(8,128)(2,1)} %get-tuple-element.56), channel_id=1, source_target_pairs={{0,72},{2,74},{8,80},{10,82},{12,68},{14,70},{16,88},{18,90},{20,7... | collective-permute-start | bytes 2359304 | tf_op jit(solution)/shard_map/ppermute | solution.py:34
  68.2 19.0 %copy-start.14 = (bf16[256,768]{1,0:T(8,128)(2,1)S(1)}, bf16[256,768]{1,0:T(8,128)(2,1)}, u32[]{:S(2)}) copy-start(bf16[256,768]{1,0:T(8,128)(2,1)} %get-tuple-element.59) | copy-start | bytes 1179652
  68.2 17.8 %collective-permute-start.10 = (bf16[512,768]{1,0:T(8,128)(2,1)}, bf16[512,768]{1,0:T(8,128)(2,1)S(1)}, u32[]{:S(2)}, u32[]{:S(2)}) collective-permute-start(bf16[512,768]{1,0:T(8,128)(2,1)} %get-tuple-element.54), channel_id=1, source_target_pairs={{0,64},{64,0},{1,65},{65,1},{2,66},{66,2},{3,67},{67,3},{4,68},{68... | collective-permute-start | bytes 2359304 | tf_op jit(solution)/shard_map/ppermute | solution.py:21
  86.4 12.1 %collective-permute-start.15 = (bf16[256,768]{1,0:T(8,128)(2,1)S(1)}, bf16[256,768]{1,0:T(8,128)(2,1)S(1)}, u32[]{:S(2)}, u32[]{:S(2)}) collective-permute-start(bf16[256,768]{1,0:T(8,128)(2,1)S(1)} %slice.36), channel_id=1, source_target_pairs={{0,2},{2,0},{4,6},{6,4},{8,10},{10,8},{12,14},{14,12},{16,18},{18,... | collective-permute-start | bytes 1179656 | tf_op jit(solution)/shard_map/ppermute | solution.py:21
  87.2 12.1 %collective-permute-start.16 = (bf16[256,768]{1,0:T(8,128)(2,1)S(1)}, bf16[256,768]{1,0:T(8,128)(2,1)S(1)}, u32[]{:S(2)}, u32[]{:S(2)}) collective-permute-start(bf16[256,768]{1,0:T(8,128)(2,1)S(1)} %copy-done.14), channel_id=1, source_target_pairs={{0,6},{2,4},{4,2},{6,0},{8,14},{10,12},{12,10},{14,8},{16,22},{18,... | collective-permute-start | bytes 1179656 | tf_op jit(solution)/shard_map/ppermute | solution.py:21
  89.5 24.6 %collective-permute-start.13 = (bf16[256,1536]{1,0:T(8,128)(2,1)}, bf16[256,1536]{1,0:T(8,128)(2,1)S(1)}, u32[]{:S(2)}, u32[]{:S(2)}) collective-permute-start(bf16[256,1536]{1,0:T(8,128)(2,1)} %collective-permute-done.9.own_z), channel_id=1, source_target_pairs={{0,2},{2,0},{4,6},{6,4},{8,10},{10,8},{12,14},{14,12},{16,18},{18,... | collective-permute-start | bytes 2359304 | tf_op jit(solution)/shard_map/ppermute | solution.py:21
  90.9 23.3 %collective-permute-start.14 = (bf16[512,768]{1,0:T(8,128)(2,1)S(1)}, bf16[512,768]{1,0:T(8,128)(2,1)}, u32[]{:S(2)}, u32[]{:S(2)}) collective-permute-start(bf16[512,768]{1,0:T(8,128)(2,1)S(1)} %add_convert_fusion.1.grad), channel_id=1, source_target_pairs={{0,32},{2,34},{4,36},{6,38},{8,40},{10,42},{12,44},{14,46},{16,48}... | collective-permute-start | bytes 2359304 | tf_op jit(solution)/shard_map/ppermute | solution.py:21
  107.4 18.3 %collective-permute-start.17 = (bf16[256,1024]{1,0:T(8,128)(2,1)S(1)}, bf16[256,1024]{1,0:T(8,128)(2,1)S(1)}, u32[]{:S(2)}, u32[]{:S(2)}) collective-permute-start(bf16[256,1024]{1,0:T(8,128)(2,1)S(1)} %slice.37), channel_id=1, source_target_pairs={{0,1},{1,0},{2,3},{3,2},{4,5},{5,4},{6,7},{7,6},{8,9},{9,8},{10,11... | collective-permute-start | bytes 1572872 | tf_op jit(solution)/shard_map/ppermute | solution.py:21
  111.2 14.5 %collective-permute-start.18 = (bf16[256,768]{1,0:T(8,128)(2,1)}, bf16[256,768]{1,0:T(8,128)(2,1)S(1)}, u32[]{:S(2)}, u32[]{:S(2)}) collective-permute-start(bf16[256,768]{1,0:T(8,128)(2,1)} %get-tuple-element.64), channel_id=1, source_target_pairs={{0,4},{2,6},{4,0},{6,2},{8,12},{10,14},{12,8},{14,10},{16,20},{18,... | collective-permute-start | bytes 1179656 | tf_op jit(solution)/shard_map/ppermute | solution.py:21
  127.2 41.1 %all-to-all-start = ((bf16[16,96,768]{2,1,0:T(8,128)(2,1)}), bf16[16,96,768]{2,1,0:T(8,128)(2,1)}, u32[]{:S(2)}, u32[]{:S(2)}) async-start(bf16[16,96,768]{2,1,0:T(8,128)(2,1)} %bitcast.18), calls=%async_computation | async-start | bytes 4718592 | tf_op jit(solution)/shard_map/all_to_all | solution.py:347
  132.0 26.7 %collective-permute-start.19 = (bf16[256,2048]{1,0:T(8,128)(2,1)S(1)}, bf16[256,2048]{1,0:T(8,128)(2,1)S(1)}, u32[]{:S(2)}, u32[]{:S(2)}) collective-permute-start(bf16[256,2048]{1,0:T(8,128)(2,1)S(1)} %slice.38), channel_id=1, source_target_pairs={{0,1},{1,0},{2,3},{3,2},{4,5},{5,4},{6,7},{7,6},{8,9},{9,8},{10,11... | collective-permute-start | bytes 3145736 | tf_op jit(solution)/shard_map/ppermute | solution.py:21
  (12 other events, 62.2 us)

commit v4 on v3

--- a/solution.py
+++ b/solution.py
@@ -59,15 +59,45 @@
     return lax.dot_general(a, b, ((dims[0], dims[1]), ((), ())), preferred_element_type=F32)
 
 
-def projection_kernel(which, context, weight, kv, weight_out, total):
+def total_kernel(parts, out):
+    columns = parts.shape[2]
+    heads = columns // (2 * HD)
+    for half in range(PAIR):
+        total = parts[half].astype(F32)
+        for source in range(half + PAIR, parts.shape[0], PAIR):
+            total += parts[source].astype(F32)
+        for h in range(heads):
+            for side in range(2):
+                begin = (2 * h + side) * HD
+                place = side * columns + (half * heads + h) * HD
+                out[:, place : place + HD] = total[:, begin : begin + HD].astype(BF16)
+
+
+def weight_total(parts):
+    rows, columns = parts.shape[1:]
+    block = rows // 2
+    return pl.pallas_call(
+        total_kernel,
+        out_shape=jax.ShapeDtypeStruct((rows, 2 * columns), BF16),
+        grid=(rows // block,),
+        in_specs=[pl.BlockSpec((parts.shape[0], block, columns), lambda i: (0, i, 0))],
+        out_specs=pl.BlockSpec((block, 2 * columns), lambda i: (i, 0)),
+        compiler_params=pltpu.CompilerParams(vmem_limit_bytes=24 * 2**20),
+        name="weight_total",
+    )(parts)
+
+
+def head_columns(weight):
+    sides = jnp.swapaxes(weight, 0, 1)
+    heads = sides.shape[2] // HD
+    return jnp.concatenate(
+        [sides[side, :, h * HD : (h + 1) * HD] for h in range(heads) for side in range(2)], axis=1
+    )
+
+
+def projection_kernel(which, context, weight, kv, total):
     step = pl.program_id(0)
-    sides = jnp.swapaxes(weight[...], 0, 1)
-    heads = sides.shape[2] // HD
-    block = jnp.concatenate(
-        [sides[side, :, h * HD : (h + 1) * HD] for h in range(heads) for side in range(2)], axis=1
-    )
-    weight_out[...] = block
-    part = dot(context[...], block, ((1,), (0,)))
+    part = dot(context[...], head_columns(weight[...]), ((1,), (0,)))
 
     @pl.when(step == 0)
     def _():
@@ -88,10 +118,7 @@
     depth = width // 3
     return pl.pallas_call(
         projection_kernel,
-        out_shape=[
-            jax.ShapeDtypeStruct((rows, 2 * columns), BF16),
-            jax.ShapeDtypeStruct((width, 2 * columns), BF16),
-        ],
+        out_shape=jax.ShapeDtypeStruct((rows, 2 * columns), BF16),
         grid_spec=pltpu.PrefetchScalarGridSpec(
             num_scalar_prefetch=1,
             grid=(width // depth,),
@@ -99,13 +126,10 @@
                 pl.BlockSpec((rows, depth), lambda i, w: (0, i)),
                 pl.BlockSpec((depth, 2, columns), lambda i, w: (i, 0, w[0])),
             ],
-            out_specs=[
-                pl.BlockSpec((rows, 2 * columns), lambda i, w: (0, 0)),
-                pl.BlockSpec((depth, 2 * columns), lambda i, w: (i, 0)),
-            ],
+            out_specs=pl.BlockSpec((rows, 2 * columns), lambda i, w: (0, 0)),
             scratch_shapes=[pltpu.VMEM((rows, 2 * columns), F32)],
         ),
-        compiler_params=pltpu.CompilerParams(vmem_limit_bytes=60 * 2**20),
+        compiler_params=pltpu.CompilerParams(vmem_limit_bytes=56 * 2**20),
         cost_estimate=pl.CostEstimate(
             flops=4 * rows * width * columns, bytes_accessed=20 * 2**20, transcendentals=0
         ),
@@ -202,7 +226,7 @@
                 pltpu.VMEM((WINDOW * rows, 2 * HD), F32),
             ],
         ),
-        compiler_params=pltpu.CompilerParams(vmem_limit_bytes=62 * 2**20),
+        compiler_params=pltpu.CompilerParams(vmem_limit_bytes=56 * 2**20),
         cost_estimate=pl.CostEstimate(
             flops=work * 10 * HD, bytes_accessed=8 * 2**20, transcendentals=work
         ),
@@ -239,30 +263,38 @@
     )(*contexts, *grads)
 
 
-def context_kernel(grad, grad_next, weight, weight_next, out):
-    total = dot(grad[...], weight[...], ((1,), (1,)))
-    total += dot(grad_next[...], weight_next[...], ((1,), (1,)))
-    out[...] = total.astype(BF16)
-
-
-def context_partial(returned, other_rows, weight_same, weight_next):
+def context_kernel(member, grad, grad_next, weight, out, both):
+    half = grad.shape[1]
+
+    @pl.when(pl.program_id(0) == 0)
+    def _():
+        both[:, pl.ds(pl.multiple_of(member[0] * half, half), half)] = grad[...]
+        both[:, pl.ds(pl.multiple_of((1 - member[0]) * half, half), half)] = grad_next[...]
+
+    out[...] = dot(both[...], head_columns(weight[...]), ((1,), (1,))).astype(BF16)
+
+
+def context_partial(member, returned, other_rows, weight):
     rows, columns = other_rows.shape
-    width = weight_same.shape[0]
+    width = weight.shape[0]
     block = width // 4
-    grad = pl.BlockSpec((rows, columns), lambda i: (0, 0))
-    weight = pl.BlockSpec((block, columns), lambda i: (i, 0))
+    grad = pl.BlockSpec((rows, columns), lambda i, m: (0, 0))
     return pl.pallas_call(
         context_kernel,
         out_shape=jax.ShapeDtypeStruct((rows, width), BF16),
-        grid=(width // block,),
-        in_specs=[grad, grad, weight, weight],
-        out_specs=pl.BlockSpec((rows, block), lambda i: (0, i)),
-        compiler_params=pltpu.CompilerParams(vmem_limit_bytes=60 * 2**20),
+        grid_spec=pltpu.PrefetchScalarGridSpec(
+            num_scalar_prefetch=1,
+            grid=(width // block,),
+            in_specs=[grad, grad, pl.BlockSpec((block, 2, columns), lambda i, m: (i, 0, 0))],
+            out_specs=pl.BlockSpec((rows, block), lambda i, m: (0, i)),
+            scratch_shapes=[pltpu.VMEM((rows, 2 * columns), BF16)],
+        ),
+        compiler_params=pltpu.CompilerParams(vmem_limit_bytes=50 * 2**20),
         cost_estimate=pl.CostEstimate(
             flops=4 * rows * width * columns, bytes_accessed=12 * 2**20, transcendentals=0
         ),
         name="context_partial",
-    )(returned, other_rows, weight_same, weight_next)
+    )(member.reshape(1), returned, other_rows, weight)
 
 
 def local(queries, context, kv_weight, spans, cotangent):
@@ -294,9 +326,9 @@
     qc_a = moved(qc_of(member), "seq", same_x)
     qc_b = moved(qc_of(1 - member), "seq", cross_x)
 
-    next_half, weight_next = projection(1 - member, context, kv_weight[0])
+    next_half = projection(1 - member, context, kv_weight[0])
     late_context, _ = lax.optimization_barrier((context, next_half))
-    same_half, weight_same = projection(member, late_context, kv_weight[0])
+    same_half = projection(member, late_context, kv_weight[0])
     same_half, qc_a, qc_b = lax.optimization_barrier((same_half, qc_a, qc_b))
     kv_blocks = [
         swapped(same_half, "tower"),
@@ -331,7 +363,7 @@
     od_b, _ = lax.optimization_barrier((od_b, returned))
     od_b = moved(od_b, "seq", cross_x)
     other_rows, od_b = lax.optimization_barrier((other_rows, od_b))
-    partial_ctx = context_partial(returned, other_rows, weight_same, weight_next)
+    partial_ctx = context_partial(member, returned, other_rows, kv_weight[0])
     od_a, _ = lax.optimization_barrier((od_a, partial_ctx))
     od_a = moved(od_a, "seq", same_x)
     sum_parts = [partial_ctx[:, : width // 3], partial_ctx[:, width // 3 :]]
@@ -347,13 +379,7 @@
     parts = lax.all_to_all(
         partial_w.reshape(plane, -1, columns), "seq", 0, 0, axis_index_groups=groups
     )
-    weight_grad = (
-        jnp.sum(parts.reshape(plane // PAIR, PAIR, -1, columns).astype(F32), axis=0)
-        .astype(BF16)
-        .reshape(PAIR, -1, heads // PAIR, 2, HD)
-        .transpose(1, 3, 0, 2, 4)
-        .reshape(1, -1, 2, columns)
-    )
+    weight_grad = weight_total(parts).reshape(-1, 2, columns)[None]
 
     context_grad = jnp.concatenate(
         [

time: 172 us -> 168 us (0.977)
  local copies, waits for them, and re-layouts: 9.55 us -> 6.17 us
  waiting for transfers between devices: 70.4 us -> 67.9 us
    pallas_call x1, Pallas kernels: 7 us -> 10.3 us  [context_partial(): pl.pallas_call(context_kernel, out_shape=jax.ShapeDtypeStruct((rows, widt...]
    ppermute x13, waiting for transfers between devices: 34.2 us -> 31.7 us  [moved(): return lax.ppermute(value, axis, pairs)]
    reduce_sum x1 -> x0, other arithmetic: 2.07 us -> none  [local(): jnp.sum(parts.reshape(plane // PAIR, PAIR, -1, columns).astype(F32), axis=0)]
    all_to_all x1, waiting for transfers between devices: 8.06 us -> 6.18 us  [local(): lax.all_to_all(partial_w.reshape(plane, -1, columns), 'seq', 0, 0, axis_i...]
    ppermute x7, waiting for transfers between devices: 28.1 us -> 30 us  [moved_across(): return lax.ppermute(value, ('tower', 'seq'), both)]
    unnamed x32 -> x16, local copies, waits for them, and re-layouts: 3.84 us -> 2.21 us
    pallas_call x2 -> x3, Pallas kernels: 16.6 us -> 16.3 us  [the longest x2 14.5 us: projection(): pl.pallas_call(projection_kernel, out_shape=jax.ShapeDtypeStruct((rows, 2...]
  transfers between devices with their start and end apart: 21 -> 21, of which waited for: 10 -> 9; matrix products, arithmetic and copies ran while one was open for 5% -> 4% of each run, Pallas kernels for 25% -> 26%
where the time goes in v4:
time: 168 us; the launch traced here: 167 us
  waiting for transfers between devices  67.9 us (40%)
  Pallas kernels  44.5 us (26%)
  starting transfers between devices  42.4 us (25%)
  local copies, waits for them, and re-layouts  6.17 us (4%)
  other arithmetic  5.51 us (3%)
    ppermute x13, waiting for transfers between devices, moved(): return lax.ppermute(value, axis, pairs)  31.7 us
    ppermute x7, waiting for transfers between devices, moved_across(): return lax.ppermute(value, ('tower', 'seq'), both)  30 us
    ppermute x13, starting transfers between devices, moved(): return lax.ppermute(value, axis, pairs)  20.4 us
    ppermute x7, starting transfers between devices, moved_across(): return lax.ppermute(value, ('tower', 'seq'), both)  15.7 us
    pallas_call x2, Pallas kernels, projection(): pl.pallas_call(projection_kernel, out_shape=jax.ShapeDtypeStruct((rows, 2...  14.5 us
    pallas_call x1, Pallas kernels, attention(): pl.pallas_call(attention_kernel, out_shape=[shape] * 2 + [pair_shape] * 3...  13.5 us
    pallas_call x1, Pallas kernels, context_partial(): pl.pallas_call(context_kernel, out_shape=jax.ShapeDtypeStruct((rows, widt...  10.3 us
    all_to_all x1, starting transfers between devices, local(): lax.all_to_all(partial_w.reshape(plane, -1, columns), 'seq', 0, 0, axis_i...  6.29 us
  transfers between devices with their start and end apart: 21, of which 9 were waited for; matrix products, arithmetic and copies ran while one was open for 4% of the time, Pallas kernels for 26%

profile of v4, /device:TPU:0, one launch (start us, length us, event | category | flops | bytes accessed | tf_op | source)
XLA Modules:
  0.0 167.4 jit_solution(4200693114444309850)
XLA Ops:
  2.7 2.9 %collective-permute-start.1 = (bf16[272,768]{1,0:T(8,128)(2,1)S(1)}, bf16[272,768]{1,0:T(8,128)(2,1)S(1)}, u32[]{:S(2)}, u32[]{:S(2)}) collective-permute-start(bf16[272,768]{1,0:T(8,128)(2,1)S(1)} %get-tuple-element.74), channel_id=1, source_target_pairs={{0,6},{2,4},{4,2},{6,0},{8,14},{10,12},{12,10},{14,8},{16,22},{18,... | collective-permute-start | bytes 1253384 | tf_op jit(solution)/shard_map/ppermute | solution.py:21
  6.5 7.2 %projection.2 = bf16[256,768]{1,0:T(8,128)(2,1)} custom-call(s32[1]{0:T(128)} %bitcast.4.which, bf16[256,3072]{1,0:T(8,128)(2,1)} %bitcast.35, bf16[3072,2,768]{2,1,0:T(2,128)(2,1)} %bitcast.32), custom_call_target="tpu_custom_call" | custom-call | flops 1207959552 | bytes 20971520 | tf_op jit(solution)/shard_map/projection/pallas_call | solution.py:119
  14.9 5.4 %collective-permute-start.5 = (bf16[256,768]{1,0:T(8,128)(2,1)}, bf16[256,768]{1,0:T(8,128)(2,1)}, u32[]{:S(2)}, u32[]{:S(2)}) collective-permute-start(bf16[256,768]{1,0:T(8,128)(2,1)} %projection.2), channel_id=1, source_target_pairs={{0,70},{2,68},{4,66},{6,64},{8,78},{10,76},{12,74},{14,72},{16,86}... | collective-permute-start | bytes 1179656 | tf_op jit(solution)/shard_map/ppermute | solution.py:34
  20.4 7.3 %projection.3 = bf16[256,768]{1,0:T(8,128)(2,1)} custom-call(s32[1]{0:T(128)} %bitcast.1.which.member, bf16[256,3072]{1,0:T(8,128)(2,1)} %bitcast.36, bf16[3072,2,768]{2,1,0:T(2,128)(2,1)} %bitcast.33), custom_call_target="tpu_custom_call" | custom-call | flops 1207959552 | bytes 20971520 | tf_op jit(solution)/shard_map/projection/pallas_call | solution.py:119
  29.0 3.5 %collective-permute-start.4 = (bf16[256,768]{1,0:T(8,128)(2,1)}, bf16[256,768]{1,0:T(8,128)(2,1)}, u32[]{:S(2)}, u32[]{:S(2)}) collective-permute-start(bf16[256,768]{1,0:T(8,128)(2,1)} %projection.3), channel_id=1, source_target_pairs={{0,68},{2,70},{4,64},{6,66},{8,76},{10,78},{12,72},{14,74},{16,84}... | collective-permute-start | bytes 1179656 | tf_op jit(solution)/shard_map/ppermute | solution.py:34
  33.6 7.3 %collective-permute-done.6.refs_4_ = bf16[256,768]{1,0:T(8,128)(2,1)} collective-permute-done((bf16[256,768]{1,0:T(8,128)(2,1)}, bf16[256,768]{1,0:T(8,128)(2,1)}, u32[]{:S(2)}, u32[]{:S(2)}) %collective-permute-start.6) | collective-permute-done | bytes 393248 | tf_op jit(solution)/shard_map/ppermute | solution.py:34
  40.9 5.3 %collective-permute-done.4.refs_2_ = bf16[256,768]{1,0:T(8,128)(2,1)} collective-permute-done((bf16[256,768]{1,0:T(8,128)(2,1)}, bf16[256,768]{1,0:T(8,128)(2,1)}, u32[]{:S(2)}, u32[]{:S(2)}) %collective-permute-start.4) | collective-permute-done | bytes 393248 | tf_op jit(solution)/shard_map/ppermute | solution.py:34
  46.7 1.9 %collective-permute-start.9 = (bf16[256,1536]{1,0:T(8,128)(2,1)}, bf16[256,1536]{1,0:T(8,128)(2,1)}, u32[]{:S(2)}, u32[]{:S(2)}) collective-permute-start(bf16[256,1536]{1,0:T(8,128)(2,1)} %get-tuple-element.45), channel_id=1, source_target_pairs={{0,32},{2,34},{4,36},{6,38},{8,40},{10,42},{12,44},{14,46},{16,48}... | collective-permute-start | bytes 2359304 | tf_op jit(solution)/shard_map/ppermute | solution.py:21
  49.3 13.5 %attention.1 = (bf16[256,768]{1,0:T(8,128)(2,1)}, bf16[256,768]{1,0:T(8,128)(2,1)}, bf16[512,768]{1,0:T(8,128)(2,1)}, bf16[512,768]{1,0:T(8,128)(2,1)}, bf16[512,768]{1,0:T(8,128)(2,1)}) custom-call(s32[7]{0:T(128)} %concatenate.28.meta, bf16[272,768]{1,0:T(8,128)(2,1)} %copy-done.5, bf16[272,768]{1,0:T(8,128)(2,1)} %copy-done.5, ...), custom_call_target="tpu_custom_call" | custom-call | flops 2516582400 | bytes 8388608 | tf_op jit(solution)/shard_map/attention/pallas_call | solution.py:214
  62.8 1.7 %collective-permute-start.11 = (bf16[512,768]{1,0:T(8,128)(2,1)}, bf16[512,768]{1,0:T(8,128)(2,1)S(1)}, u32[]{:S(2)}, u32[]{:S(2)}) collective-permute-start(bf16[512,768]{1,0:T(8,128)(2,1)} %get-tuple-element.49), channel_id=1, source_target_pairs={{0,68},{2,70},{4,64},{6,66},{8,76},{10,78},{12,72},{14,74},{16,84}... | collective-permute-start | bytes 2359304 | tf_op jit(solution)/shard_map/ppermute | solution.py:34
  64.5 2.5 %collective-permute-start.12 = (bf16[512,768]{1,0:T(8,128)(2,1)}, bf16[512,768]{1,0:T(8,128)(2,1)S(1)}, u32[]{:S(2)}, u32[]{:S(2)}) collective-permute-start(bf16[512,768]{1,0:T(8,128)(2,1)} %get-tuple-element.50), channel_id=1, source_target_pairs={{0,72},{2,74},{8,80},{10,82},{12,68},{14,70},{16,88},{18,90},{20,7... | collective-permute-start | bytes 2359304 | tf_op jit(solution)/shard_map/ppermute | solution.py:34
  67.4 17.0 %collective-permute-done.11 = bf16[512,768]{1,0:T(8,128)(2,1)S(1)} collective-permute-done((bf16[512,768]{1,0:T(8,128)(2,1)}, bf16[512,768]{1,0:T(8,128)(2,1)S(1)}, u32[]{:S(2)}, u32[]{:S(2)}) %collective-permute-start.11) | collective-permute-done | bytes 786464 | tf_op jit(solution)/shard_map/ppermute | solution.py:34
  85.5 2.8 %collective-permute-start.16 = (bf16[256,768]{1,0:T(8,128)(2,1)S(1)}, bf16[256,768]{1,0:T(8,128)(2,1)S(1)}, u32[]{:S(2)}, u32[]{:S(2)}) collective-permute-start(bf16[256,768]{1,0:T(8,128)(2,1)S(1)} %copy-done.7), channel_id=1, source_target_pairs={{0,6},{2,4},{4,2},{6,0},{8,14},{10,12},{12,10},{14,8},{16,22},{18,... | collective-permute-start | bytes 1179656 | tf_op jit(solution)/shard_map/ppermute | solution.py:21
  89.9 7.3 %collective-permute-done.15.grad_next = bf16[256,768]{1,0:T(8,128)(2,1)S(1)} collective-permute-done((bf16[256,768]{1,0:T(8,128)(2,1)S(1)}, bf16[256,768]{1,0:T(8,128)(2,1)S(1)}, u32[]{:S(2)}, u32[]{:S(2)}) %collective-permute-start.15) | collective-permute-done | bytes 393248 | tf_op jit(solution)/shard_map/ppermute | solution.py:21
  98.1 10.3 %context_partial.1 = bf16[256,3072]{1,0:T(8,128)(2,1)S(1)} custom-call(s32[1]{0:T(128)} %bitcast.1.which.member, bf16[512,768]{1,0:T(8,128)(2,1)S(1)} %add_convert_fusion.1.grad, bf16[256,768]{1,0:T(8,128)(2,1)S(1)} %collective-permute-done.15.grad_next, bf16[3072,2,768]{2,1,0:T(2,128)(2,1)} %bitcast.34), custom_call_target="tpu_custom_call" | custom-call | flops 2415919104 | bytes 12582912 | tf_op jit(solution)/shard_map/context_partial/pallas_call | solution.py:282
  108.4 3.7 %collective-permute-start.17 = (bf16[256,1024]{1,0:T(8,128)(2,1)S(1)}, bf16[256,1024]{1,0:T(8,128)(2,1)}, u32[]{:S(2)}, u32[]{:S(2)}) collective-permute-start(bf16[256,1024]{1,0:T(8,128)(2,1)S(1)} %slice.37), channel_id=1, source_target_pairs={{0,1},{1,0},{2,3},{3,2},{4,5},{5,4},{6,7},{7,6},{8,9},{9,8},{10,11... | collective-permute-start | bytes 1572872 | tf_op jit(solution)/shard_map/ppermute | solution.py:21
  112.1 2.8 %collective-permute-start.18 = (bf16[256,768]{1,0:T(8,128)(2,1)S(1)}, bf16[256,768]{1,0:T(8,128)(2,1)S(1)}, u32[]{:S(2)}, u32[]{:S(2)}) collective-permute-start(bf16[256,768]{1,0:T(8,128)(2,1)S(1)} %copy-done.6), channel_id=1, source_target_pairs={{0,4},{2,6},{4,0},{6,2},{8,12},{10,14},{12,8},{14,10},{16,20},{18,... | collective-permute-start | bytes 1179656 | tf_op jit(solution)/shard_map/ppermute | solution.py:21
  114.9 4.5 %weight_partial.1 = bf16[1536,768]{1,0:T(8,128)(2,1)S(1)} custom-call(bf16[256,1536]{1,0:T(8,128)(2,1)S(1)} %get-tuple-element.44.own, bf16[256,1536]{1,0:T(8,128)(2,1)} %collective-permute-done.9.own_z, bf16[256,1536]{1,0:T(8,128)(2,1)S(1)} %collective-permute-done.8.pair, bf16[256,1536]{1,0:T(8,128)(2,1)S(1)} %collective-permute-done.13.pair_z, ...), custom_call_target="tpu_custom_call" | custom-call | flops 2415919104 | bytes 8388608 | tf_op jit(solution)/shard_map/weight_partial/pallas_call | solution.py:251
  120.8 3.6 %collective-permute-done.18 = bf16[256,768]{1,0:T(8,128)(2,1)S(1)} collective-permute-done((bf16[256,768]{1,0:T(8,128)(2,1)S(1)}, bf16[256,768]{1,0:T(8,128)(2,1)S(1)}, u32[]{:S(2)}, u32[]{:S(2)}) %collective-permute-start.18) | collective-permute-done | bytes 393248 | tf_op jit(solution)/shard_map/ppermute | solution.py:21
  125.2 6.3 %all-to-all-start = ((bf16[16,96,768]{2,1,0:T(8,128)(2,1)}), bf16[16,96,768]{2,1,0:T(8,128)(2,1)}, u32[]{:S(2)}, u32[]{:S(2)}) async-start(bf16[16,96,768]{2,1,0:T(8,128)(2,1)} %bitcast.31), calls=%async_computation | async-start | bytes 4718592 | tf_op jit(solution)/shard_map/all_to_all | solution.py:379
  131.6 2.5 %collective-permute-start.19 = (bf16[256,2048]{1,0:T(8,128)(2,1)S(1)}, bf16[256,2048]{1,0:T(8,128)(2,1)S(1)}, u32[]{:S(2)}, u32[]{:S(2)}) collective-permute-start(bf16[256,2048]{1,0:T(8,128)(2,1)S(1)} %slice.38), channel_id=1, source_target_pairs={{0,1},{1,0},{2,3},{3,2},{4,5},{5,4},{6,7},{7,6},{8,9},{9,8},{10,11... | collective-permute-start | bytes 3145736 | tf_op jit(solution)/shard_map/ppermute | solution.py:21
  137.0 20.0 %collective-permute-done.19 = bf16[256,2048]{1,0:T(8,128)(2,1)S(1)} collective-permute-done((bf16[256,2048]{1,0:T(8,128)(2,1)S(1)}, bf16[256,2048]{1,0:T(8,128)(2,1)S(1)}, u32[]{:S(2)}, u32[]{:S(2)}) %collective-permute-start.19) | collective-permute-done | bytes 1048608 | tf_op jit(solution)/shard_map/ppermute | solution.py:21
  158.6 6.2 %all-to-all-done.parts = bf16[16,96,768]{2,1,0:T(8,128)(2,1)} async-done(((bf16[16,96,768]{2,1,0:T(8,128)(2,1)}), bf16[16,96,768]{2,1,0:T(8,128)(2,1)}, u32[]{:S(2)}, u32[]{:S(2)}) %all-to-all-start) | async-done | bytes 2359328 | tf_op jit(solution)/shard_map/all_to_all | solution.py:379
  164.8 1.8 %weight_total.1 = bf16[96,1536]{1,0:T(8,128)(2,1)S(1)} custom-call(bf16[16,96,768]{2,1,0:T(8,128)(2,1)} %all-to-all-done.parts), custom_call_target="tpu_custom_call" | custom-call | tf_op jit(solution)/shard_map/weight_total/pallas_call | solution.py:79
  (59 shorter events, 19.4 us)
Async XLA Ops:
  2.7 24.9 %collective-permute-start.1 = (bf16[272,768]{1,0:T(8,128)(2,1)S(1)}, bf16[272,768]{1,0:T(8,128)(2,1)S(1)}, u32[]{:S(2)}, u32[]{:S(2)}) collective-permute-start(bf16[272,768]{1,0:T(8,128)(2,1)S(1)} %get-tuple-element.74), channel_id=1, source_target_pairs={{0,6},{2,4},{4,2},{6,0},{8,14},{10,12},{12,10},{14,8},{16,22},{18,... | collective-permute-start | bytes 1253384 | tf_op jit(solution)/shard_map/ppermute | solution.py:21
  5.7 22.0 %collective-permute-start = (bf16[272,768]{1,0:T(8,128)(2,1)S(1)}, bf16[272,768]{1,0:T(8,128)(2,1)S(1)}, u32[]{:S(2)}, u32[]{:S(2)}) collective-permute-start(bf16[272,768]{1,0:T(8,128)(2,1)S(1)} %get-tuple-element.75), channel_id=1, source_target_pairs={{0,4},{2,6},{4,0},{6,2},{8,12},{10,14},{12,8},{14,10},{16,20},{18,... | collective-permute-start | bytes 1253384 | tf_op jit(solution)/shard_map/ppermute | solution.py:21
  13.7 18.9 %collective-permute-start.7 = (bf16[256,768]{1,0:T(8,128)(2,1)}, bf16[256,768]{1,0:T(8,128)(2,1)}, u32[]{:S(2)}, u32[]{:S(2)}) collective-permute-start(bf16[256,768]{1,0:T(8,128)(2,1)} %projection.2), channel_id=1, source_target_pairs={{4,78},{6,76},{8,66},{10,64},{12,86},{14,84},{16,74},{18,72},{20,9... | collective-permute-start | bytes 1179656 | tf_op jit(solution)/shard_map/ppermute | solution.py:34
  14.9 18.6 %collective-permute-start.5 = (bf16[256,768]{1,0:T(8,128)(2,1)}, bf16[256,768]{1,0:T(8,128)(2,1)}, u32[]{:S(2)}, u32[]{:S(2)}) collective-permute-start(bf16[256,768]{1,0:T(8,128)(2,1)} %projection.2), channel_id=1, source_target_pairs={{0,70},{2,68},{4,66},{6,64},{8,78},{10,76},{12,74},{14,72},{16,86}... | collective-permute-start | bytes 1179656 | tf_op jit(solution)/shard_map/ppermute | solution.py:34
  20.4 13.2 %collective-permute-start.3 = (bf16[256,768]{1,0:T(8,128)(2,1)}, bf16[256,768]{1,0:T(8,128)(2,1)}, u32[]{:S(2)}, u32[]{:S(2)}) collective-permute-start(bf16[256,768]{1,0:T(8,128)(2,1)} %projection.2), channel_id=1, source_target_pairs={{0,66},{2,64},{4,70},{6,68},{8,74},{10,72},{12,78},{14,76},{16,82}... | collective-permute-start | bytes 1179656 | tf_op jit(solution)/shard_map/ppermute | solution.py:34
  27.7 21.0 %copy-start.4 = (bf16[272,768]{1,0:T(8,128)(2,1)}, bf16[272,768]{1,0:T(8,128)(2,1)S(1)}, u32[]{:S(2)}) copy-start(bf16[272,768]{1,0:T(8,128)(2,1)S(1)} %collective-permute-done.1.q_b.c_b) | copy-start | bytes 1253380
  27.7 21.0 %copy-start.5 = (bf16[272,768]{1,0:T(8,128)(2,1)}, bf16[272,768]{1,0:T(8,128)(2,1)S(1)}, u32[]{:S(2)}) copy-start(bf16[272,768]{1,0:T(8,128)(2,1)S(1)} %collective-permute-done.q_a.c_a) | copy-start | bytes 1253380
  27.7 13.2 %collective-permute-start.6 = (bf16[256,768]{1,0:T(8,128)(2,1)}, bf16[256,768]{1,0:T(8,128)(2,1)}, u32[]{:S(2)}, u32[]{:S(2)}) collective-permute-start(bf16[256,768]{1,0:T(8,128)(2,1)} %projection.3), channel_id=1, source_target_pairs={{4,76},{6,78},{8,64},{10,66},{12,84},{14,86},{16,72},{18,74},{20,9... | collective-permute-start | bytes 1179656 | tf_op jit(solution)/shard_map/ppermute | solution.py:34
  29.0 17.1 %collective-permute-start.4 = (bf16[256,768]{1,0:T(8,128)(2,1)}, bf16[256,768]{1,0:T(8,128)(2,1)}, u32[]{:S(2)}, u32[]{:S(2)}) collective-permute-start(bf16[256,768]{1,0:T(8,128)(2,1)} %projection.3), channel_id=1, source_target_pairs={{0,68},{2,70},{4,64},{6,66},{8,76},{10,78},{12,72},{14,74},{16,84}... | collective-permute-start | bytes 1179656 | tf_op jit(solution)/shard_map/ppermute | solution.py:34
  32.5 13.6 %collective-permute-start.2 = (bf16[256,768]{1,0:T(8,128)(2,1)}, bf16[256,768]{1,0:T(8,128)(2,1)}, u32[]{:S(2)}, u32[]{:S(2)}) collective-permute-start(bf16[256,768]{1,0:T(8,128)(2,1)} %projection.3), channel_id=1, source_target_pairs={{0,64},{64,0},{1,65},{65,1},{2,66},{66,2},{3,67},{67,3},{4,68},{68... | collective-permute-start | bytes 1179656 | tf_op jit(solution)/shard_map/ppermute | solution.py:21
  46.1 20.9 %collective-permute-start.8 = (bf16[256,1536]{1,0:T(8,128)(2,1)S(1)}, bf16[256,1536]{1,0:T(8,128)(2,1)S(1)}, u32[]{:S(2)}, u32[]{:S(2)}) collective-permute-start(bf16[256,1536]{1,0:T(8,128)(2,1)S(1)} %get-tuple-element.44.own), channel_id=1, source_target_pairs={{0,2},{2,0},{4,6},{6,4},{8,10},{10,8},{12,14},{14,12},{16,18},{18,... | collective-permute-start | bytes 2359304 | tf_op jit(solution)/shard_map/ppermute | solution.py:21
  46.7 20.3 %collective-permute-start.9 = (bf16[256,1536]{1,0:T(8,128)(2,1)}, bf16[256,1536]{1,0:T(8,128)(2,1)}, u32[]{:S(2)}, u32[]{:S(2)}) collective-permute-start(bf16[256,1536]{1,0:T(8,128)(2,1)} %get-tuple-element.45), channel_id=1, source_target_pairs={{0,32},{2,34},{4,36},{6,38},{8,40},{10,42},{12,44},{14,46},{16,48}... | collective-permute-start | bytes 2359304 | tf_op jit(solution)/shard_map/ppermute | solution.py:21
  62.8 21.6 %collective-permute-start.11 = (bf16[512,768]{1,0:T(8,128)(2,1)}, bf16[512,768]{1,0:T(8,128)(2,1)S(1)}, u32[]{:S(2)}, u32[]{:S(2)}) collective-permute-start(bf16[512,768]{1,0:T(8,128)(2,1)} %get-tuple-element.49), channel_id=1, source_target_pairs={{0,68},{2,70},{4,64},{6,66},{8,76},{10,78},{12,72},{14,74},{16,84}... | collective-permute-start | bytes 2359304 | tf_op jit(solution)/shard_map/ppermute | solution.py:34
  64.5 20.3 %collective-permute-start.12 = (bf16[512,768]{1,0:T(8,128)(2,1)}, bf16[512,768]{1,0:T(8,128)(2,1)S(1)}, u32[]{:S(2)}, u32[]{:S(2)}) collective-permute-start(bf16[512,768]{1,0:T(8,128)(2,1)} %get-tuple-element.50), channel_id=1, source_target_pairs={{0,72},{2,74},{8,80},{10,82},{12,68},{14,70},{16,88},{18,90},{20,7... | collective-permute-start | bytes 2359304 | tf_op jit(solution)/shard_map/ppermute | solution.py:34
  67.0 17.8 %collective-permute-start.10 = (bf16[512,768]{1,0:T(8,128)(2,1)}, bf16[512,768]{1,0:T(8,128)(2,1)S(1)}, u32[]{:S(2)}, u32[]{:S(2)}) collective-permute-start(bf16[512,768]{1,0:T(8,128)(2,1)} %get-tuple-element.48), channel_id=1, source_target_pairs={{0,64},{64,0},{1,65},{65,1},{2,66},{66,2},{3,67},{67,3},{4,68},{68... | collective-permute-start | bytes 2359304 | tf_op jit(solution)/shard_map/ppermute | solution.py:21
  85.1 27.0 %copy-start.6 = (bf16[256,768]{1,0:T(8,128)(2,1)S(1)}, bf16[256,768]{1,0:T(8,128)(2,1)}, u32[]{:S(2)}) copy-start(bf16[256,768]{1,0:T(8,128)(2,1)} %get-tuple-element.56) | copy-start | bytes 1179652
  85.1 12.1 %collective-permute-start.15 = (bf16[256,768]{1,0:T(8,128)(2,1)S(1)}, bf16[256,768]{1,0:T(8,128)(2,1)S(1)}, u32[]{:S(2)}, u32[]{:S(2)}) collective-permute-start(bf16[256,768]{1,0:T(8,128)(2,1)S(1)} %slice.36), channel_id=1, source_target_pairs={{0,2},{2,0},{4,6},{6,4},{8,10},{10,8},{12,14},{14,12},{16,18},{18,... | collective-permute-start | bytes 1179656 | tf_op jit(solution)/shard_map/ppermute | solution.py:21
  85.5 12.6 %collective-permute-start.16 = (bf16[256,768]{1,0:T(8,128)(2,1)S(1)}, bf16[256,768]{1,0:T(8,128)(2,1)S(1)}, u32[]{:S(2)}, u32[]{:S(2)}) collective-permute-start(bf16[256,768]{1,0:T(8,128)(2,1)S(1)} %copy-done.7), channel_id=1, source_target_pairs={{0,6},{2,4},{4,2},{6,0},{8,14},{10,12},{12,10},{14,8},{16,22},{18,... | collective-permute-start | bytes 1179656 | tf_op jit(solution)/shard_map/ppermute | solution.py:21
  88.3 26.7 %collective-permute-start.13 = (bf16[256,1536]{1,0:T(8,128)(2,1)}, bf16[256,1536]{1,0:T(8,128)(2,1)S(1)}, u32[]{:S(2)}, u32[]{:S(2)}) collective-permute-start(bf16[256,1536]{1,0:T(8,128)(2,1)} %collective-permute-done.9.own_z), channel_id=1, source_target_pairs={{0,2},{2,0},{4,6},{6,4},{8,10},{10,8},{12,14},{14,12},{16,18},{18,... | collective-permute-start | bytes 2359304 | tf_op jit(solution)/shard_map/ppermute | solution.py:21
  89.6 25.3 %collective-permute-start.14 = (bf16[512,768]{1,0:T(8,128)(2,1)S(1)}, bf16[512,768]{1,0:T(8,128)(2,1)S(1)}, u32[]{:S(2)}, u32[]{:S(2)}) collective-permute-start(bf16[512,768]{1,0:T(8,128)(2,1)S(1)} %add_convert_fusion.1.grad), channel_id=1, source_target_pairs={{0,32},{2,34},{4,36},{6,38},{8,40},{10,42},{12,44},{14,46},{16,48}... | collective-permute-start | bytes 2359304 | tf_op jit(solution)/shard_map/ppermute | solution.py:21
  108.4 16.0 %collective-permute-start.17 = (bf16[256,1024]{1,0:T(8,128)(2,1)S(1)}, bf16[256,1024]{1,0:T(8,128)(2,1)}, u32[]{:S(2)}, u32[]{:S(2)}) collective-permute-start(bf16[256,1024]{1,0:T(8,128)(2,1)S(1)} %slice.37), channel_id=1, source_target_pairs={{0,1},{1,0},{2,3},{3,2},{4,5},{5,4},{6,7},{7,6},{8,9},{9,8},{10,11... | collective-permute-start | bytes 1572872 | tf_op jit(solution)/shard_map/ppermute | solution.py:21
  112.1 12.3 %collective-permute-start.18 = (bf16[256,768]{1,0:T(8,128)(2,1)S(1)}, bf16[256,768]{1,0:T(8,128)(2,1)S(1)}, u32[]{:S(2)}, u32[]{:S(2)}) collective-permute-start(bf16[256,768]{1,0:T(8,128)(2,1)S(1)} %copy-done.6), channel_id=1, source_target_pairs={{0,4},{2,6},{4,0},{6,2},{8,12},{10,14},{12,8},{14,10},{16,20},{18,... | collective-permute-start | bytes 1179656 | tf_op jit(solution)/shard_map/ppermute | solution.py:21
  125.2 39.6 %all-to-all-start = ((bf16[16,96,768]{2,1,0:T(8,128)(2,1)}), bf16[16,96,768]{2,1,0:T(8,128)(2,1)}, u32[]{:S(2)}, u32[]{:S(2)}) async-start(bf16[16,96,768]{2,1,0:T(8,128)(2,1)} %bitcast.31), calls=%async_computation | async-start | bytes 4718592 | tf_op jit(solution)/shard_map/all_to_all | solution.py:379
  131.6 25.4 %collective-permute-start.19 = (bf16[256,2048]{1,0:T(8,128)(2,1)S(1)}, bf16[256,2048]{1,0:T(8,128)(2,1)S(1)}, u32[]{:S(2)}, u32[]{:S(2)}) collective-permute-start(bf16[256,2048]{1,0:T(8,128)(2,1)S(1)} %slice.38), channel_id=1, source_target_pairs={{0,1},{1,0},{2,3},{3,2},{4,5},{5,4},{6,7},{7,6},{8,9},{9,8},{10,11... | collective-permute-start | bytes 3145736 | tf_op jit(solution)/shard_map/ppermute | solution.py:21
  (5 other events, 35.5 us)

commit v5 on v4

--- a/solution.py
+++ b/solution.py
@@ -144,7 +144,7 @@
     member, side = meta[0], meta[6]
     scale = HD ** (-0.5)
     unit = scale * LOG2E
-    results = []
+    results, terms = [], []
     near, far = 4 * side, 4 * (1 - side)
     order = (near + member, near + 1 - member, 2 + member, 3 - member, far + member, far + 1 - member)
     for ref, place in zip(kv_refs, order):
@@ -152,17 +152,24 @@
     for ref, other, scratch in ((q_a, q_b, q_s), (c_a, c_b, c_s)):
         scratch[pl.ds(pl.multiple_of(member * rows, rows), rows), :] = ref[...]
         scratch[pl.ds(pl.multiple_of((1 - member) * rows, rows), rows), :] = other[...]
-    g_s[...] = jnp.zeros_like(g_s)
     span = 2 * REACH + 1
+    block = lambda v, j: v[j * rows : (j + 1) * rows]
+    products = []
     for i in range(PAIR):
-        q = q_s[i * rows : (i + 1) * rows, :]
-        c = c_s[i * rows : (i + 1) * rows, :]
+        shard = slice(i * rows, (i + 1) * rows)
+        window = slice(i * rows, (i + span) * rows)
+        products.append(
+            (
+                dot(kv_s[window, :HD], q_s[shard, :], ((1,), (1,))),
+                dot(kv_s[window, HD:], c_s[shard, :], ((1,), (1,))),
+            )
+        )
+    for i in range(PAIR):
         window = slice(i * rows, (i + span) * rows)
         keys = kv_s[window, :HD]
         values = kv_s[window, HD:]
         low, high = meta[2 + 2 * i], meta[3 + 2 * i]
-        scores = dot(keys, q, ((1,), (1,)))
-        block = lambda v, j: v[j * rows : (j + 1) * rows]
+        scores, dprobs = products[i]
         offsets = []
         for j in range(span):
             shard = meta[1] + i + j
@@ -177,26 +184,31 @@
         norm = functools.reduce(jnp.add, [jnp.sum(e, axis=0, keepdims=True) for e in expo])
         probs = jnp.concatenate(expo, axis=0) * (1.0 / norm)
         rounded = probs.astype(BF16)
-        dprobs = dot(values, c, ((1,), (1,)))
         delta = jnp.sum(dprobs * probs, axis=0, keepdims=True)
         dscores = (probs * (dprobs - delta)).astype(BF16)
         out = dot(values, rounded, ((0,), (0,)))
         dq = dot(keys, dscores, ((0,), (0,))) * scale
-        g_s[window, :HD] += dot(dscores, q, ((1,), (0,)))
-        g_s[window, HD:] += dot(rounded, c, ((1,), (0,)))
+        terms.append((dscores, rounded))
         results.append([value.T.astype(BF16) for value in (out, dq)])
     head = pl.program_id(0)
     for part, (first, second) in enumerate(zip(*results)):
         columns = pl.ds(pl.multiple_of((part * heads + head) * HD, HD), HD)
         od_a[:, columns] = jnp.where(member == 0, first, second)
         od_b[:, columns] = jnp.where(member == 0, second, first)
-    g_s[:, :HD] *= scale
+    for w in range(WINDOW):
+        users = [i for i in range(PAIR) if 0 <= w - i < span]
+        over = slice(users[0] * rows, (users[-1] + 1) * rows)
+        for part, (scratch, factor) in enumerate(((q_s, scale), (c_s, 1.0))):
+            left = jnp.concatenate([block(terms[i][part], w - i) for i in users], axis=1)
+            value = dot(left, scratch[over, :], ((1,), (0,)))
+            value = value * factor if factor != 1.0 else value
+            g_s[w * rows : (w + 1) * rows, part * HD : (part + 1) * HD] = value.astype(BF16)
 
     for index, place in enumerate(order):
         begin = index % PAIR * rows
         g_refs[index // PAIR][begin : begin + rows, :] = g_s[
             pl.ds(pl.multiple_of(place * rows, rows), rows), :
-        ].astype(BF16)
+        ]
 
 
 def attention(meta, qc_a, qc_b, kv_blocks):
@@ -223,7 +235,7 @@
                 pltpu.VMEM((WINDOW * rows, 2 * HD), BF16),
                 pltpu.VMEM((PAIR * rows, HD), BF16),
                 pltpu.VMEM((PAIR * rows, HD), BF16),
-                pltpu.VMEM((WINDOW * rows, 2 * HD), F32),
+                pltpu.VMEM((WINDOW * rows, 2 * HD), BF16),
             ],
         ),
         compiler_params=pltpu.CompilerParams(vmem_limit_bytes=56 * 2**20),

time: 168 us -> 167 us (level)
  transfers between devices with their start and end apart: 21 -> 21, of which waited for: 9 -> 9; matrix products, arithmetic and copies ran while one was open for 4% -> 4% of each run, Pallas kernels for 26% -> 25%
where the time goes in v5:
time: 167 us; the launch traced here: 166 us
  waiting for transfers between devices  67.9 us (41%)
  Pallas kernels  43.7 us (26%)
  starting transfers between devices  42.4 us (25%)
  local copies, waits for them, and re-layouts  6.17 us (4%)
  other arithmetic  5.51 us (3%)
    ppermute x13, waiting for transfers between devices, moved(): return lax.ppermute(value, axis, pairs)  31.7 us
    ppermute x7, waiting for transfers between devices, moved_across(): return lax.ppermute(value, ('tower', 'seq'), both)  30 us
    ppermute x13, starting transfers between devices, moved(): return lax.ppermute(value, axis, pairs)  20.4 us
    ppermute x7, starting transfers between devices, moved_across(): return lax.ppermute(value, ('tower', 'seq'), both)  15.7 us
    pallas_call x2, Pallas kernels, projection(): pl.pallas_call(projection_kernel, out_shape=jax.ShapeDtypeStruct((rows, 2...  14.5 us
    pallas_call x1, Pallas kernels, attention(): pl.pallas_call(attention_kernel, out_shape=[shape] * 2 + [pair_shape] * 3...  12.6 us
    pallas_call x1, Pallas kernels, context_partial(): pl.pallas_call(context_kernel, out_shape=jax.ShapeDtypeStruct((rows, widt...  10.3 us
    all_to_all x1, starting transfers between devices, local(): lax.all_to_all(partial_w.reshape(plane, -1, columns), 'seq', 0, 0, axis_i...  6.28 us
  transfers between devices with their start and end apart: 21, of which 9 were waited for; matrix products, arithmetic and copies ran while one was open for 4% of the time, Pallas kernels for 25%

profile of v5, /device:TPU:0, one launch (start us, length us, event | category | flops | bytes accessed | tf_op | source)
XLA Modules:
  0.0 166.5 jit_solution(14894481406261317745)
XLA Ops:
  2.7 2.9 %collective-permute-start.1 = (bf16[272,768]{1,0:T(8,128)(2,1)S(1)}, bf16[272,768]{1,0:T(8,128)(2,1)S(1)}, u32[]{:S(2)}, u32[]{:S(2)}) collective-permute-start(bf16[272,768]{1,0:T(8,128)(2,1)S(1)} %get-tuple-element.74), channel_id=1, source_target_pairs={{0,6},{2,4},{4,2},{6,0},{8,14},{10,12},{12,10},{14,8},{16,22},{18,... | collective-permute-start | bytes 1253384 | tf_op jit(solution)/shard_map/ppermute | solution.py:21
  6.5 7.2 %projection.2 = bf16[256,768]{1,0:T(8,128)(2,1)} custom-call(s32[1]{0:T(128)} %bitcast.4.which, bf16[256,3072]{1,0:T(8,128)(2,1)} %bitcast.35, bf16[3072,2,768]{2,1,0:T(2,128)(2,1)} %bitcast.32), custom_call_target="tpu_custom_call" | custom-call | flops 1207959552 | bytes 20971520 | tf_op jit(solution)/shard_map/projection/pallas_call | solution.py:119
  14.9 5.4 %collective-permute-start.5 = (bf16[256,768]{1,0:T(8,128)(2,1)}, bf16[256,768]{1,0:T(8,128)(2,1)}, u32[]{:S(2)}, u32[]{:S(2)}) collective-permute-start(bf16[256,768]{1,0:T(8,128)(2,1)} %projection.2), channel_id=1, source_target_pairs={{0,70},{2,68},{4,66},{6,64},{8,78},{10,76},{12,74},{14,72},{16,86}... | collective-permute-start | bytes 1179656 | tf_op jit(solution)/shard_map/ppermute | solution.py:34
  20.4 7.3 %projection.3 = bf16[256,768]{1,0:T(8,128)(2,1)} custom-call(s32[1]{0:T(128)} %bitcast.1.which.member, bf16[256,3072]{1,0:T(8,128)(2,1)} %bitcast.36, bf16[3072,2,768]{2,1,0:T(2,128)(2,1)} %bitcast.33), custom_call_target="tpu_custom_call" | custom-call | flops 1207959552 | bytes 20971520 | tf_op jit(solution)/shard_map/projection/pallas_call | solution.py:119
  29.0 3.5 %collective-permute-start.4 = (bf16[256,768]{1,0:T(8,128)(2,1)}, bf16[256,768]{1,0:T(8,128)(2,1)}, u32[]{:S(2)}, u32[]{:S(2)}) collective-permute-start(bf16[256,768]{1,0:T(8,128)(2,1)} %projection.3), channel_id=1, source_target_pairs={{0,68},{2,70},{4,64},{6,66},{8,76},{10,78},{12,72},{14,74},{16,84}... | collective-permute-start | bytes 1179656 | tf_op jit(solution)/shard_map/ppermute | solution.py:34
  33.6 7.3 %collective-permute-done.6.refs_4_ = bf16[256,768]{1,0:T(8,128)(2,1)} collective-permute-done((bf16[256,768]{1,0:T(8,128)(2,1)}, bf16[256,768]{1,0:T(8,128)(2,1)}, u32[]{:S(2)}, u32[]{:S(2)}) %collective-permute-start.6) | collective-permute-done | bytes 393248 | tf_op jit(solution)/shard_map/ppermute | solution.py:34
  40.9 5.3 %collective-permute-done.4.refs_2_ = bf16[256,768]{1,0:T(8,128)(2,1)} collective-permute-done((bf16[256,768]{1,0:T(8,128)(2,1)}, bf16[256,768]{1,0:T(8,128)(2,1)}, u32[]{:S(2)}, u32[]{:S(2)}) %collective-permute-start.4) | collective-permute-done | bytes 393248 | tf_op jit(solution)/shard_map/ppermute | solution.py:34
  46.7 1.9 %collective-permute-start.9 = (bf16[256,1536]{1,0:T(8,128)(2,1)}, bf16[256,1536]{1,0:T(8,128)(2,1)}, u32[]{:S(2)}, u32[]{:S(2)}) collective-permute-start(bf16[256,1536]{1,0:T(8,128)(2,1)} %get-tuple-element.45), channel_id=1, source_target_pairs={{0,32},{2,34},{4,36},{6,38},{8,40},{10,42},{12,44},{14,46},{16,48}... | collective-permute-start | bytes 2359304 | tf_op jit(solution)/shard_map/ppermute | solution.py:21
  49.3 12.6 %attention.1 = (bf16[256,768]{1,0:T(8,128)(2,1)}, bf16[256,768]{1,0:T(8,128)(2,1)}, bf16[512,768]{1,0:T(8,128)(2,1)}, bf16[512,768]{1,0:T(8,128)(2,1)}, bf16[512,768]{1,0:T(8,128)(2,1)}) custom-call(s32[7]{0:T(128)} %concatenate.28.meta, bf16[272,768]{1,0:T(8,128)(2,1)} %copy-done.5, bf16[272,768]{1,0:T(8,128)(2,1)} %copy-done.5, ...), custom_call_target="tpu_custom_call" | custom-call | flops 2516582400 | bytes 8388608 | tf_op jit(solution)/shard_map/attention/pallas_call | solution.py:226
  61.9 1.7 %collective-permute-start.11 = (bf16[512,768]{1,0:T(8,128)(2,1)}, bf16[512,768]{1,0:T(8,128)(2,1)S(1)}, u32[]{:S(2)}, u32[]{:S(2)}) collective-permute-start(bf16[512,768]{1,0:T(8,128)(2,1)} %get-tuple-element.49), channel_id=1, source_target_pairs={{0,68},{2,70},{4,64},{6,66},{8,76},{10,78},{12,72},{14,74},{16,84}... | collective-permute-start | bytes 2359304 | tf_op jit(solution)/shard_map/ppermute | solution.py:34
  63.7 2.5 %collective-permute-start.12 = (bf16[512,768]{1,0:T(8,128)(2,1)}, bf16[512,768]{1,0:T(8,128)(2,1)S(1)}, u32[]{:S(2)}, u32[]{:S(2)}) collective-permute-start(bf16[512,768]{1,0:T(8,128)(2,1)} %get-tuple-element.50), channel_id=1, source_target_pairs={{0,72},{2,74},{8,80},{10,82},{12,68},{14,70},{16,88},{18,90},{20,7... | collective-permute-start | bytes 2359304 | tf_op jit(solution)/shard_map/ppermute | solution.py:34
  66.6 17.0 %collective-permute-done.11 = bf16[512,768]{1,0:T(8,128)(2,1)S(1)} collective-permute-done((bf16[512,768]{1,0:T(8,128)(2,1)}, bf16[512,768]{1,0:T(8,128)(2,1)S(1)}, u32[]{:S(2)}, u32[]{:S(2)}) %collective-permute-start.11) | collective-permute-done | bytes 786464 | tf_op jit(solution)/shard_map/ppermute | solution.py:34
  84.7 2.8 %collective-permute-start.16 = (bf16[256,768]{1,0:T(8,128)(2,1)S(1)}, bf16[256,768]{1,0:T(8,128)(2,1)S(1)}, u32[]{:S(2)}, u32[]{:S(2)}) collective-permute-start(bf16[256,768]{1,0:T(8,128)(2,1)S(1)} %copy-done.7), channel_id=1, source_target_pairs={{0,6},{2,4},{4,2},{6,0},{8,14},{10,12},{12,10},{14,8},{16,22},{18,... | collective-permute-start | bytes 1179656 | tf_op jit(solution)/shard_map/ppermute | solution.py:21
  89.1 7.3 %collective-permute-done.15.grad_next = bf16[256,768]{1,0:T(8,128)(2,1)S(1)} collective-permute-done((bf16[256,768]{1,0:T(8,128)(2,1)S(1)}, bf16[256,768]{1,0:T(8,128)(2,1)S(1)}, u32[]{:S(2)}, u32[]{:S(2)}) %collective-permute-start.15) | collective-permute-done | bytes 393248 | tf_op jit(solution)/shard_map/ppermute | solution.py:21
  97.2 10.3 %context_partial.1 = bf16[256,3072]{1,0:T(8,128)(2,1)S(1)} custom-call(s32[1]{0:T(128)} %bitcast.1.which.member, bf16[512,768]{1,0:T(8,128)(2,1)S(1)} %add_convert_fusion.1.grad, bf16[256,768]{1,0:T(8,128)(2,1)S(1)} %collective-permute-done.15.grad_next, bf16[3072,2,768]{2,1,0:T(2,128)(2,1)} %bitcast.34), custom_call_target="tpu_custom_call" | custom-call | flops 2415919104 | bytes 12582912 | tf_op jit(solution)/shard_map/context_partial/pallas_call | solution.py:294
  107.6 3.7 %collective-permute-start.17 = (bf16[256,1024]{1,0:T(8,128)(2,1)S(1)}, bf16[256,1024]{1,0:T(8,128)(2,1)}, u32[]{:S(2)}, u32[]{:S(2)}) collective-permute-start(bf16[256,1024]{1,0:T(8,128)(2,1)S(1)} %slice.37), channel_id=1, source_target_pairs={{0,1},{1,0},{2,3},{3,2},{4,5},{5,4},{6,7},{7,6},{8,9},{9,8},{10,11... | collective-permute-start | bytes 1572872 | tf_op jit(solution)/shard_map/ppermute | solution.py:21
  111.3 2.8 %collective-permute-start.18 = (bf16[256,768]{1,0:T(8,128)(2,1)S(1)}, bf16[256,768]{1,0:T(8,128)(2,1)S(1)}, u32[]{:S(2)}, u32[]{:S(2)}) collective-permute-start(bf16[256,768]{1,0:T(8,128)(2,1)S(1)} %copy-done.6), channel_id=1, source_target_pairs={{0,4},{2,6},{4,0},{6,2},{8,12},{10,14},{12,8},{14,10},{16,20},{18,... | collective-permute-start | bytes 1179656 | tf_op jit(solution)/shard_map/ppermute | solution.py:21
  114.1 4.5 %weight_partial.1 = bf16[1536,768]{1,0:T(8,128)(2,1)S(1)} custom-call(bf16[256,1536]{1,0:T(8,128)(2,1)S(1)} %get-tuple-element.44.own, bf16[256,1536]{1,0:T(8,128)(2,1)} %collective-permute-done.9.own_z, bf16[256,1536]{1,0:T(8,128)(2,1)S(1)} %collective-permute-done.8.pair, bf16[256,1536]{1,0:T(8,128)(2,1)S(1)} %collective-permute-done.13.pair_z, ...), custom_call_target="tpu_custom_call" | custom-call | flops 2415919104 | bytes 8388608 | tf_op jit(solution)/shard_map/weight_partial/pallas_call | solution.py:263
  120.0 3.6 %collective-permute-done.18 = bf16[256,768]{1,0:T(8,128)(2,1)S(1)} collective-permute-done((bf16[256,768]{1,0:T(8,128)(2,1)S(1)}, bf16[256,768]{1,0:T(8,128)(2,1)S(1)}, u32[]{:S(2)}, u32[]{:S(2)}) %collective-permute-start.18) | collective-permute-done | bytes 393248 | tf_op jit(solution)/shard_map/ppermute | solution.py:21
  124.3 6.3 %all-to-all-start = ((bf16[16,96,768]{2,1,0:T(8,128)(2,1)}), bf16[16,96,768]{2,1,0:T(8,128)(2,1)}, u32[]{:S(2)}, u32[]{:S(2)}) async-start(bf16[16,96,768]{2,1,0:T(8,128)(2,1)} %bitcast.31), calls=%async_computation | async-start | bytes 4718592 | tf_op jit(solution)/shard_map/all_to_all | solution.py:391
  130.7 2.5 %collective-permute-start.19 = (bf16[256,2048]{1,0:T(8,128)(2,1)S(1)}, bf16[256,2048]{1,0:T(8,128)(2,1)S(1)}, u32[]{:S(2)}, u32[]{:S(2)}) collective-permute-start(bf16[256,2048]{1,0:T(8,128)(2,1)S(1)} %slice.38), channel_id=1, source_target_pairs={{0,1},{1,0},{2,3},{3,2},{4,5},{5,4},{6,7},{7,6},{8,9},{9,8},{10,11... | collective-permute-start | bytes 3145736 | tf_op jit(solution)/shard_map/ppermute | solution.py:21
  136.1 20.0 %collective-permute-done.19 = bf16[256,2048]{1,0:T(8,128)(2,1)S(1)} collective-permute-done((bf16[256,2048]{1,0:T(8,128)(2,1)S(1)}, bf16[256,2048]{1,0:T(8,128)(2,1)S(1)}, u32[]{:S(2)}, u32[]{:S(2)}) %collective-permute-start.19) | collective-permute-done | bytes 1048608 | tf_op jit(solution)/shard_map/ppermute | solution.py:21
  157.7 6.2 %all-to-all-done.parts = bf16[16,96,768]{2,1,0:T(8,128)(2,1)} async-done(((bf16[16,96,768]{2,1,0:T(8,128)(2,1)}), bf16[16,96,768]{2,1,0:T(8,128)(2,1)}, u32[]{:S(2)}, u32[]{:S(2)}) %all-to-all-start) | async-done | bytes 2359328 | tf_op jit(solution)/shard_map/all_to_all | solution.py:391
  163.9 1.8 %weight_total.1 = bf16[96,1536]{1,0:T(8,128)(2,1)S(1)} custom-call(bf16[16,96,768]{2,1,0:T(8,128)(2,1)} %all-to-all-done.parts), custom_call_target="tpu_custom_call" | custom-call | tf_op jit(solution)/shard_map/weight_total/pallas_call | solution.py:79
  (59 shorter events, 19.4 us)
Async XLA Ops:
  2.7 24.9 %collective-permute-start.1 = (bf16[272,768]{1,0:T(8,128)(2,1)S(1)}, bf16[272,768]{1,0:T(8,128)(2,1)S(1)}, u32[]{:S(2)}, u32[]{:S(2)}) collective-permute-start(bf16[272,768]{1,0:T(8,128)(2,1)S(1)} %get-tuple-element.74), channel_id=1, source_target_pairs={{0,6},{2,4},{4,2},{6,0},{8,14},{10,12},{12,10},{14,8},{16,22},{18,... | collective-permute-start | bytes 1253384 | tf_op jit(solution)/shard_map/ppermute | solution.py:21
  5.7 22.0 %collective-permute-start = (bf16[272,768]{1,0:T(8,128)(2,1)S(1)}, bf16[272,768]{1,0:T(8,128)(2,1)S(1)}, u32[]{:S(2)}, u32[]{:S(2)}) collective-permute-start(bf16[272,768]{1,0:T(8,128)(2,1)S(1)} %get-tuple-element.75), channel_id=1, source_target_pairs={{0,4},{2,6},{4,0},{6,2},{8,12},{10,14},{12,8},{14,10},{16,20},{18,... | collective-permute-start | bytes 1253384 | tf_op jit(solution)/shard_map/ppermute | solution.py:21
  13.7 18.9 %collective-permute-start.7 = (bf16[256,768]{1,0:T(8,128)(2,1)}, bf16[256,768]{1,0:T(8,128)(2,1)}, u32[]{:S(2)}, u32[]{:S(2)}) collective-permute-start(bf16[256,768]{1,0:T(8,128)(2,1)} %projection.2), channel_id=1, source_target_pairs={{4,78},{6,76},{8,66},{10,64},{12,86},{14,84},{16,74},{18,72},{20,9... | collective-permute-start | bytes 1179656 | tf_op jit(solution)/shard_map/ppermute | solution.py:34
  14.9 18.6 %collective-permute-start.5 = (bf16[256,768]{1,0:T(8,128)(2,1)}, bf16[256,768]{1,0:T(8,128)(2,1)}, u32[]{:S(2)}, u32[]{:S(2)}) collective-permute-start(bf16[256,768]{1,0:T(8,128)(2,1)} %projection.2), channel_id=1, source_target_pairs={{0,70},{2,68},{4,66},{6,64},{8,78},{10,76},{12,74},{14,72},{16,86}... | collective-permute-start | bytes 1179656 | tf_op jit(solution)/shard_map/ppermute | solution.py:34
  20.4 13.2 %collective-permute-start.3 = (bf16[256,768]{1,0:T(8,128)(2,1)}, bf16[256,768]{1,0:T(8,128)(2,1)}, u32[]{:S(2)}, u32[]{:S(2)}) collective-permute-start(bf16[256,768]{1,0:T(8,128)(2,1)} %projection.2), channel_id=1, source_target_pairs={{0,66},{2,64},{4,70},{6,68},{8,74},{10,72},{12,78},{14,76},{16,82}... | collective-permute-start | bytes 1179656 | tf_op jit(solution)/shard_map/ppermute | solution.py:34
  27.7 21.0 %copy-start.4 = (bf16[272,768]{1,0:T(8,128)(2,1)}, bf16[272,768]{1,0:T(8,128)(2,1)S(1)}, u32[]{:S(2)}) copy-start(bf16[272,768]{1,0:T(8,128)(2,1)S(1)} %collective-permute-done.1.q_b.c_b) | copy-start | bytes 1253380
  27.7 21.0 %copy-start.5 = (bf16[272,768]{1,0:T(8,128)(2,1)}, bf16[272,768]{1,0:T(8,128)(2,1)S(1)}, u32[]{:S(2)}) copy-start(bf16[272,768]{1,0:T(8,128)(2,1)S(1)} %collective-permute-done.q_a.c_a) | copy-start | bytes 1253380
  27.7 13.2 %collective-permute-start.6 = (bf16[256,768]{1,0:T(8,128)(2,1)}, bf16[256,768]{1,0:T(8,128)(2,1)}, u32[]{:S(2)}, u32[]{:S(2)}) collective-permute-start(bf16[256,768]{1,0:T(8,128)(2,1)} %projection.3), channel_id=1, source_target_pairs={{4,76},{6,78},{8,64},{10,66},{12,84},{14,86},{16,72},{18,74},{20,9... | collective-permute-start | bytes 1179656 | tf_op jit(solution)/shard_map/ppermute | solution.py:34
  29.0 17.1 %collective-permute-start.4 = (bf16[256,768]{1,0:T(8,128)(2,1)}, bf16[256,768]{1,0:T(8,128)(2,1)}, u32[]{:S(2)}, u32[]{:S(2)}) collective-permute-start(bf16[256,768]{1,0:T(8,128)(2,1)} %projection.3), channel_id=1, source_target_pairs={{0,68},{2,70},{4,64},{6,66},{8,76},{10,78},{12,72},{14,74},{16,84}... | collective-permute-start | bytes 1179656 | tf_op jit(solution)/shard_map/ppermute | solution.py:34
  32.5 13.6 %collective-permute-start.2 = (bf16[256,768]{1,0:T(8,128)(2,1)}, bf16[256,768]{1,0:T(8,128)(2,1)}, u32[]{:S(2)}, u32[]{:S(2)}) collective-permute-start(bf16[256,768]{1,0:T(8,128)(2,1)} %projection.3), channel_id=1, source_target_pairs={{0,64},{64,0},{1,65},{65,1},{2,66},{66,2},{3,67},{67,3},{4,68},{68... | collective-permute-start | bytes 1179656 | tf_op jit(solution)/shard_map/ppermute | solution.py:21
  46.1 20.0 %collective-permute-start.8 = (bf16[256,1536]{1,0:T(8,128)(2,1)S(1)}, bf16[256,1536]{1,0:T(8,128)(2,1)S(1)}, u32[]{:S(2)}, u32[]{:S(2)}) collective-permute-start(bf16[256,1536]{1,0:T(8,128)(2,1)S(1)} %get-tuple-element.44.own), channel_id=1, source_target_pairs={{0,2},{2,0},{4,6},{6,4},{8,10},{10,8},{12,14},{14,12},{16,18},{18,... | collective-permute-start | bytes 2359304 | tf_op jit(solution)/shard_map/ppermute | solution.py:21
  46.7 19.4 %collective-permute-start.9 = (bf16[256,1536]{1,0:T(8,128)(2,1)}, bf16[256,1536]{1,0:T(8,128)(2,1)}, u32[]{:S(2)}, u32[]{:S(2)}) collective-permute-start(bf16[256,1536]{1,0:T(8,128)(2,1)} %get-tuple-element.45), channel_id=1, source_target_pairs={{0,32},{2,34},{4,36},{6,38},{8,40},{10,42},{12,44},{14,46},{16,48}... | collective-permute-start | bytes 2359304 | tf_op jit(solution)/shard_map/ppermute | solution.py:21
  61.9 21.6 %collective-permute-start.11 = (bf16[512,768]{1,0:T(8,128)(2,1)}, bf16[512,768]{1,0:T(8,128)(2,1)S(1)}, u32[]{:S(2)}, u32[]{:S(2)}) collective-permute-start(bf16[512,768]{1,0:T(8,128)(2,1)} %get-tuple-element.49), channel_id=1, source_target_pairs={{0,68},{2,70},{4,64},{6,66},{8,76},{10,78},{12,72},{14,74},{16,84}... | collective-permute-start | bytes 2359304 | tf_op jit(solution)/shard_map/ppermute | solution.py:34
  63.7 20.3 %collective-permute-start.12 = (bf16[512,768]{1,0:T(8,128)(2,1)}, bf16[512,768]{1,0:T(8,128)(2,1)S(1)}, u32[]{:S(2)}, u32[]{:S(2)}) collective-permute-start(bf16[512,768]{1,0:T(8,128)(2,1)} %get-tuple-element.50), channel_id=1, source_target_pairs={{0,72},{2,74},{8,80},{10,82},{12,68},{14,70},{16,88},{18,90},{20,7... | collective-permute-start | bytes 2359304 | tf_op jit(solution)/shard_map/ppermute | solution.py:34
  66.2 17.8 %collective-permute-start.10 = (bf16[512,768]{1,0:T(8,128)(2,1)}, bf16[512,768]{1,0:T(8,128)(2,1)S(1)}, u32[]{:S(2)}, u32[]{:S(2)}) collective-permute-start(bf16[512,768]{1,0:T(8,128)(2,1)} %get-tuple-element.48), channel_id=1, source_target_pairs={{0,64},{64,0},{1,65},{65,1},{2,66},{66,2},{3,67},{67,3},{4,68},{68... | collective-permute-start | bytes 2359304 | tf_op jit(solution)/shard_map/ppermute | solution.py:21
  84.3 27.0 %copy-start.6 = (bf16[256,768]{1,0:T(8,128)(2,1)S(1)}, bf16[256,768]{1,0:T(8,128)(2,1)}, u32[]{:S(2)}) copy-start(bf16[256,768]{1,0:T(8,128)(2,1)} %get-tuple-element.56) | copy-start | bytes 1179652
  84.3 12.1 %collective-permute-start.15 = (bf16[256,768]{1,0:T(8,128)(2,1)S(1)}, bf16[256,768]{1,0:T(8,128)(2,1)S(1)}, u32[]{:S(2)}, u32[]{:S(2)}) collective-permute-start(bf16[256,768]{1,0:T(8,128)(2,1)S(1)} %slice.36), channel_id=1, source_target_pairs={{0,2},{2,0},{4,6},{6,4},{8,10},{10,8},{12,14},{14,12},{16,18},{18,... | collective-permute-start | bytes 1179656 | tf_op jit(solution)/shard_map/ppermute | solution.py:21
  84.7 12.6 %collective-permute-start.16 = (bf16[256,768]{1,0:T(8,128)(2,1)S(1)}, bf16[256,768]{1,0:T(8,128)(2,1)S(1)}, u32[]{:S(2)}, u32[]{:S(2)}) collective-permute-start(bf16[256,768]{1,0:T(8,128)(2,1)S(1)} %copy-done.7), channel_id=1, source_target_pairs={{0,6},{2,4},{4,2},{6,0},{8,14},{10,12},{12,10},{14,8},{16,22},{18,... | collective-permute-start | bytes 1179656 | tf_op jit(solution)/shard_map/ppermute | solution.py:21
  87.4 26.7 %collective-permute-start.13 = (bf16[256,1536]{1,0:T(8,128)(2,1)}, bf16[256,1536]{1,0:T(8,128)(2,1)S(1)}, u32[]{:S(2)}, u32[]{:S(2)}) collective-permute-start(bf16[256,1536]{1,0:T(8,128)(2,1)} %collective-permute-done.9.own_z), channel_id=1, source_target_pairs={{0,2},{2,0},{4,6},{6,4},{8,10},{10,8},{12,14},{14,12},{16,18},{18,... | collective-permute-start | bytes 2359304 | tf_op jit(solution)/shard_map/ppermute | solution.py:21
  88.7 25.3 %collective-permute-start.14 = (bf16[512,768]{1,0:T(8,128)(2,1)S(1)}, bf16[512,768]{1,0:T(8,128)(2,1)S(1)}, u32[]{:S(2)}, u32[]{:S(2)}) collective-permute-start(bf16[512,768]{1,0:T(8,128)(2,1)S(1)} %add_convert_fusion.1.grad), channel_id=1, source_target_pairs={{0,32},{2,34},{4,36},{6,38},{8,40},{10,42},{12,44},{14,46},{16,48}... | collective-permute-start | bytes 2359304 | tf_op jit(solution)/shard_map/ppermute | solution.py:21
  107.6 16.0 %collective-permute-start.17 = (bf16[256,1024]{1,0:T(8,128)(2,1)S(1)}, bf16[256,1024]{1,0:T(8,128)(2,1)}, u32[]{:S(2)}, u32[]{:S(2)}) collective-permute-start(bf16[256,1024]{1,0:T(8,128)(2,1)S(1)} %slice.37), channel_id=1, source_target_pairs={{0,1},{1,0},{2,3},{3,2},{4,5},{5,4},{6,7},{7,6},{8,9},{9,8},{10,11... | collective-permute-start | bytes 1572872 | tf_op jit(solution)/shard_map/ppermute | solution.py:21
  111.3 12.3 %collective-permute-start.18 = (bf16[256,768]{1,0:T(8,128)(2,1)S(1)}, bf16[256,768]{1,0:T(8,128)(2,1)S(1)}, u32[]{:S(2)}, u32[]{:S(2)}) collective-permute-start(bf16[256,768]{1,0:T(8,128)(2,1)S(1)} %copy-done.6), channel_id=1, source_target_pairs={{0,4},{2,6},{4,0},{6,2},{8,12},{10,14},{12,8},{14,10},{16,20},{18,... | collective-permute-start | bytes 1179656 | tf_op jit(solution)/shard_map/ppermute | solution.py:21
  124.3 39.6 %all-to-all-start = ((bf16[16,96,768]{2,1,0:T(8,128)(2,1)}), bf16[16,96,768]{2,1,0:T(8,128)(2,1)}, u32[]{:S(2)}, u32[]{:S(2)}) async-start(bf16[16,96,768]{2,1,0:T(8,128)(2,1)} %bitcast.31), calls=%async_computation | async-start | bytes 4718592 | tf_op jit(solution)/shard_map/all_to_all | solution.py:391
  130.7 25.4 %collective-permute-start.19 = (bf16[256,2048]{1,0:T(8,128)(2,1)S(1)}, bf16[256,2048]{1,0:T(8,128)(2,1)S(1)}, u32[]{:S(2)}, u32[]{:S(2)}) collective-permute-start(bf16[256,2048]{1,0:T(8,128)(2,1)S(1)} %slice.38), channel_id=1, source_target_pairs={{0,1},{1,0},{2,3},{3,2},{4,5},{5,4},{6,7},{7,6},{8,9},{9,8},{10,11... | collective-permute-start | bytes 3145736 | tf_op jit(solution)/shard_map/ppermute | solution.py:21
  (5 other events, 35.5 us)

commit v6 on v5

--- a/solution.py
+++ b/solution.py
@@ -154,7 +154,7 @@
         scratch[pl.ds(pl.multiple_of((1 - member) * rows, rows), rows), :] = other[...]
     span = 2 * REACH + 1
     block = lambda v, j: v[j * rows : (j + 1) * rows]
-    products = []
+    products, halves = [], []
     for i in range(PAIR):
         shard = slice(i * rows, (i + 1) * rows)
         window = slice(i * rows, (i + span) * rows)
@@ -185,8 +185,10 @@
         probs = jnp.concatenate(expo, axis=0) * (1.0 / norm)
         rounded = probs.astype(BF16)
         delta = jnp.sum(dprobs * probs, axis=0, keepdims=True)
+        out = dot(values, rounded, ((0,), (0,)))
+        halves.append((keys, probs, rounded, dprobs, delta, out))
+    for keys, probs, rounded, dprobs, delta, out in halves:
         dscores = (probs * (dprobs - delta)).astype(BF16)
-        out = dot(values, rounded, ((0,), (0,)))
         dq = dot(keys, dscores, ((0,), (0,))) * scale
         terms.append((dscores, rounded))
         results.append([value.T.astype(BF16) for value in (out, dq)])

time: 167 us -> 167 us (level)
  transfers between devices with their start and end apart: 21 -> 21, of which waited for: 9 -> 10; matrix products, arithmetic and copies ran while one was open for 4% -> 4% of each run, Pallas kernels for 25% -> 25%
where the time goes in v6:
time: 167 us; the launch traced here: 166 us
  waiting for transfers between devices  68 us (41%)
  Pallas kernels  43.4 us (26%)
  starting transfers between devices  42.3 us (25%)
  local copies, waits for them, and re-layouts  6.17 us (4%)
  other arithmetic  5.51 us (3%)
    ppermute x13, waiting for transfers between devices, moved(): return lax.ppermute(value, axis, pairs)  31.9 us
    ppermute x7, waiting for transfers between devices, moved_across(): return lax.ppermute(value, ('tower', 'seq'), both)  30 us
    ppermute x13, starting transfers between devices, moved(): return lax.ppermute(value, axis, pairs)  20.3 us
    ppermute x7, starting transfers between devices, moved_across(): return lax.ppermute(value, ('tower', 'seq'), both)  15.7 us
    pallas_call x2, Pallas kernels, projection(): pl.pallas_call(projection_kernel, out_shape=jax.ShapeDtypeStruct((rows, 2...  14.5 us
    pallas_call x1, Pallas kernels, attention(): pl.pallas_call(attention_kernel, out_shape=[shape] * 2 + [pair_shape] * 3...  12.3 us
    pallas_call x1, Pallas kernels, context_partial(): pl.pallas_call(context_kernel, out_shape=jax.ShapeDtypeStruct((rows, widt...  10.3 us
    all_to_all x1, starting transfers between devices, local(): lax.all_to_all(partial_w.reshape(plane, -1, columns), 'seq', 0, 0, axis_i...  6.28 us
  transfers between devices with their start and end apart: 21, of which 10 were waited for; matrix products, arithmetic and copies ran while one was open for 4% of the time, Pallas kernels for 25%

profile of v6, /device:TPU:0, one launch (start us, length us, event | category | flops | bytes accessed | tf_op | source)
XLA Modules:
  0.0 166.3 jit_solution(17364883248746476689)
XLA Ops:
  2.7 2.9 %collective-permute-start.1 = (bf16[272,768]{1,0:T(8,128)(2,1)S(1)}, bf16[272,768]{1,0:T(8,128)(2,1)S(1)}, u32[]{:S(2)}, u32[]{:S(2)}) collective-permute-start(bf16[272,768]{1,0:T(8,128)(2,1)S(1)} %get-tuple-element.74), channel_id=1, source_target_pairs={{0,6},{2,4},{4,2},{6,0},{8,14},{10,12},{12,10},{14,8},{16,22},{18,... | collective-permute-start | bytes 1253384 | tf_op jit(solution)/shard_map/ppermute | solution.py:21
  6.5 7.2 %projection.2 = bf16[256,768]{1,0:T(8,128)(2,1)} custom-call(s32[1]{0:T(128)} %bitcast.4.which, bf16[256,3072]{1,0:T(8,128)(2,1)} %bitcast.35, bf16[3072,2,768]{2,1,0:T(2,128)(2,1)} %bitcast.32), custom_call_target="tpu_custom_call" | custom-call | flops 1207959552 | bytes 20971520 | tf_op jit(solution)/shard_map/projection/pallas_call | solution.py:119
  14.9 5.4 %collective-permute-start.5 = (bf16[256,768]{1,0:T(8,128)(2,1)}, bf16[256,768]{1,0:T(8,128)(2,1)}, u32[]{:S(2)}, u32[]{:S(2)}) collective-permute-start(bf16[256,768]{1,0:T(8,128)(2,1)} %projection.2), channel_id=1, source_target_pairs={{0,70},{2,68},{4,66},{6,64},{8,78},{10,76},{12,74},{14,72},{16,86}... | collective-permute-start | bytes 1179656 | tf_op jit(solution)/shard_map/ppermute | solution.py:34
  20.4 7.3 %projection.3 = bf16[256,768]{1,0:T(8,128)(2,1)} custom-call(s32[1]{0:T(128)} %bitcast.1.which.member, bf16[256,3072]{1,0:T(8,128)(2,1)} %bitcast.36, bf16[3072,2,768]{2,1,0:T(2,128)(2,1)} %bitcast.33), custom_call_target="tpu_custom_call" | custom-call | flops 1207959552 | bytes 20971520 | tf_op jit(solution)/shard_map/projection/pallas_call | solution.py:119
  29.0 3.5 %collective-permute-start.4 = (bf16[256,768]{1,0:T(8,128)(2,1)}, bf16[256,768]{1,0:T(8,128)(2,1)}, u32[]{:S(2)}, u32[]{:S(2)}) collective-permute-start(bf16[256,768]{1,0:T(8,128)(2,1)} %projection.3), channel_id=1, source_target_pairs={{0,68},{2,70},{4,64},{6,66},{8,76},{10,78},{12,72},{14,74},{16,84}... | collective-permute-start | bytes 1179656 | tf_op jit(solution)/shard_map/ppermute | solution.py:34
  33.6 7.3 %collective-permute-done.6.refs_4_ = bf16[256,768]{1,0:T(8,128)(2,1)} collective-permute-done((bf16[256,768]{1,0:T(8,128)(2,1)}, bf16[256,768]{1,0:T(8,128)(2,1)}, u32[]{:S(2)}, u32[]{:S(2)}) %collective-permute-start.6) | collective-permute-done | bytes 393248 | tf_op jit(solution)/shard_map/ppermute | solution.py:34
  40.9 5.3 %collective-permute-done.4.refs_2_ = bf16[256,768]{1,0:T(8,128)(2,1)} collective-permute-done((bf16[256,768]{1,0:T(8,128)(2,1)}, bf16[256,768]{1,0:T(8,128)(2,1)}, u32[]{:S(2)}, u32[]{:S(2)}) %collective-permute-start.4) | collective-permute-done | bytes 393248 | tf_op jit(solution)/shard_map/ppermute | solution.py:34
  46.7 1.9 %collective-permute-start.9 = (bf16[256,1536]{1,0:T(8,128)(2,1)}, bf16[256,1536]{1,0:T(8,128)(2,1)}, u32[]{:S(2)}, u32[]{:S(2)}) collective-permute-start(bf16[256,1536]{1,0:T(8,128)(2,1)} %get-tuple-element.45), channel_id=1, source_target_pairs={{0,32},{2,34},{4,36},{6,38},{8,40},{10,42},{12,44},{14,46},{16,48}... | collective-permute-start | bytes 2359304 | tf_op jit(solution)/shard_map/ppermute | solution.py:21
  49.3 12.3 %attention.1 = (bf16[256,768]{1,0:T(8,128)(2,1)}, bf16[256,768]{1,0:T(8,128)(2,1)}, bf16[512,768]{1,0:T(8,128)(2,1)}, bf16[512,768]{1,0:T(8,128)(2,1)}, bf16[512,768]{1,0:T(8,128)(2,1)}) custom-call(s32[7]{0:T(128)} %concatenate.28.meta, bf16[272,768]{1,0:T(8,128)(2,1)} %copy-done.5, bf16[272,768]{1,0:T(8,128)(2,1)} %copy-done.5, ...), custom_call_target="tpu_custom_call" | custom-call | flops 2516582400 | bytes 8388608 | tf_op jit(solution)/shard_map/attention/pallas_call | solution.py:228
  61.7 1.7 %collective-permute-start.11 = (bf16[512,768]{1,0:T(8,128)(2,1)}, bf16[512,768]{1,0:T(8,128)(2,1)S(1)}, u32[]{:S(2)}, u32[]{:S(2)}) collective-permute-start(bf16[512,768]{1,0:T(8,128)(2,1)} %get-tuple-element.49), channel_id=1, source_target_pairs={{0,68},{2,70},{4,64},{6,66},{8,76},{10,78},{12,72},{14,74},{16,84}... | collective-permute-start | bytes 2359304 | tf_op jit(solution)/shard_map/ppermute | solution.py:34
  63.4 2.5 %collective-permute-start.12 = (bf16[512,768]{1,0:T(8,128)(2,1)}, bf16[512,768]{1,0:T(8,128)(2,1)S(1)}, u32[]{:S(2)}, u32[]{:S(2)}) collective-permute-start(bf16[512,768]{1,0:T(8,128)(2,1)} %get-tuple-element.50), channel_id=1, source_target_pairs={{0,72},{2,74},{8,80},{10,82},{12,68},{14,70},{16,88},{18,90},{20,7... | collective-permute-start | bytes 2359304 | tf_op jit(solution)/shard_map/ppermute | solution.py:34
  66.3 17.0 %collective-permute-done.11 = bf16[512,768]{1,0:T(8,128)(2,1)S(1)} collective-permute-done((bf16[512,768]{1,0:T(8,128)(2,1)}, bf16[512,768]{1,0:T(8,128)(2,1)S(1)}, u32[]{:S(2)}, u32[]{:S(2)}) %collective-permute-start.11) | collective-permute-done | bytes 786464 | tf_op jit(solution)/shard_map/ppermute | solution.py:34
  84.4 2.8 %collective-permute-start.16 = (bf16[256,768]{1,0:T(8,128)(2,1)S(1)}, bf16[256,768]{1,0:T(8,128)(2,1)S(1)}, u32[]{:S(2)}, u32[]{:S(2)}) collective-permute-start(bf16[256,768]{1,0:T(8,128)(2,1)S(1)} %copy-done.7), channel_id=1, source_target_pairs={{0,6},{2,4},{4,2},{6,0},{8,14},{10,12},{12,10},{14,8},{16,22},{18,... | collective-permute-start | bytes 1179656 | tf_op jit(solution)/shard_map/ppermute | solution.py:21
  88.8 7.3 %collective-permute-done.15.grad_next = bf16[256,768]{1,0:T(8,128)(2,1)S(1)} collective-permute-done((bf16[256,768]{1,0:T(8,128)(2,1)S(1)}, bf16[256,768]{1,0:T(8,128)(2,1)S(1)}, u32[]{:S(2)}, u32[]{:S(2)}) %collective-permute-start.15) | collective-permute-done | bytes 393248 | tf_op jit(solution)/shard_map/ppermute | solution.py:21
  97.0 10.3 %context_partial.1 = bf16[256,3072]{1,0:T(8,128)(2,1)S(1)} custom-call(s32[1]{0:T(128)} %bitcast.1.which.member, bf16[512,768]{1,0:T(8,128)(2,1)S(1)} %add_convert_fusion.1.grad, bf16[256,768]{1,0:T(8,128)(2,1)S(1)} %collective-permute-done.15.grad_next, bf16[3072,2,768]{2,1,0:T(2,128)(2,1)} %bitcast.34), custom_call_target="tpu_custom_call" | custom-call | flops 2415919104 | bytes 12582912 | tf_op jit(solution)/shard_map/context_partial/pallas_call | solution.py:296
  107.3 3.7 %collective-permute-start.17 = (bf16[256,1024]{1,0:T(8,128)(2,1)S(1)}, bf16[256,1024]{1,0:T(8,128)(2,1)}, u32[]{:S(2)}, u32[]{:S(2)}) collective-permute-start(bf16[256,1024]{1,0:T(8,128)(2,1)S(1)} %slice.37), channel_id=1, source_target_pairs={{0,1},{1,0},{2,3},{3,2},{4,5},{5,4},{6,7},{7,6},{8,9},{9,8},{10,11... | collective-permute-start | bytes 1572872 | tf_op jit(solution)/shard_map/ppermute | solution.py:21
  111.0 2.8 %collective-permute-start.18 = (bf16[256,768]{1,0:T(8,128)(2,1)S(1)}, bf16[256,768]{1,0:T(8,128)(2,1)S(1)}, u32[]{:S(2)}, u32[]{:S(2)}) collective-permute-start(bf16[256,768]{1,0:T(8,128)(2,1)S(1)} %copy-done.6), channel_id=1, source_target_pairs={{0,4},{2,6},{4,0},{6,2},{8,12},{10,14},{12,8},{14,10},{16,20},{18,... | collective-permute-start | bytes 1179656 | tf_op jit(solution)/shard_map/ppermute | solution.py:21
  113.8 4.5 %weight_partial.1 = bf16[1536,768]{1,0:T(8,128)(2,1)S(1)} custom-call(bf16[256,1536]{1,0:T(8,128)(2,1)S(1)} %get-tuple-element.44.own, bf16[256,1536]{1,0:T(8,128)(2,1)} %collective-permute-done.9.own_z, bf16[256,1536]{1,0:T(8,128)(2,1)S(1)} %collective-permute-done.8.pair, bf16[256,1536]{1,0:T(8,128)(2,1)S(1)} %collective-permute-done.13.pair_z, ...), custom_call_target="tpu_custom_call" | custom-call | flops 2415919104 | bytes 8388608 | tf_op jit(solution)/shard_map/weight_partial/pallas_call | solution.py:265
  119.7 3.6 %collective-permute-done.18 = bf16[256,768]{1,0:T(8,128)(2,1)S(1)} collective-permute-done((bf16[256,768]{1,0:T(8,128)(2,1)S(1)}, bf16[256,768]{1,0:T(8,128)(2,1)S(1)}, u32[]{:S(2)}, u32[]{:S(2)}) %collective-permute-start.18) | collective-permute-done | bytes 393248 | tf_op jit(solution)/shard_map/ppermute | solution.py:21
  124.1 6.3 %all-to-all-start = ((bf16[16,96,768]{2,1,0:T(8,128)(2,1)}), bf16[16,96,768]{2,1,0:T(8,128)(2,1)}, u32[]{:S(2)}, u32[]{:S(2)}) async-start(bf16[16,96,768]{2,1,0:T(8,128)(2,1)} %bitcast.31), calls=%async_computation | async-start | bytes 4718592 | tf_op jit(solution)/shard_map/all_to_all | solution.py:393
  130.5 2.5 %collective-permute-start.19 = (bf16[256,2048]{1,0:T(8,128)(2,1)S(1)}, bf16[256,2048]{1,0:T(8,128)(2,1)S(1)}, u32[]{:S(2)}, u32[]{:S(2)}) collective-permute-start(bf16[256,2048]{1,0:T(8,128)(2,1)S(1)} %slice.38), channel_id=1, source_target_pairs={{0,1},{1,0},{2,3},{3,2},{4,5},{5,4},{6,7},{7,6},{8,9},{9,8},{10,11... | collective-permute-start | bytes 3145736 | tf_op jit(solution)/shard_map/ppermute | solution.py:21
  135.9 20.0 %collective-permute-done.19 = bf16[256,2048]{1,0:T(8,128)(2,1)S(1)} collective-permute-done((bf16[256,2048]{1,0:T(8,128)(2,1)S(1)}, bf16[256,2048]{1,0:T(8,128)(2,1)S(1)}, u32[]{:S(2)}, u32[]{:S(2)}) %collective-permute-start.19) | collective-permute-done | bytes 1048608 | tf_op jit(solution)/shard_map/ppermute | solution.py:21
  157.5 6.2 %all-to-all-done.parts = bf16[16,96,768]{2,1,0:T(8,128)(2,1)} async-done(((bf16[16,96,768]{2,1,0:T(8,128)(2,1)}), bf16[16,96,768]{2,1,0:T(8,128)(2,1)}, u32[]{:S(2)}, u32[]{:S(2)}) %all-to-all-start) | async-done | bytes 2359328 | tf_op jit(solution)/shard_map/all_to_all | solution.py:393
  163.7 1.8 %weight_total.1 = bf16[96,1536]{1,0:T(8,128)(2,1)S(1)} custom-call(bf16[16,96,768]{2,1,0:T(8,128)(2,1)} %all-to-all-done.parts), custom_call_target="tpu_custom_call" | custom-call | tf_op jit(solution)/shard_map/weight_total/pallas_call | solution.py:79
  (59 shorter events, 19.4 us)
Async XLA Ops:
  2.7 24.9 %collective-permute-start.1 = (bf16[272,768]{1,0:T(8,128)(2,1)S(1)}, bf16[272,768]{1,0:T(8,128)(2,1)S(1)}, u32[]{:S(2)}, u32[]{:S(2)}) collective-permute-start(bf16[272,768]{1,0:T(8,128)(2,1)S(1)} %get-tuple-element.74), channel_id=1, source_target_pairs={{0,6},{2,4},{4,2},{6,0},{8,14},{10,12},{12,10},{14,8},{16,22},{18,... | collective-permute-start | bytes 1253384 | tf_op jit(solution)/shard_map/ppermute | solution.py:21
  5.7 22.0 %collective-permute-start = (bf16[272,768]{1,0:T(8,128)(2,1)S(1)}, bf16[272,768]{1,0:T(8,128)(2,1)S(1)}, u32[]{:S(2)}, u32[]{:S(2)}) collective-permute-start(bf16[272,768]{1,0:T(8,128)(2,1)S(1)} %get-tuple-element.75), channel_id=1, source_target_pairs={{0,4},{2,6},{4,0},{6,2},{8,12},{10,14},{12,8},{14,10},{16,20},{18,... | collective-permute-start | bytes 1253384 | tf_op jit(solution)/shard_map/ppermute | solution.py:21
  13.7 18.9 %collective-permute-start.7 = (bf16[256,768]{1,0:T(8,128)(2,1)}, bf16[256,768]{1,0:T(8,128)(2,1)}, u32[]{:S(2)}, u32[]{:S(2)}) collective-permute-start(bf16[256,768]{1,0:T(8,128)(2,1)} %projection.2), channel_id=1, source_target_pairs={{4,78},{6,76},{8,66},{10,64},{12,86},{14,84},{16,74},{18,72},{20,9... | collective-permute-start | bytes 1179656 | tf_op jit(solution)/shard_map/ppermute | solution.py:34
  14.9 18.6 %collective-permute-start.5 = (bf16[256,768]{1,0:T(8,128)(2,1)}, bf16[256,768]{1,0:T(8,128)(2,1)}, u32[]{:S(2)}, u32[]{:S(2)}) collective-permute-start(bf16[256,768]{1,0:T(8,128)(2,1)} %projection.2), channel_id=1, source_target_pairs={{0,70},{2,68},{4,66},{6,64},{8,78},{10,76},{12,74},{14,72},{16,86}... | collective-permute-start | bytes 1179656 | tf_op jit(solution)/shard_map/ppermute | solution.py:34
  20.4 13.2 %collective-permute-start.3 = (bf16[256,768]{1,0:T(8,128)(2,1)}, bf16[256,768]{1,0:T(8,128)(2,1)}, u32[]{:S(2)}, u32[]{:S(2)}) collective-permute-start(bf16[256,768]{1,0:T(8,128)(2,1)} %projection.2), channel_id=1, source_target_pairs={{0,66},{2,64},{4,70},{6,68},{8,74},{10,72},{12,78},{14,76},{16,82}... | collective-permute-start | bytes 1179656 | tf_op jit(solution)/shard_map/ppermute | solution.py:34
  27.7 21.0 %copy-start.4 = (bf16[272,768]{1,0:T(8,128)(2,1)}, bf16[272,768]{1,0:T(8,128)(2,1)S(1)}, u32[]{:S(2)}) copy-start(bf16[272,768]{1,0:T(8,128)(2,1)S(1)} %collective-permute-done.1.q_b.c_b) | copy-start | bytes 1253380
  27.7 21.0 %copy-start.5 = (bf16[272,768]{1,0:T(8,128)(2,1)}, bf16[272,768]{1,0:T(8,128)(2,1)S(1)}, u32[]{:S(2)}) copy-start(bf16[272,768]{1,0:T(8,128)(2,1)S(1)} %collective-permute-done.q_a.c_a) | copy-start | bytes 1253380
  27.7 13.2 %collective-permute-start.6 = (bf16[256,768]{1,0:T(8,128)(2,1)}, bf16[256,768]{1,0:T(8,128)(2,1)}, u32[]{:S(2)}, u32[]{:S(2)}) collective-permute-start(bf16[256,768]{1,0:T(8,128)(2,1)} %projection.3), channel_id=1, source_target_pairs={{4,76},{6,78},{8,64},{10,66},{12,84},{14,86},{16,72},{18,74},{20,9... | collective-permute-start | bytes 1179656 | tf_op jit(solution)/shard_map/ppermute | solution.py:34
  29.0 17.1 %collective-permute-start.4 = (bf16[256,768]{1,0:T(8,128)(2,1)}, bf16[256,768]{1,0:T(8,128)(2,1)}, u32[]{:S(2)}, u32[]{:S(2)}) collective-permute-start(bf16[256,768]{1,0:T(8,128)(2,1)} %projection.3), channel_id=1, source_target_pairs={{0,68},{2,70},{4,64},{6,66},{8,76},{10,78},{12,72},{14,74},{16,84}... | collective-permute-start | bytes 1179656 | tf_op jit(solution)/shard_map/ppermute | solution.py:34
  32.5 13.6 %collective-permute-start.2 = (bf16[256,768]{1,0:T(8,128)(2,1)}, bf16[256,768]{1,0:T(8,128)(2,1)}, u32[]{:S(2)}, u32[]{:S(2)}) collective-permute-start(bf16[256,768]{1,0:T(8,128)(2,1)} %projection.3), channel_id=1, source_target_pairs={{0,64},{64,0},{1,65},{65,1},{2,66},{66,2},{3,67},{67,3},{4,68},{68... | collective-permute-start | bytes 1179656 | tf_op jit(solution)/shard_map/ppermute | solution.py:21
  46.1 19.8 %collective-permute-start.8 = (bf16[256,1536]{1,0:T(8,128)(2,1)S(1)}, bf16[256,1536]{1,0:T(8,128)(2,1)S(1)}, u32[]{:S(2)}, u32[]{:S(2)}) collective-permute-start(bf16[256,1536]{1,0:T(8,128)(2,1)S(1)} %get-tuple-element.44.own), channel_id=1, source_target_pairs={{0,2},{2,0},{4,6},{6,4},{8,10},{10,8},{12,14},{14,12},{16,18},{18,... | collective-permute-start | bytes 2359304 | tf_op jit(solution)/shard_map/ppermute | solution.py:21
  46.7 19.3 %collective-permute-start.9 = (bf16[256,1536]{1,0:T(8,128)(2,1)}, bf16[256,1536]{1,0:T(8,128)(2,1)}, u32[]{:S(2)}, u32[]{:S(2)}) collective-permute-start(bf16[256,1536]{1,0:T(8,128)(2,1)} %get-tuple-element.45), channel_id=1, source_target_pairs={{0,32},{2,34},{4,36},{6,38},{8,40},{10,42},{12,44},{14,46},{16,48}... | collective-permute-start | bytes 2359304 | tf_op jit(solution)/shard_map/ppermute | solution.py:21
  61.7 21.6 %collective-permute-start.11 = (bf16[512,768]{1,0:T(8,128)(2,1)}, bf16[512,768]{1,0:T(8,128)(2,1)S(1)}, u32[]{:S(2)}, u32[]{:S(2)}) collective-permute-start(bf16[512,768]{1,0:T(8,128)(2,1)} %get-tuple-element.49), channel_id=1, source_target_pairs={{0,68},{2,70},{4,64},{6,66},{8,76},{10,78},{12,72},{14,74},{16,84}... | collective-permute-start | bytes 2359304 | tf_op jit(solution)/shard_map/ppermute | solution.py:34
  63.4 20.3 %collective-permute-start.12 = (bf16[512,768]{1,0:T(8,128)(2,1)}, bf16[512,768]{1,0:T(8,128)(2,1)S(1)}, u32[]{:S(2)}, u32[]{:S(2)}) collective-permute-start(bf16[512,768]{1,0:T(8,128)(2,1)} %get-tuple-element.50), channel_id=1, source_target_pairs={{0,72},{2,74},{8,80},{10,82},{12,68},{14,70},{16,88},{18,90},{20,7... | collective-permute-start | bytes 2359304 | tf_op jit(solution)/shard_map/ppermute | solution.py:34
  66.0 17.7 %collective-permute-start.10 = (bf16[512,768]{1,0:T(8,128)(2,1)}, bf16[512,768]{1,0:T(8,128)(2,1)S(1)}, u32[]{:S(2)}, u32[]{:S(2)}) collective-permute-start(bf16[512,768]{1,0:T(8,128)(2,1)} %get-tuple-element.48), channel_id=1, source_target_pairs={{0,64},{64,0},{1,65},{65,1},{2,66},{66,2},{3,67},{67,3},{4,68},{68... | collective-permute-start | bytes 2359304 | tf_op jit(solution)/shard_map/ppermute | solution.py:21
  84.0 27.0 %copy-start.6 = (bf16[256,768]{1,0:T(8,128)(2,1)S(1)}, bf16[256,768]{1,0:T(8,128)(2,1)}, u32[]{:S(2)}) copy-start(bf16[256,768]{1,0:T(8,128)(2,1)} %get-tuple-element.56) | copy-start | bytes 1179652
  84.0 12.1 %collective-permute-start.15 = (bf16[256,768]{1,0:T(8,128)(2,1)S(1)}, bf16[256,768]{1,0:T(8,128)(2,1)S(1)}, u32[]{:S(2)}, u32[]{:S(2)}) collective-permute-start(bf16[256,768]{1,0:T(8,128)(2,1)S(1)} %slice.36), channel_id=1, source_target_pairs={{0,2},{2,0},{4,6},{6,4},{8,10},{10,8},{12,14},{14,12},{16,18},{18,... | collective-permute-start | bytes 1179656 | tf_op jit(solution)/shard_map/ppermute | solution.py:21
  84.4 12.6 %collective-permute-start.16 = (bf16[256,768]{1,0:T(8,128)(2,1)S(1)}, bf16[256,768]{1,0:T(8,128)(2,1)S(1)}, u32[]{:S(2)}, u32[]{:S(2)}) collective-permute-start(bf16[256,768]{1,0:T(8,128)(2,1)S(1)} %copy-done.7), channel_id=1, source_target_pairs={{0,6},{2,4},{4,2},{6,0},{8,14},{10,12},{12,10},{14,8},{16,22},{18,... | collective-permute-start | bytes 1179656 | tf_op jit(solution)/shard_map/ppermute | solution.py:21
  87.2 26.7 %collective-permute-start.13 = (bf16[256,1536]{1,0:T(8,128)(2,1)}, bf16[256,1536]{1,0:T(8,128)(2,1)S(1)}, u32[]{:S(2)}, u32[]{:S(2)}) collective-permute-start(bf16[256,1536]{1,0:T(8,128)(2,1)} %collective-permute-done.9.own_z), channel_id=1, source_target_pairs={{0,2},{2,0},{4,6},{6,4},{8,10},{10,8},{12,14},{14,12},{16,18},{18,... | collective-permute-start | bytes 2359304 | tf_op jit(solution)/shard_map/ppermute | solution.py:21
  88.5 25.3 %collective-permute-start.14 = (bf16[512,768]{1,0:T(8,128)(2,1)S(1)}, bf16[512,768]{1,0:T(8,128)(2,1)S(1)}, u32[]{:S(2)}, u32[]{:S(2)}) collective-permute-start(bf16[512,768]{1,0:T(8,128)(2,1)S(1)} %add_convert_fusion.1.grad), channel_id=1, source_target_pairs={{0,32},{2,34},{4,36},{6,38},{8,40},{10,42},{12,44},{14,46},{16,48}... | collective-permute-start | bytes 2359304 | tf_op jit(solution)/shard_map/ppermute | solution.py:21
  107.3 16.0 %collective-permute-start.17 = (bf16[256,1024]{1,0:T(8,128)(2,1)S(1)}, bf16[256,1024]{1,0:T(8,128)(2,1)}, u32[]{:S(2)}, u32[]{:S(2)}) collective-permute-start(bf16[256,1024]{1,0:T(8,128)(2,1)S(1)} %slice.37), channel_id=1, source_target_pairs={{0,1},{1,0},{2,3},{3,2},{4,5},{5,4},{6,7},{7,6},{8,9},{9,8},{10,11... | collective-permute-start | bytes 1572872 | tf_op jit(solution)/shard_map/ppermute | solution.py:21
  111.0 12.3 %collective-permute-start.18 = (bf16[256,768]{1,0:T(8,128)(2,1)S(1)}, bf16[256,768]{1,0:T(8,128)(2,1)S(1)}, u32[]{:S(2)}, u32[]{:S(2)}) collective-permute-start(bf16[256,768]{1,0:T(8,128)(2,1)S(1)} %copy-done.6), channel_id=1, source_target_pairs={{0,4},{2,6},{4,0},{6,2},{8,12},{10,14},{12,8},{14,10},{16,20},{18,... | collective-permute-start | bytes 1179656 | tf_op jit(solution)/shard_map/ppermute | solution.py:21
  124.1 39.6 %all-to-all-start = ((bf16[16,96,768]{2,1,0:T(8,128)(2,1)}), bf16[16,96,768]{2,1,0:T(8,128)(2,1)}, u32[]{:S(2)}, u32[]{:S(2)}) async-start(bf16[16,96,768]{2,1,0:T(8,128)(2,1)} %bitcast.31), calls=%async_computation | async-start | bytes 4718592 | tf_op jit(solution)/shard_map/all_to_all | solution.py:393
  130.5 25.4 %collective-permute-start.19 = (bf16[256,2048]{1,0:T(8,128)(2,1)S(1)}, bf16[256,2048]{1,0:T(8,128)(2,1)S(1)}, u32[]{:S(2)}, u32[]{:S(2)}) collective-permute-start(bf16[256,2048]{1,0:T(8,128)(2,1)S(1)} %slice.38), channel_id=1, source_target_pairs={{0,1},{1,0},{2,3},{3,2},{4,5},{5,4},{6,7},{7,6},{8,9},{9,8},{10,11... | collective-permute-start | bytes 3145736 | tf_op jit(solution)/shard_map/ppermute | solution.py:21
  (5 other events, 35.4 us)

commit v7 on v6

--- a/solution.py
+++ b/solution.py
@@ -62,6 +62,7 @@
 def total_kernel(parts, out):
     columns = parts.shape[2]
     heads = columns // (2 * HD)
+    sides = ([], [])
     for half in range(PAIR):
         total = parts[half].astype(F32)
         for source in range(half + PAIR, parts.shape[0], PAIR):
@@ -69,8 +70,9 @@
         for h in range(heads):
             for side in range(2):
                 begin = (2 * h + side) * HD
-                place = side * columns + (half * heads + h) * HD
-                out[:, place : place + HD] = total[:, begin : begin + HD].astype(BF16)
+                sides[side].append(total[:, begin : begin + HD].astype(BF16))
+    both = jnp.stack([jnp.concatenate(side, axis=1) for side in sides], axis=0)
+    out[...] = jnp.swapaxes(both, 0, 1)
 
 
 def weight_total(parts):
@@ -78,10 +80,10 @@
     block = rows // 2
     return pl.pallas_call(
         total_kernel,
-        out_shape=jax.ShapeDtypeStruct((rows, 2 * columns), BF16),
+        out_shape=jax.ShapeDtypeStruct((rows, 2, columns), BF16),
         grid=(rows // block,),
         in_specs=[pl.BlockSpec((parts.shape[0], block, columns), lambda i: (0, i, 0))],
-        out_specs=pl.BlockSpec((block, 2 * columns), lambda i: (i, 0)),
+        out_specs=pl.BlockSpec((block, 2, columns), lambda i: (i, 0, 0)),
         compiler_params=pltpu.CompilerParams(vmem_limit_bytes=24 * 2**20),
         name="weight_total",
     )(parts)
@@ -393,7 +395,7 @@
     parts = lax.all_to_all(
         partial_w.reshape(plane, -1, columns), "seq", 0, 0, axis_index_groups=groups
     )
-    weight_grad = weight_total(parts).reshape(-1, 2, columns)[None]
+    weight_grad = weight_total(parts)[None]
 
     context_grad = jnp.concatenate(
         [

time: 167 us -> 167 us (level)
  no operation moved by 1% of the time
where the time goes in v7:
time: 167 us; the launch traced here: 166 us
  waiting for transfers between devices  68 us (41%)
  Pallas kernels  44.2 us (26%)
  starting transfers between devices  42.3 us (25%)
  other arithmetic  5.51 us (3%)
  local copies, waits for them, and re-layouts  5.39 us (3%)
    ppermute x13, waiting for transfers between devices, moved(): return lax.ppermute(value, axis, pairs)  31.9 us
    ppermute x7, waiting for transfers between devices, moved_across(): return lax.ppermute(value, ('tower', 'seq'), both)  30 us
    ppermute x13, starting transfers between devices, moved(): return lax.ppermute(value, axis, pairs)  20.3 us
    ppermute x7, starting transfers between devices, moved_across(): return lax.ppermute(value, ('tower', 'seq'), both)  15.7 us
    pallas_call x2, Pallas kernels, projection(): pl.pallas_call(projection_kernel, out_shape=jax.ShapeDtypeStruct((rows, 2...  14.5 us
    pallas_call x1, Pallas kernels, attention(): pl.pallas_call(attention_kernel, out_shape=[shape] * 2 + [pair_shape] * 3...  12.3 us
    pallas_call x1, Pallas kernels, context_partial(): pl.pallas_call(context_kernel, out_shape=jax.ShapeDtypeStruct((rows, widt...  10.3 us
    all_to_all x1, starting transfers between devices, local(): lax.all_to_all(partial_w.reshape(plane, -1, columns), 'seq', 0, 0, axis_i...  6.28 us
  transfers between devices with their start and end apart: 21, of which 10 were waited for; matrix products, arithmetic and copies ran while one was open for 4% of the time, Pallas kernels for 25%

profile of v7, /device:TPU:0, one launch (start us, length us, event | category | flops | bytes accessed | tf_op | source)
XLA Modules:
  0.0 166.2 jit_solution(4112403856514440256)
XLA Ops:
  2.7 2.9 %collective-permute-start.1 = (bf16[272,768]{1,0:T(8,128)(2,1)S(1)}, bf16[272,768]{1,0:T(8,128)(2,1)S(1)}, u32[]{:S(2)}, u32[]{:S(2)}) collective-permute-start(bf16[272,768]{1,0:T(8,128)(2,1)S(1)} %get-tuple-element.74), channel_id=1, source_target_pairs={{0,6},{2,4},{4,2},{6,0},{8,14},{10,12},{12,10},{14,8},{16,22},{18,... | collective-permute-start | bytes 1253384 | tf_op jit(solution)/shard_map/ppermute | solution.py:21
  6.5 7.2 %projection.2 = bf16[256,768]{1,0:T(8,128)(2,1)} custom-call(s32[1]{0:T(128)} %bitcast.4.which, bf16[256,3072]{1,0:T(8,128)(2,1)} %bitcast.36, bf16[3072,2,768]{2,1,0:T(2,128)(2,1)} %bitcast.33), custom_call_target="tpu_custom_call" | custom-call | flops 1207959552 | bytes 20971520 | tf_op jit(solution)/shard_map/projection/pallas_call | solution.py:121
  14.9 5.4 %collective-permute-start.5 = (bf16[256,768]{1,0:T(8,128)(2,1)}, bf16[256,768]{1,0:T(8,128)(2,1)}, u32[]{:S(2)}, u32[]{:S(2)}) collective-permute-start(bf16[256,768]{1,0:T(8,128)(2,1)} %projection.2), channel_id=1, source_target_pairs={{0,70},{2,68},{4,66},{6,64},{8,78},{10,76},{12,74},{14,72},{16,86}... | collective-permute-start | bytes 1179656 | tf_op jit(solution)/shard_map/ppermute | solution.py:34
  20.4 7.3 %projection.3 = bf16[256,768]{1,0:T(8,128)(2,1)} custom-call(s32[1]{0:T(128)} %bitcast.1.which.member, bf16[256,3072]{1,0:T(8,128)(2,1)} %bitcast.37, bf16[3072,2,768]{2,1,0:T(2,128)(2,1)} %bitcast.34), custom_call_target="tpu_custom_call" | custom-call | flops 1207959552 | bytes 20971520 | tf_op jit(solution)/shard_map/projection/pallas_call | solution.py:121
  29.0 3.5 %collective-permute-start.4 = (bf16[256,768]{1,0:T(8,128)(2,1)}, bf16[256,768]{1,0:T(8,128)(2,1)}, u32[]{:S(2)}, u32[]{:S(2)}) collective-permute-start(bf16[256,768]{1,0:T(8,128)(2,1)} %projection.3), channel_id=1, source_target_pairs={{0,68},{2,70},{4,64},{6,66},{8,76},{10,78},{12,72},{14,74},{16,84}... | collective-permute-start | bytes 1179656 | tf_op jit(solution)/shard_map/ppermute | solution.py:34
  33.6 7.3 %collective-permute-done.6.refs_4_ = bf16[256,768]{1,0:T(8,128)(2,1)} collective-permute-done((bf16[256,768]{1,0:T(8,128)(2,1)}, bf16[256,768]{1,0:T(8,128)(2,1)}, u32[]{:S(2)}, u32[]{:S(2)}) %collective-permute-start.6) | collective-permute-done | bytes 393248 | tf_op jit(solution)/shard_map/ppermute | solution.py:34
  40.9 5.3 %collective-permute-done.4.refs_2_ = bf16[256,768]{1,0:T(8,128)(2,1)} collective-permute-done((bf16[256,768]{1,0:T(8,128)(2,1)}, bf16[256,768]{1,0:T(8,128)(2,1)}, u32[]{:S(2)}, u32[]{:S(2)}) %collective-permute-start.4) | collective-permute-done | bytes 393248 | tf_op jit(solution)/shard_map/ppermute | solution.py:34
  46.7 1.9 %collective-permute-start.9 = (bf16[256,1536]{1,0:T(8,128)(2,1)}, bf16[256,1536]{1,0:T(8,128)(2,1)}, u32[]{:S(2)}, u32[]{:S(2)}) collective-permute-start(bf16[256,1536]{1,0:T(8,128)(2,1)} %get-tuple-element.45), channel_id=1, source_target_pairs={{0,32},{2,34},{4,36},{6,38},{8,40},{10,42},{12,44},{14,46},{16,48}... | collective-permute-start | bytes 2359304 | tf_op jit(solution)/shard_map/ppermute | solution.py:21
  49.3 12.3 %attention.1 = (bf16[256,768]{1,0:T(8,128)(2,1)}, bf16[256,768]{1,0:T(8,128)(2,1)}, bf16[512,768]{1,0:T(8,128)(2,1)}, bf16[512,768]{1,0:T(8,128)(2,1)}, bf16[512,768]{1,0:T(8,128)(2,1)}) custom-call(s32[7]{0:T(128)} %concatenate.28.meta, bf16[272,768]{1,0:T(8,128)(2,1)} %copy-done.5, bf16[272,768]{1,0:T(8,128)(2,1)} %copy-done.5, ...), custom_call_target="tpu_custom_call" | custom-call | flops 2516582400 | bytes 8388608 | tf_op jit(solution)/shard_map/attention/pallas_call | solution.py:230
  61.7 1.7 %collective-permute-start.11 = (bf16[512,768]{1,0:T(8,128)(2,1)}, bf16[512,768]{1,0:T(8,128)(2,1)S(1)}, u32[]{:S(2)}, u32[]{:S(2)}) collective-permute-start(bf16[512,768]{1,0:T(8,128)(2,1)} %get-tuple-element.49), channel_id=1, source_target_pairs={{0,68},{2,70},{4,64},{6,66},{8,76},{10,78},{12,72},{14,74},{16,84}... | collective-permute-start | bytes 2359304 | tf_op jit(solution)/shard_map/ppermute | solution.py:34
  63.4 2.5 %collective-permute-start.12 = (bf16[512,768]{1,0:T(8,128)(2,1)}, bf16[512,768]{1,0:T(8,128)(2,1)S(1)}, u32[]{:S(2)}, u32[]{:S(2)}) collective-permute-start(bf16[512,768]{1,0:T(8,128)(2,1)} %get-tuple-element.50), channel_id=1, source_target_pairs={{0,72},{2,74},{8,80},{10,82},{12,68},{14,70},{16,88},{18,90},{20,7... | collective-permute-start | bytes 2359304 | tf_op jit(solution)/shard_map/ppermute | solution.py:34
  66.3 17.0 %collective-permute-done.11 = bf16[512,768]{1,0:T(8,128)(2,1)S(1)} collective-permute-done((bf16[512,768]{1,0:T(8,128)(2,1)}, bf16[512,768]{1,0:T(8,128)(2,1)S(1)}, u32[]{:S(2)}, u32[]{:S(2)}) %collective-permute-start.11) | collective-permute-done | bytes 786464 | tf_op jit(solution)/shard_map/ppermute | solution.py:34
  84.4 2.8 %collective-permute-start.16 = (bf16[256,768]{1,0:T(8,128)(2,1)S(1)}, bf16[256,768]{1,0:T(8,128)(2,1)S(1)}, u32[]{:S(2)}, u32[]{:S(2)}) collective-permute-start(bf16[256,768]{1,0:T(8,128)(2,1)S(1)} %copy-done.7), channel_id=1, source_target_pairs={{0,6},{2,4},{4,2},{6,0},{8,14},{10,12},{12,10},{14,8},{16,22},{18,... | collective-permute-start | bytes 1179656 | tf_op jit(solution)/shard_map/ppermute | solution.py:21
  88.8 7.3 %collective-permute-done.15.grad_next = bf16[256,768]{1,0:T(8,128)(2,1)S(1)} collective-permute-done((bf16[256,768]{1,0:T(8,128)(2,1)S(1)}, bf16[256,768]{1,0:T(8,128)(2,1)S(1)}, u32[]{:S(2)}, u32[]{:S(2)}) %collective-permute-start.15) | collective-permute-done | bytes 393248 | tf_op jit(solution)/shard_map/ppermute | solution.py:21
  97.0 10.3 %context_partial.1 = bf16[256,3072]{1,0:T(8,128)(2,1)S(1)} custom-call(s32[1]{0:T(128)} %bitcast.1.which.member, bf16[512,768]{1,0:T(8,128)(2,1)S(1)} %add_convert_fusion.1.grad, bf16[256,768]{1,0:T(8,128)(2,1)S(1)} %collective-permute-done.15.grad_next, bf16[3072,2,768]{2,1,0:T(2,128)(2,1)} %bitcast.35), custom_call_target="tpu_custom_call" | custom-call | flops 2415919104 | bytes 12582912 | tf_op jit(solution)/shard_map/context_partial/pallas_call | solution.py:298
  107.3 3.7 %collective-permute-start.17 = (bf16[256,1024]{1,0:T(8,128)(2,1)S(1)}, bf16[256,1024]{1,0:T(8,128)(2,1)}, u32[]{:S(2)}, u32[]{:S(2)}) collective-permute-start(bf16[256,1024]{1,0:T(8,128)(2,1)S(1)} %slice.37), channel_id=1, source_target_pairs={{0,1},{1,0},{2,3},{3,2},{4,5},{5,4},{6,7},{7,6},{8,9},{9,8},{10,11... | collective-permute-start | bytes 1572872 | tf_op jit(solution)/shard_map/ppermute | solution.py:21
  111.0 2.8 %collective-permute-start.18 = (bf16[256,768]{1,0:T(8,128)(2,1)S(1)}, bf16[256,768]{1,0:T(8,128)(2,1)S(1)}, u32[]{:S(2)}, u32[]{:S(2)}) collective-permute-start(bf16[256,768]{1,0:T(8,128)(2,1)S(1)} %copy-done.6), channel_id=1, source_target_pairs={{0,4},{2,6},{4,0},{6,2},{8,12},{10,14},{12,8},{14,10},{16,20},{18,... | collective-permute-start | bytes 1179656 | tf_op jit(solution)/shard_map/ppermute | solution.py:21
  113.8 4.5 %weight_partial.1 = bf16[1536,768]{1,0:T(8,128)(2,1)S(1)} custom-call(bf16[256,1536]{1,0:T(8,128)(2,1)S(1)} %get-tuple-element.44.own, bf16[256,1536]{1,0:T(8,128)(2,1)} %collective-permute-done.9.own_z, bf16[256,1536]{1,0:T(8,128)(2,1)S(1)} %collective-permute-done.8.pair, bf16[256,1536]{1,0:T(8,128)(2,1)S(1)} %collective-permute-done.13.pair_z, ...), custom_call_target="tpu_custom_call" | custom-call | flops 2415919104 | bytes 8388608 | tf_op jit(solution)/shard_map/weight_partial/pallas_call | solution.py:267
  119.7 3.6 %collective-permute-done.18 = bf16[256,768]{1,0:T(8,128)(2,1)S(1)} collective-permute-done((bf16[256,768]{1,0:T(8,128)(2,1)S(1)}, bf16[256,768]{1,0:T(8,128)(2,1)S(1)}, u32[]{:S(2)}, u32[]{:S(2)}) %collective-permute-start.18) | collective-permute-done | bytes 393248 | tf_op jit(solution)/shard_map/ppermute | solution.py:21
  124.1 6.3 %all-to-all-start = ((bf16[16,96,768]{2,1,0:T(8,128)(2,1)}), bf16[16,96,768]{2,1,0:T(8,128)(2,1)}, u32[]{:S(2)}, u32[]{:S(2)}) async-start(bf16[16,96,768]{2,1,0:T(8,128)(2,1)} %bitcast.32), calls=%async_computation | async-start | bytes 4718592 | tf_op jit(solution)/shard_map/all_to_all | solution.py:395
  130.5 2.5 %collective-permute-start.19 = (bf16[256,2048]{1,0:T(8,128)(2,1)S(1)}, bf16[256,2048]{1,0:T(8,128)(2,1)S(1)}, u32[]{:S(2)}, u32[]{:S(2)}) collective-permute-start(bf16[256,2048]{1,0:T(8,128)(2,1)S(1)} %slice.38), channel_id=1, source_target_pairs={{0,1},{1,0},{2,3},{3,2},{4,5},{5,4},{6,7},{7,6},{8,9},{9,8},{10,11... | collective-permute-start | bytes 3145736 | tf_op jit(solution)/shard_map/ppermute | solution.py:21
  135.9 20.0 %collective-permute-done.19 = bf16[256,2048]{1,0:T(8,128)(2,1)S(1)} collective-permute-done((bf16[256,2048]{1,0:T(8,128)(2,1)S(1)}, bf16[256,2048]{1,0:T(8,128)(2,1)S(1)}, u32[]{:S(2)}, u32[]{:S(2)}) %collective-permute-start.19) | collective-permute-done | bytes 1048608 | tf_op jit(solution)/shard_map/ppermute | solution.py:21
  157.5 6.2 %all-to-all-done.parts = bf16[16,96,768]{2,1,0:T(8,128)(2,1)} async-done(((bf16[16,96,768]{2,1,0:T(8,128)(2,1)}), bf16[16,96,768]{2,1,0:T(8,128)(2,1)}, u32[]{:S(2)}, u32[]{:S(2)}) %all-to-all-start) | async-done | bytes 2359328 | tf_op jit(solution)/shard_map/all_to_all | solution.py:395
  163.7 2.6 %weight_total.1 = bf16[96,2,768]{2,1,0:T(2,128)(2,1)} custom-call(bf16[16,96,768]{2,1,0:T(8,128)(2,1)} %all-to-all-done.parts), custom_call_target="tpu_custom_call" | custom-call | tf_op jit(solution)/shard_map/weight_total/pallas_call | solution.py:81
  (58 shorter events, 18.6 us)
Async XLA Ops:
  2.7 24.9 %collective-permute-start.1 = (bf16[272,768]{1,0:T(8,128)(2,1)S(1)}, bf16[272,768]{1,0:T(8,128)(2,1)S(1)}, u32[]{:S(2)}, u32[]{:S(2)}) collective-permute-start(bf16[272,768]{1,0:T(8,128)(2,1)S(1)} %get-tuple-element.74), channel_id=1, source_target_pairs={{0,6},{2,4},{4,2},{6,0},{8,14},{10,12},{12,10},{14,8},{16,22},{18,... | collective-permute-start | bytes 1253384 | tf_op jit(solution)/shard_map/ppermute | solution.py:21
  5.7 22.0 %collective-permute-start = (bf16[272,768]{1,0:T(8,128)(2,1)S(1)}, bf16[272,768]{1,0:T(8,128)(2,1)S(1)}, u32[]{:S(2)}, u32[]{:S(2)}) collective-permute-start(bf16[272,768]{1,0:T(8,128)(2,1)S(1)} %get-tuple-element.75), channel_id=1, source_target_pairs={{0,4},{2,6},{4,0},{6,2},{8,12},{10,14},{12,8},{14,10},{16,20},{18,... | collective-permute-start | bytes 1253384 | tf_op jit(solution)/shard_map/ppermute | solution.py:21
  13.7 18.9 %collective-permute-start.7 = (bf16[256,768]{1,0:T(8,128)(2,1)}, bf16[256,768]{1,0:T(8,128)(2,1)}, u32[]{:S(2)}, u32[]{:S(2)}) collective-permute-start(bf16[256,768]{1,0:T(8,128)(2,1)} %projection.2), channel_id=1, source_target_pairs={{4,78},{6,76},{8,66},{10,64},{12,86},{14,84},{16,74},{18,72},{20,9... | collective-permute-start | bytes 1179656 | tf_op jit(solution)/shard_map/ppermute | solution.py:34
  14.9 18.6 %collective-permute-start.5 = (bf16[256,768]{1,0:T(8,128)(2,1)}, bf16[256,768]{1,0:T(8,128)(2,1)}, u32[]{:S(2)}, u32[]{:S(2)}) collective-permute-start(bf16[256,768]{1,0:T(8,128)(2,1)} %projection.2), channel_id=1, source_target_pairs={{0,70},{2,68},{4,66},{6,64},{8,78},{10,76},{12,74},{14,72},{16,86}... | collective-permute-start | bytes 1179656 | tf_op jit(solution)/shard_map/ppermute | solution.py:34
  20.4 13.2 %collective-permute-start.3 = (bf16[256,768]{1,0:T(8,128)(2,1)}, bf16[256,768]{1,0:T(8,128)(2,1)}, u32[]{:S(2)}, u32[]{:S(2)}) collective-permute-start(bf16[256,768]{1,0:T(8,128)(2,1)} %projection.2), channel_id=1, source_target_pairs={{0,66},{2,64},{4,70},{6,68},{8,74},{10,72},{12,78},{14,76},{16,82}... | collective-permute-start | bytes 1179656 | tf_op jit(solution)/shard_map/ppermute | solution.py:34
  27.7 21.0 %copy-start.4 = (bf16[272,768]{1,0:T(8,128)(2,1)}, bf16[272,768]{1,0:T(8,128)(2,1)S(1)}, u32[]{:S(2)}) copy-start(bf16[272,768]{1,0:T(8,128)(2,1)S(1)} %collective-permute-done.1.q_b.c_b) | copy-start | bytes 1253380
  27.7 21.0 %copy-start.5 = (bf16[272,768]{1,0:T(8,128)(2,1)}, bf16[272,768]{1,0:T(8,128)(2,1)S(1)}, u32[]{:S(2)}) copy-start(bf16[272,768]{1,0:T(8,128)(2,1)S(1)} %collective-permute-done.q_a.c_a) | copy-start | bytes 1253380
  27.7 13.2 %collective-permute-start.6 = (bf16[256,768]{1,0:T(8,128)(2,1)}, bf16[256,768]{1,0:T(8,128)(2,1)}, u32[]{:S(2)}, u32[]{:S(2)}) collective-permute-start(bf16[256,768]{1,0:T(8,128)(2,1)} %projection.3), channel_id=1, source_target_pairs={{4,76},{6,78},{8,64},{10,66},{12,84},{14,86},{16,72},{18,74},{20,9... | collective-permute-start | bytes 1179656 | tf_op jit(solution)/shard_map/ppermute | solution.py:34
  29.0 17.1 %collective-permute-start.4 = (bf16[256,768]{1,0:T(8,128)(2,1)}, bf16[256,768]{1,0:T(8,128)(2,1)}, u32[]{:S(2)}, u32[]{:S(2)}) collective-permute-start(bf16[256,768]{1,0:T(8,128)(2,1)} %projection.3), channel_id=1, source_target_pairs={{0,68},{2,70},{4,64},{6,66},{8,76},{10,78},{12,72},{14,74},{16,84}... | collective-permute-start | bytes 1179656 | tf_op jit(solution)/shard_map/ppermute | solution.py:34
  32.5 13.6 %collective-permute-start.2 = (bf16[256,768]{1,0:T(8,128)(2,1)}, bf16[256,768]{1,0:T(8,128)(2,1)}, u32[]{:S(2)}, u32[]{:S(2)}) collective-permute-start(bf16[256,768]{1,0:T(8,128)(2,1)} %projection.3), channel_id=1, source_target_pairs={{0,64},{64,0},{1,65},{65,1},{2,66},{66,2},{3,67},{67,3},{4,68},{68... | collective-permute-start | bytes 1179656 | tf_op jit(solution)/shard_map/ppermute | solution.py:21
  46.1 19.8 %collective-permute-start.8 = (bf16[256,1536]{1,0:T(8,128)(2,1)S(1)}, bf16[256,1536]{1,0:T(8,128)(2,1)S(1)}, u32[]{:S(2)}, u32[]{:S(2)}) collective-permute-start(bf16[256,1536]{1,0:T(8,128)(2,1)S(1)} %get-tuple-element.44.own), channel_id=1, source_target_pairs={{0,2},{2,0},{4,6},{6,4},{8,10},{10,8},{12,14},{14,12},{16,18},{18,... | collective-permute-start | bytes 2359304 | tf_op jit(solution)/shard_map/ppermute | solution.py:21
  46.7 19.3 %collective-permute-start.9 = (bf16[256,1536]{1,0:T(8,128)(2,1)}, bf16[256,1536]{1,0:T(8,128)(2,1)}, u32[]{:S(2)}, u32[]{:S(2)}) collective-permute-start(bf16[256,1536]{1,0:T(8,128)(2,1)} %get-tuple-element.45), channel_id=1, source_target_pairs={{0,32},{2,34},{4,36},{6,38},{8,40},{10,42},{12,44},{14,46},{16,48}... | collective-permute-start | bytes 2359304 | tf_op jit(solution)/shard_map/ppermute | solution.py:21
  61.7 21.6 %collective-permute-start.11 = (bf16[512,768]{1,0:T(8,128)(2,1)}, bf16[512,768]{1,0:T(8,128)(2,1)S(1)}, u32[]{:S(2)}, u32[]{:S(2)}) collective-permute-start(bf16[512,768]{1,0:T(8,128)(2,1)} %get-tuple-element.49), channel_id=1, source_target_pairs={{0,68},{2,70},{4,64},{6,66},{8,76},{10,78},{12,72},{14,74},{16,84}... | collective-permute-start | bytes 2359304 | tf_op jit(solution)/shard_map/ppermute | solution.py:34
  63.4 20.3 %collective-permute-start.12 = (bf16[512,768]{1,0:T(8,128)(2,1)}, bf16[512,768]{1,0:T(8,128)(2,1)S(1)}, u32[]{:S(2)}, u32[]{:S(2)}) collective-permute-start(bf16[512,768]{1,0:T(8,128)(2,1)} %get-tuple-element.50), channel_id=1, source_target_pairs={{0,72},{2,74},{8,80},{10,82},{12,68},{14,70},{16,88},{18,90},{20,7... | collective-permute-start | bytes 2359304 | tf_op jit(solution)/shard_map/ppermute | solution.py:34
  66.0 17.7 %collective-permute-start.10 = (bf16[512,768]{1,0:T(8,128)(2,1)}, bf16[512,768]{1,0:T(8,128)(2,1)S(1)}, u32[]{:S(2)}, u32[]{:S(2)}) collective-permute-start(bf16[512,768]{1,0:T(8,128)(2,1)} %get-tuple-element.48), channel_id=1, source_target_pairs={{0,64},{64,0},{1,65},{65,1},{2,66},{66,2},{3,67},{67,3},{4,68},{68... | collective-permute-start | bytes 2359304 | tf_op jit(solution)/shard_map/ppermute | solution.py:21
  84.0 27.0 %copy-start.6 = (bf16[256,768]{1,0:T(8,128)(2,1)S(1)}, bf16[256,768]{1,0:T(8,128)(2,1)}, u32[]{:S(2)}) copy-start(bf16[256,768]{1,0:T(8,128)(2,1)} %get-tuple-element.56) | copy-start | bytes 1179652
  84.0 12.1 %collective-permute-start.15 = (bf16[256,768]{1,0:T(8,128)(2,1)S(1)}, bf16[256,768]{1,0:T(8,128)(2,1)S(1)}, u32[]{:S(2)}, u32[]{:S(2)}) collective-permute-start(bf16[256,768]{1,0:T(8,128)(2,1)S(1)} %slice.36), channel_id=1, source_target_pairs={{0,2},{2,0},{4,6},{6,4},{8,10},{10,8},{12,14},{14,12},{16,18},{18,... | collective-permute-start | bytes 1179656 | tf_op jit(solution)/shard_map/ppermute | solution.py:21
  84.4 12.6 %collective-permute-start.16 = (bf16[256,768]{1,0:T(8,128)(2,1)S(1)}, bf16[256,768]{1,0:T(8,128)(2,1)S(1)}, u32[]{:S(2)}, u32[]{:S(2)}) collective-permute-start(bf16[256,768]{1,0:T(8,128)(2,1)S(1)} %copy-done.7), channel_id=1, source_target_pairs={{0,6},{2,4},{4,2},{6,0},{8,14},{10,12},{12,10},{14,8},{16,22},{18,... | collective-permute-start | bytes 1179656 | tf_op jit(solution)/shard_map/ppermute | solution.py:21
  87.2 26.7 %collective-permute-start.13 = (bf16[256,1536]{1,0:T(8,128)(2,1)}, bf16[256,1536]{1,0:T(8,128)(2,1)S(1)}, u32[]{:S(2)}, u32[]{:S(2)}) collective-permute-start(bf16[256,1536]{1,0:T(8,128)(2,1)} %collective-permute-done.9.own_z), channel_id=1, source_target_pairs={{0,2},{2,0},{4,6},{6,4},{8,10},{10,8},{12,14},{14,12},{16,18},{18,... | collective-permute-start | bytes 2359304 | tf_op jit(solution)/shard_map/ppermute | solution.py:21
  88.5 25.3 %collective-permute-start.14 = (bf16[512,768]{1,0:T(8,128)(2,1)S(1)}, bf16[512,768]{1,0:T(8,128)(2,1)S(1)}, u32[]{:S(2)}, u32[]{:S(2)}) collective-permute-start(bf16[512,768]{1,0:T(8,128)(2,1)S(1)} %add_convert_fusion.1.grad), channel_id=1, source_target_pairs={{0,32},{2,34},{4,36},{6,38},{8,40},{10,42},{12,44},{14,46},{16,48}... | collective-permute-start | bytes 2359304 | tf_op jit(solution)/shard_map/ppermute | solution.py:21
  107.3 16.0 %collective-permute-start.17 = (bf16[256,1024]{1,0:T(8,128)(2,1)S(1)}, bf16[256,1024]{1,0:T(8,128)(2,1)}, u32[]{:S(2)}, u32[]{:S(2)}) collective-permute-start(bf16[256,1024]{1,0:T(8,128)(2,1)S(1)} %slice.37), channel_id=1, source_target_pairs={{0,1},{1,0},{2,3},{3,2},{4,5},{5,4},{6,7},{7,6},{8,9},{9,8},{10,11... | collective-permute-start | bytes 1572872 | tf_op jit(solution)/shard_map/ppermute | solution.py:21
  111.0 12.3 %collective-permute-start.18 = (bf16[256,768]{1,0:T(8,128)(2,1)S(1)}, bf16[256,768]{1,0:T(8,128)(2,1)S(1)}, u32[]{:S(2)}, u32[]{:S(2)}) collective-permute-start(bf16[256,768]{1,0:T(8,128)(2,1)S(1)} %copy-done.6), channel_id=1, source_target_pairs={{0,4},{2,6},{4,0},{6,2},{8,12},{10,14},{12,8},{14,10},{16,20},{18,... | collective-permute-start | bytes 1179656 | tf_op jit(solution)/shard_map/ppermute | solution.py:21
  124.1 39.6 %all-to-all-start = ((bf16[16,96,768]{2,1,0:T(8,128)(2,1)}), bf16[16,96,768]{2,1,0:T(8,128)(2,1)}, u32[]{:S(2)}, u32[]{:S(2)}) async-start(bf16[16,96,768]{2,1,0:T(8,128)(2,1)} %bitcast.32), calls=%async_computation | async-start | bytes 4718592 | tf_op jit(solution)/shard_map/all_to_all | solution.py:395
  130.5 25.4 %collective-permute-start.19 = (bf16[256,2048]{1,0:T(8,128)(2,1)S(1)}, bf16[256,2048]{1,0:T(8,128)(2,1)S(1)}, u32[]{:S(2)}, u32[]{:S(2)}) collective-permute-start(bf16[256,2048]{1,0:T(8,128)(2,1)S(1)} %slice.38), channel_id=1, source_target_pairs={{0,1},{1,0},{2,3},{3,2},{4,5},{5,4},{6,7},{7,6},{8,9},{9,8},{10,11... | collective-permute-start | bytes 3145736 | tf_op jit(solution)/shard_map/ppermute | solution.py:21
  (5 other events, 35.4 us)
